TPU v7x, 128 devices: a whole 4x4x4 slice. The times are simulated.
128 devices in a mesh: section: 2 (over z_lo), dp: 16 (over x, z_hi, core), tensor: 4 (over y).
Axes of the slice: x: 4, y: 4, z: 4 (z_hi: 2, z_lo: 2; z = z_hi * 2 + z_lo), core: 2. Of those that a mesh axis runs over, the one named last changes fastest.
Arguments:
- inputs: bfloat16 [2, 32, 1024, 512], P('section', 'dp', 'tensor'), may hold values from -6 to 6
- lengths: int32 [32, 16], P('dp'), may hold values from 1 to 160, 1004 in all within a row
- w_qkv: bfloat16 [2, 3, 512, 512], P('section', None, None, 'tensor'), may hold values from -0.25 to 0.25
- w_out: bfloat16 [2, 512, 512], P('section', 'tensor'), may hold values from -1.5 to 1.5
- w_cross: bfloat16 [2, 2, 512, 512], P('section', None, None, 'tensor'), may hold values from -0.375 to 0.375
- w_up: bfloat16 [2, 512, 2048], P('section', None, 'tensor'), may hold values from -0.25 to 0.25
- w_down: bfloat16 [2, 2048, 512], P('section', 'tensor'), may hold values from -0.1875 to 0.1875
- norm_gain: float32 [2, 3, 512], P('section'), may hold values from 0.25 to 1.75
- norm_bias: float32 [2, 3, 512], P('section'), may hold values from -1.75 to 1.75
- cotangent: float32 [2, 32, 1024, 512], P('section', 'dp', 'tensor'), may hold values from -6 to 6
Outputs:
- outputs: float32 [2, 32, 1024, 512], P('section', 'dp', 'tensor')
- d_inputs: float32 [2, 32, 1024, 512], P('section', 'dp', 'tensor')
- grad_qkv: float32 [2, 3, 512, 512], P('section', None, None, 'tensor')
- grad_out: float32 [2, 512, 512], P('section', 'tensor')
- grad_cross: float32 [2, 2, 512, 512], P('section', None, None, 'tensor')
- grad_up: float32 [2, 512, 2048], P('section', None, 'tensor')
- grad_down: float32 [2, 2048, 512], P('section', 'tensor')
- grad_gain: float32 [2, 3, 512], P('section')
- grad_bias: float32 [2, 3, 512], P('section')
Inputs may be any that keep to these rules, and one draw needn't show every extreme that they name: In each row the 16 lengths sum to 1004, and the largest is 160.
All inputs are finite; a program needn't handle non-finite values.
Results may differ from a plain program's by a relative error of at most 0.038.
Values may be sent and summed in bfloat16 or wider, within the bound.
A program may use at most 192 MiB of HBM per device.

v0:
```python
import jax
import jax.numpy as jnp
from jax import lax
from jax.sharding import PartitionSpec as P

HD = 64
MEM = 20
MICRO = 2


NORM_EPS = 1e-05
MASK_FILL = -1e30


def spread_2(array, axis, root):
    mine = lax.axis_index(axis) == root
    return lax.psum(jnp.where(mine, array, jnp.zeros_like(array)), axis)


def shifted(array, axis, by):
    count = lax.axis_size(axis)
    pairs = [(i, i + by) for i in range(count) if 0 <= i + by < count]
    return lax.ppermute(array, axis, pairs)


def layer_norm(summed_in, gain_vec, bias_vec):
    average = jnp.mean(summed_in, axis=-1, keepdims=True)
    centred = summed_in - average
    spread = jnp.mean(centred * centred, axis=-1, keepdims=True)
    return centred * lax.rsqrt(spread + NORM_EPS) * gain_vec + bias_vec


def norm_back(summed_in, gain_vec, bias_vec, gradient):
    return jax.vjp(layer_norm, summed_in, gain_vec, bias_vec)[1](gradient)


def smooth(value):
    return jax.nn.gelu(value, approximate=True)


def smooth_back(value, gradient):
    return jax.vjp(smooth, value)[1](gradient)[0]


def segment_ids(seg_lengths, seq_length, memory):
    seg_ends = jnp.cumsum(seg_lengths, axis=-1, dtype=jnp.int32)
    offset_pos = jnp.arange(seq_length, dtype=jnp.int32) - memory
    seg_count = jnp.sum(
        (offset_pos[None, :, None] >= seg_ends[:, None, :]).astype(jnp.int32),
        axis=-1,
        dtype=jnp.int32,
    )
    return jnp.where(offset_pos[None, :] >= 0, seg_count + 1, 0)


def split_heads(value, head_size):
    return value.reshape(value.shape[0], value.shape[1], value.shape[2] // head_size, head_size)


def merge_heads(value):
    return value.reshape(value.shape[0], value.shape[1], value.shape[2] * value.shape[3])


def attention_probs(queries, key_rows, allowed, score_scale):
    scores = (
        jnp.einsum("bqhd,bkhd->bhqk", queries, key_rows, preferred_element_type=jnp.float32)
        * score_scale
    )
    if allowed is not None:
        scores = jnp.where(allowed[:, None], scores, MASK_FILL)
    return jax.nn.softmax(scores, axis=-1)


def attention_context(attn_probs, value_rows):
    context = jnp.einsum(
        "bhqk,bkhd->bqhd",
        attn_probs.astype(jnp.bfloat16),
        value_rows,
        preferred_element_type=jnp.float32,
    )
    return merge_heads(context.astype(jnp.bfloat16))


def attention_back(queries, key_rows, value_rows, attn_probs, d_context, score_scale):
    d_probs = jnp.einsum(
        "bqhd,bkhd->bhqk", d_context, value_rows, preferred_element_type=jnp.float32
    )
    centre = jnp.sum(d_probs * attn_probs, axis=-1, keepdims=True)
    d_scores = (attn_probs * (d_probs - centre)).astype(jnp.bfloat16)
    d_queries = (
        jnp.einsum("bhqk,bkhd->bqhd", d_scores, key_rows, preferred_element_type=jnp.float32)
        * score_scale
    )
    d_keys = (
        jnp.einsum("bhqk,bqhd->bkhd", d_scores, queries, preferred_element_type=jnp.float32)
        * score_scale
    )
    d_values = jnp.einsum(
        "bhqk,bqhd->bkhd",
        attn_probs.astype(jnp.bfloat16),
        d_context,
        preferred_element_type=jnp.float32,
    )
    return (merge_heads(d_queries), merge_heads(d_keys), merge_heads(d_values))


def project(row_vals, weight):
    return jnp.einsum("bnd,dk->bnk", row_vals, weight, preferred_element_type=jnp.float32)


def project_back(gradients, weight):
    return jnp.einsum("bnk,dk->bnd", gradients, weight, preferred_element_type=jnp.float32)


def weight_grad(row_vals, gradients):
    return jnp.einsum("bnd,bnk->dk", row_vals, gradients, preferred_element_type=jnp.float32)


def shards(inputs, lengths, w_qkv, w_out, w_cross, w_up, w_down, norm_gain, norm_bias, cotangent):
    row_block = inputs.shape[2]
    model_width = inputs.shape[3]
    batch_rows = inputs.shape[1] // MICRO
    section_at = lax.axis_index("section")
    tensor_at = lax.axis_index("tensor")
    decoder_side = section_at == 1
    first_tensor = (tensor_at == 0).astype(jnp.float32)
    score_scale = HD ** (-0.5)
    seq_length = row_block * lax.axis_size("tensor")
    qkv_w, out_w, cross_w, up_w, down_w = (w_qkv[0], w_out[0], w_cross[0], w_up[0], w_down[0])
    gain_in = norm_gain[0]
    bias_in = norm_bias[0]
    last_gain = jnp.where(decoder_side, gain_in[2], gain_in[1])
    last_bias = jnp.where(decoder_side, bias_in[2], bias_in[1])
    key_width = qkv_w.shape[2]
    positions = jnp.arange(seq_length, dtype=jnp.int32)
    query_pos = jnp.arange(seq_length, dtype=jnp.int32)

    def enter_rows(row_vals):
        return lax.all_gather(row_vals, "tensor", axis=1, tiled=True)

    def leave_rows(term):
        return lax.psum_scatter(
            term.astype(jnp.bfloat16), "tensor", scatter_dimension=1, tiled=True
        ).astype(jnp.float32)

    def leave_back(gradient):
        return lax.all_gather(gradient, "tensor", axis=1, tiled=True)

    def enter_back(term):
        return lax.psum_scatter(
            term.astype(jnp.bfloat16), "tensor", scatter_dimension=1, tiled=True
        ).astype(jnp.float32)

    def share_keys(key_rows, value_rows):
        return (key_rows, value_rows)

    def allowed_mask(seg_ids):
        same_seg = seg_ids[:, :, None] == seg_ids[:, None, :]
        open_mask = same_seg | (seg_ids[:, :, None] == 0) | (seg_ids[:, None, :] == 0)
        causal = same_seg & (positions[None, None, :] <= query_pos[None, :, None])
        return jnp.where(decoder_side, causal, open_mask)

    def forward(x_rows, mem_keys, mem_values, seg_ids):
        allowed = allowed_mask(seg_ids)
        entered_x = enter_rows(x_rows.astype(jnp.bfloat16))
        queries = project(entered_x, qkv_w[0]).astype(jnp.bfloat16)
        key_rows, value_rows = share_keys(
            project(entered_x, qkv_w[1]).astype(jnp.bfloat16),
            project(entered_x, qkv_w[2]).astype(jnp.bfloat16),
        )
        attn_probs = attention_probs(
            split_heads(queries, HD), split_heads(key_rows, HD), allowed, score_scale
        )
        context = attention_context(attn_probs, split_heads(value_rows, HD))
        first_sum = x_rows + leave_rows(project(context, out_w))
        h_one = layer_norm(first_sum, gain_in[0], bias_in[0])
        entered_h = enter_rows(h_one.astype(jnp.bfloat16))
        cross_query = project(entered_h, cross_w[0]).astype(jnp.bfloat16)
        cross_probs = attention_probs(
            split_heads(cross_query, HD), split_heads(mem_keys, HD), None, score_scale
        )
        cross_context = attention_context(cross_probs, split_heads(mem_values, HD))
        second_sum = h_one + leave_rows(project_back(cross_context, cross_w[1]))
        h_two = jnp.where(decoder_side, layer_norm(second_sum, gain_in[1], bias_in[1]), h_one)
        entered_f = enter_rows(h_two.astype(jnp.bfloat16))
        up_proj = project(entered_f, up_w)
        activated = smooth(up_proj).astype(jnp.bfloat16)
        third_sum = h_two + leave_rows(project(activated, down_w))
        result = layer_norm(third_sum, last_gain, last_bias)
        return {
            "entered_x": entered_x,
            "queries": queries,
            "key_rows": key_rows,
            "value_rows": value_rows,
            "attn_probs": attn_probs,
            "context": context,
            "first_sum": first_sum,
            "entered_h": entered_h,
            "cross_query": cross_query,
            "cross_probs": cross_probs,
            "cross_context": cross_context,
            "second_sum": second_sum,
            "entered_f": entered_f,
            "up_proj": up_proj,
            "activated": activated,
            "third_sum": third_sum,
            "result": result,
        }

    def memory_back(result, spread, d_keys_in, d_values_in):
        keys_grad = d_keys_in.astype(jnp.bfloat16)
        values_grad = d_values_in.astype(jnp.bfloat16)
        mem_term = project_back(keys_grad, cross_w[0]) + project_back(values_grad, cross_w[1])
        summed = lax.psum(mem_term.astype(jnp.bfloat16), "tensor").astype(jnp.float32)
        grad_share = 1.0
        grad_memory = (
            jnp.stack([weight_grad(spread, keys_grad), weight_grad(spread, values_grad)])
            * grad_share
        )
        d_rows, d_gain, d_bias = norm_back(result[:, :MEM], gain_in[2], bias_in[2], summed)
        return (d_rows * first_tensor, grad_memory, d_gain * first_tensor, d_bias * first_tensor)

    source_all = inputs[0].astype(jnp.float32).reshape(MICRO, batch_rows, row_block, model_width)
    cot_all = cotangent[0].reshape(MICRO, batch_rows, row_block, model_width)
    seg_all = segment_ids(lengths, seq_length, MEM).reshape(MICRO, batch_rows, seq_length)
    empty_keys = jnp.zeros((batch_rows, MEM, key_width), jnp.bfloat16)
    arrived = (empty_keys, empty_keys)
    outputs_all = jnp.zeros((MICRO, batch_rows, row_block, model_width), jnp.float32)
    kept_memory = jnp.zeros((MICRO, 2, batch_rows, MEM, key_width), jnp.bfloat16)
    kept_spread = jnp.zeros((MICRO, batch_rows, MEM, model_width), jnp.bfloat16)
    for tick_num in range(MICRO + 1):
        index_now = tick_num - section_at
        in_range = (index_now >= 0) & (index_now < MICRO)
        chosen = jnp.clip(index_now, 0, MICRO - 1)
        state = forward(source_all[chosen], arrived[0], arrived[1], seg_all[chosen])
        normed = layer_norm(state["result"][:, :MEM], gain_in[2], bias_in[2]).astype(jnp.bfloat16)
        memory_spread = spread_2(normed, "tensor", 0)
        spread = memory_spread
        new_keys = project(memory_spread, cross_w[0]).astype(jnp.bfloat16)
        new_values = project(memory_spread, cross_w[1]).astype(jnp.bfloat16)
        outputs_all = jnp.where(in_range, outputs_all.at[chosen].set(state["result"]), outputs_all)
        kept_memory = jnp.where(
            in_range, kept_memory.at[chosen].set(jnp.stack([arrived[0], arrived[1]])), kept_memory
        )
        kept_spread = jnp.where(in_range, kept_spread.at[chosen].set(spread), kept_spread)
        if tick_num < MICRO:
            arrived = shifted((new_keys, new_values), "section", 1)
    zero_back = jnp.zeros((batch_rows, MEM, key_width), jnp.float32)
    returned = (zero_back, zero_back)
    d_inputs_all = jnp.zeros((MICRO, batch_rows, row_block, model_width), jnp.float32)
    running = (
        jnp.zeros(qkv_w.shape, jnp.float32),
        jnp.zeros(out_w.shape, jnp.float32),
        jnp.zeros(cross_w.shape, jnp.float32),
        jnp.zeros(up_w.shape, jnp.float32),
        jnp.zeros(down_w.shape, jnp.float32),
        jnp.zeros(gain_in.shape, jnp.float32),
        jnp.zeros(bias_in.shape, jnp.float32),
    )
    for tick_num in range(MICRO + 1):
        index_now = MICRO - tick_num - section_at
        in_range = (index_now >= 0) & (index_now < MICRO)
        factor = in_range.astype(jnp.float32)
        chosen = jnp.clip(index_now, 0, MICRO - 1)
        mem_pair = kept_memory[chosen]
        state = forward(source_all[chosen], mem_pair[0], mem_pair[1], seg_all[chosen])
        d_rows, grad_memory, d_mem_gain, d_mem_bias = memory_back(
            state["result"], kept_spread[chosen], returned[0], returned[1]
        )
        d_result = cot_all[chosen].at[:, :MEM].add(d_rows)
        d_third, d_last_gain, d_last_bias = norm_back(
            state["third_sum"], last_gain, last_bias, d_result
        )
        d_down = leave_back(d_third.astype(jnp.bfloat16))
        backward_grad_down = weight_grad(state["activated"], d_down)
        d_up = smooth_back(state["up_proj"], project_back(d_down, down_w)).astype(jnp.bfloat16)
        backward_grad_up = weight_grad(state["entered_f"], d_up)
        d_two = d_third + enter_back(project_back(d_up, up_w))
        d_second, d_mid_gain, d_mid_bias = norm_back(
            state["second_sum"], gain_in[1], bias_in[1], d_two
        )
        d_second = jnp.where(decoder_side, d_second, 0.0)
        d_cross = leave_back(d_second.astype(jnp.bfloat16))
        grad_cross_out = weight_grad(d_cross, state["cross_context"])
        d_cross_context = project(d_cross, cross_w[1]).astype(jnp.bfloat16)
        d_cross_query, d_mem_keys, d_mem_values = attention_back(
            split_heads(state["cross_query"], HD),
            split_heads(mem_pair[0], HD),
            split_heads(mem_pair[1], HD),
            state["cross_probs"],
            split_heads(d_cross_context, HD),
            score_scale,
        )
        d_cross_query = d_cross_query.astype(jnp.bfloat16)
        grad_cross_query = weight_grad(state["entered_h"], d_cross_query)
        d_one = (
            d_second
            + enter_back(project_back(d_cross_query, cross_w[0]))
            + jnp.where(decoder_side, 0.0, d_two)
        )
        d_first, d_first_gain, d_first_bias = norm_back(
            state["first_sum"], gain_in[0], bias_in[0], d_one
        )
        d_self = leave_back(d_first.astype(jnp.bfloat16))
        backward_grad_out = weight_grad(state["context"], d_self)
        d_context = project_back(d_self, out_w).astype(jnp.bfloat16)
        d_queries, d_keys_all, d_values_all = attention_back(
            split_heads(state["queries"], HD),
            split_heads(state["key_rows"], HD),
            split_heads(state["value_rows"], HD),
            state["attn_probs"],
            split_heads(d_context, HD),
            score_scale,
        )
        d_key_rows = d_keys_all
        d_value_rows = d_values_all
        d_queries = d_queries.astype(jnp.bfloat16)
        d_key_rows = d_key_rows.astype(jnp.bfloat16)
        d_value_rows = d_value_rows.astype(jnp.bfloat16)
        backward_entered_x = state["entered_x"]
        backward_grad_qkv = jnp.stack(
            [
                weight_grad(backward_entered_x, d_queries),
                weight_grad(backward_entered_x, d_key_rows),
                weight_grad(backward_entered_x, d_value_rows),
            ]
        )
        d_entered = (
            project_back(d_queries, qkv_w[0])
            + project_back(d_key_rows, qkv_w[1])
            + project_back(d_value_rows, qkv_w[2])
        )
        d_source = d_first + enter_back(d_entered)
        backward_grad_gain = jnp.stack(
            [
                d_first_gain,
                jnp.where(decoder_side, d_mid_gain, d_last_gain),
                jnp.where(decoder_side, d_last_gain, 0.0),
            ]
        )
        backward_grad_bias = jnp.stack(
            [
                d_first_bias,
                jnp.where(decoder_side, d_mid_bias, d_last_bias),
                jnp.where(decoder_side, d_last_bias, 0.0),
            ]
        )
        backward_grad_cross = jnp.stack([grad_cross_query, grad_cross_out])
        d_source, d_mem_keys, d_mem_values, tick_grads = (
            d_source,
            d_mem_keys,
            d_mem_values,
            (
                backward_grad_qkv,
                backward_grad_out,
                backward_grad_cross,
                backward_grad_up,
                backward_grad_down,
                backward_grad_gain,
                backward_grad_bias,
            ),
        )
        slot_mask = jnp.zeros((3, 1), jnp.float32).at[2].set(1.0)
        extra = (
            0.0,
            0.0,
            grad_memory,
            0.0,
            0.0,
            slot_mask * d_mem_gain[None],
            slot_mask * d_mem_bias[None],
        )
        running = jax.tree.map(
            lambda total, part, more: total + factor * (part + more), running, tick_grads, extra
        )
        d_inputs_all = jnp.where(in_range, d_inputs_all.at[chosen].set(d_source), d_inputs_all)
        if tick_num < MICRO:
            returned = shifted((d_mem_keys, d_mem_values), "section", -1)
    grad_qkv, grad_out, grad_cross, grad_up, grad_down, grad_gain, grad_bias = running
    shares = (grad_qkv, grad_out, grad_cross, grad_up, grad_down)
    total_qkv, total_out, total_cross, total_up, total_down = (
        lax.psum(shares[0].astype(jnp.bfloat16), "dp").astype(jnp.float32),
        lax.psum(shares[1].astype(jnp.bfloat16), "dp").astype(jnp.float32),
        lax.psum(shares[2].astype(jnp.bfloat16), "dp").astype(jnp.float32),
        lax.psum(shares[3].astype(jnp.bfloat16), "dp").astype(jnp.float32),
        lax.psum(shares[4].astype(jnp.bfloat16), "dp").astype(jnp.float32),
    )
    total_gain, total_bias = lax.psum((grad_gain, grad_bias), ("dp", "tensor"))
    local_rows = MICRO * batch_rows
    return (
        outputs_all.reshape(1, local_rows, row_block, model_width),
        d_inputs_all.reshape(1, local_rows, row_block, model_width),
        total_qkv[None],
        total_out[None],
        total_cross[None],
        total_up[None],
        total_down[None],
        total_gain[None],
        total_bias[None],
    )


def solution(mesh):
    return jax.shard_map(
        shards,
        mesh=mesh,
        in_specs=(
            P("section", "dp", "tensor", None),
            P("dp", None),
            P("section", None, None, "tensor"),
            P("section", "tensor", None),
            P("section", None, None, "tensor"),
            P("section", None, "tensor"),
            P("section", "tensor", None),
            P("section", None, None),
            P("section", None, None),
            P("section", "dp", "tensor", None),
        ),
        out_specs=(
            P("section", "dp", "tensor", None),
            P("section", "dp", "tensor", None),
            P("section", None, None, "tensor"),
            P("section", "tensor", None),
            P("section", None, None, "tensor"),
            P("section", None, "tensor"),
            P("section", "tensor", None),
            P("section", None, None),
            P("section", None, None),
        ),
        check_vma=False,
    )
```

profile of v0, /device:TPU:1, one launch (start us, length us, event | category | flops | bytes accessed | tf_op | source)
XLA Modules:
  0.0 1623.7 jit_solution(915161702584052923)
XLA Ops:
  20.0 16.9 %all-gather.34.cloned.1.call-done = bf16[1,1024,512]{2,1,0:T(8,128)(2,1)} async-done(((bf16[1,256,512]{2,1,0:T(8,128)(2,1)}), bf16[1,1024,512]{2,1,0:T(8,128)(2,1)}) %all-gather.34.cloned.1.call-update) | async-done | bytes 1048592 | tf_op jit(solution)/shard_map/all_gather | solution.py:139
  116.2 26.1 %reduce-scatter.31.cloned.1.call-done = bf16[1,256,512]{2,1,0:T(8,128)(2,1)} async-done(((bf16[1,1024,512]{2,1,0:T(8,128)(2,1)}), bf16[1,256,512]{2,1,0:T(8,128)(2,1)}) %reduce-scatter.31.cloned.1.call-update) | async-done | bytes 262160 | tf_op jit(solution)/shard_map/reduce_scatter | solution.py:142
  142.4 26.1 %reduce-scatter.25.cloned.1.call-done = bf16[1,256,512]{2,1,0:T(8,128)(2,1)} async-done(((bf16[1,1024,512]{2,1,0:T(8,128)(2,1)}), bf16[1,256,512]{2,1,0:T(8,128)(2,1)}) %reduce-scatter.25.cloned.1.call-update) | async-done | bytes 262160 | tf_op jit(solution)/shard_map/reduce_scatter | solution.py:142
  172.0 24.2 %all-gather.24.cloned.1.call-done = bf16[1,1024,512]{2,1,0:T(8,128)(2,1)} async-done(((bf16[1,256,512]{2,1,0:T(8,128)(2,1)}), bf16[1,1024,512]{2,1,0:T(8,128)(2,1)}) %all-gather.24.cloned.1.call-update) | async-done | bytes 1048592 | tf_op jit(solution)/shard_map/all_gather | solution.py:139
  200.9 23.2 %reduce-scatter.27.cloned.1.call-done = bf16[1,256,512]{2,1,0:T(8,128)(2,1)} async-done(((bf16[1,1024,512]{2,1,0:T(8,128)(2,1)}), bf16[1,256,512]{2,1,0:T(8,128)(2,1)}) %reduce-scatter.27.cloned.1.call-update) | async-done | bytes 262160 | tf_op jit(solution)/shard_map/reduce_scatter | solution.py:142
  229.2 23.7 %all-gather.26.cloned.1.call-done = bf16[1,1024,512]{2,1,0:T(8,128)(2,1)} async-done(((bf16[1,256,512]{2,1,0:T(8,128)(2,1)}), bf16[1,1024,512]{2,1,0:T(8,128)(2,1)}) %all-gather.26.cloned.1.call-update) | async-done | bytes 1048592 | tf_op jit(solution)/shard_map/all_gather | solution.py:139
  257.5 21.8 %all-gather.30.cloned.1.call-done = bf16[1,1024,512]{2,1,0:T(8,128)(2,1)} async-done(((bf16[1,256,512]{2,1,0:T(8,128)(2,1)}), bf16[1,1024,512]{2,1,0:T(8,128)(2,1)}) %all-gather.30.cloned.1.call-update) | async-done | bytes 1048592 | tf_op jit(solution)/shard_map/all_gather | solution.py:139
  281.0 24.7 %reduce-scatter.29.cloned.1.call-done = bf16[1,256,512]{2,1,0:T(8,128)(2,1)} async-done(((bf16[1,1024,512]{2,1,0:T(8,128)(2,1)}), bf16[1,256,512]{2,1,0:T(8,128)(2,1)}) %reduce-scatter.29.cloned.1.call-update) | async-done | bytes 262160 | tf_op jit(solution)/shard_map/reduce_scatter | solution.py:142
  330.9 28.2 %reduce-scatter.33.cloned.1.call-done = bf16[1,256,512]{2,1,0:T(8,128)(2,1)} async-done(((bf16[1,1024,512]{2,1,0:T(8,128)(2,1)}), bf16[1,256,512]{2,1,0:T(8,128)(2,1)}) %reduce-scatter.33.cloned.1.call-update) | async-done | bytes 262160 | tf_op jit(solution)/shard_map/reduce_scatter | solution.py:142
  363.6 24.1 %all-gather.32.cloned.1.call-done = bf16[1,1024,512]{2,1,0:T(8,128)(2,1)} async-done(((bf16[1,256,512]{2,1,0:T(8,128)(2,1)}), bf16[1,1024,512]{2,1,0:T(8,128)(2,1)}) %all-gather.32.cloned.1.call-update) | async-done | bytes 1048592 | tf_op jit(solution)/shard_map/all_gather | solution.py:139
  394.8 20.3 %reduce-scatter.35.cloned.1.call-done = bf16[1,256,512]{2,1,0:T(8,128)(2,1)} async-done(((bf16[1,1024,512]{2,1,0:T(8,128)(2,1)}), bf16[1,256,512]{2,1,0:T(8,128)(2,1)}) %reduce-scatter.35.cloned.1.call-update) | async-done | bytes 262160 | tf_op jit(solution)/shard_map/reduce_scatter | solution.py:142
  448.2 23.8 %reduce-scatter.43.cloned.1.call-done = bf16[1,256,512]{2,1,0:T(8,128)(2,1)} async-done(((bf16[1,1024,512]{2,1,0:T(8,128)(2,1)}), bf16[1,256,512]{2,1,0:T(8,128)(2,1)}) %reduce-scatter.43.cloned.1.call-update) | async-done | bytes 262160 | tf_op jit(solution)/shard_map/reduce_scatter | solution.py:142
  476.6 24.3 %all-gather.40.cloned.1.call-done = bf16[1,1024,512]{2,1,0:T(8,128)(2,1)} async-done(((bf16[1,256,512]{2,1,0:T(8,128)(2,1)}), bf16[1,1024,512]{2,1,0:T(8,128)(2,1)}) %all-gather.40.cloned.1.call-update) | async-done | bytes 1048592 | tf_op jit(solution)/shard_map/all_gather | solution.py:139
  508.7 20.2 %reduce-scatter.45.cloned.1.call-done = bf16[1,256,512]{2,1,0:T(8,128)(2,1)} async-done(((bf16[1,1024,512]{2,1,0:T(8,128)(2,1)}), bf16[1,256,512]{2,1,0:T(8,128)(2,1)}) %reduce-scatter.45.cloned.1.call-update) | async-done | bytes 262160 | tf_op jit(solution)/shard_map/reduce_scatter | solution.py:142
  551.3 14.6 all-gather.42.cloned.1.call-done
  572.6 19.6 %reduce-scatter.39.cloned.1.call-done = bf16[1,256,512]{2,1,0:T(8,128)(2,1)} async-done(((bf16[1,1024,512]{2,1,0:T(8,128)(2,1)}), bf16[1,256,512]{2,1,0:T(8,128)(2,1)}) %reduce-scatter.39.cloned.1.call-update) | async-done | bytes 262160 | tf_op jit(solution)/shard_map/reduce_scatter | solution.py:142
  592.3 26.3 %reduce-scatter.53.cloned.1.call-done = bf16[1,256,512]{2,1,0:T(8,128)(2,1)} async-done(((bf16[1,1024,512]{2,1,0:T(8,128)(2,1)}), bf16[1,256,512]{2,1,0:T(8,128)(2,1)}) %reduce-scatter.53.cloned.1.call-update) | async-done | bytes 262160 | tf_op jit(solution)/shard_map/reduce_scatter | solution.py:142
  618.5 26.3 %reduce-scatter.47.cloned.1.call-done = bf16[1,256,512]{2,1,0:T(8,128)(2,1)} async-done(((bf16[1,1024,512]{2,1,0:T(8,128)(2,1)}), bf16[1,256,512]{2,1,0:T(8,128)(2,1)}) %reduce-scatter.47.cloned.1.call-update) | async-done | bytes 262160 | tf_op jit(solution)/shard_map/reduce_scatter | solution.py:150
  654.9 21.1 %all-gather.48.cloned.1.call-done = bf16[1,1024,512]{2,1,0:T(8,128)(2,1)} async-done(((bf16[1,256,512]{2,1,0:T(8,128)(2,1)}), bf16[1,1024,512]{2,1,0:T(8,128)(2,1)}) %all-gather.48.cloned.1.call-update) | async-done | bytes 1048592 | tf_op jit(solution)/shard_map/all_gather | solution.py:139
  681.2 21.2 %all-gather.44.cloned.1.call-done = bf16[1,1024,512]{2,1,0:T(8,128)(2,1)} async-done(((bf16[1,256,512]{2,1,0:T(8,128)(2,1)}), bf16[1,1024,512]{2,1,0:T(8,128)(2,1)}) %all-gather.44.cloned.1.call-update) | async-done | bytes 1048592 | tf_op jit(solution)/shard_map/all_gather | solution.py:147
  748.7 21.9 %all-gather.50.cloned.1.call-done = bf16[1,1024,512]{2,1,0:T(8,128)(2,1)} async-done(((bf16[1,256,512]{2,1,0:T(8,128)(2,1)}), bf16[1,1024,512]{2,1,0:T(8,128)(2,1)}) %all-gather.50.cloned.1.call-update) | async-done | bytes 1048592 | tf_op jit(solution)/shard_map/all_gather | solution.py:147
  777.2 19.8 %reduce-scatter.63.cloned.1.call-done = bf16[1,256,512]{2,1,0:T(8,128)(2,1)} async-done(((bf16[1,1024,512]{2,1,0:T(8,128)(2,1)}), bf16[1,256,512]{2,1,0:T(8,128)(2,1)}) %reduce-scatter.63.cloned.1.call-update) | async-done | bytes 262160 | tf_op jit(solution)/shard_map/reduce_scatter | solution.py:142
  797.0 26.3 %reduce-scatter.57.cloned.1.call-done = bf16[1,256,512]{2,1,0:T(8,128)(2,1)} async-done(((bf16[1,1024,512]{2,1,0:T(8,128)(2,1)}), bf16[1,256,512]{2,1,0:T(8,128)(2,1)}) %reduce-scatter.57.cloned.1.call-update) | async-done | bytes 262160 | tf_op jit(solution)/shard_map/reduce_scatter | solution.py:150
  829.1 24.2 %all-gather.52.cloned.1.call-done = bf16[1,1024,512]{2,1,0:T(8,128)(2,1)} async-done(((bf16[1,256,512]{2,1,0:T(8,128)(2,1)}), bf16[1,1024,512]{2,1,0:T(8,128)(2,1)}) %all-gather.52.cloned.1.call-update) | async-done | bytes 1048592 | tf_op jit(solution)/shard_map/all_gather | solution.py:147
  862.5 21.4 %reduce-scatter.59.cloned.1.call-done = bf16[1,256,512]{2,1,0:T(8,128)(2,1)} async-done(((bf16[1,1024,512]{2,1,0:T(8,128)(2,1)}), bf16[1,256,512]{2,1,0:T(8,128)(2,1)}) %reduce-scatter.59.cloned.1.call-update) | async-done | bytes 262160 | tf_op jit(solution)/shard_map/reduce_scatter | solution.py:150
  890.1 25.0 %all-gather.56.cloned.1.call-done = bf16[1,1024,512]{2,1,0:T(8,128)(2,1)} async-done(((bf16[1,256,512]{2,1,0:T(8,128)(2,1)}), bf16[1,1024,512]{2,1,0:T(8,128)(2,1)}) %all-gather.56.cloned.1.call-update) | async-done | bytes 1048592 | tf_op jit(solution)/shard_map/all_gather | solution.py:139
  961.2 22.8 %all-gather.58.cloned.1.call-done = bf16[1,1024,512]{2,1,0:T(8,128)(2,1)} async-done(((bf16[1,256,512]{2,1,0:T(8,128)(2,1)}), bf16[1,1024,512]{2,1,0:T(8,128)(2,1)}) %all-gather.58.cloned.1.call-update) | async-done | bytes 1048592 | tf_op jit(solution)/shard_map/all_gather | solution.py:147
  991.8 18.7 %reduce-scatter.49.cloned.1.call-done = bf16[1,256,512]{2,1,0:T(8,128)(2,1)} async-done(((bf16[1,1024,512]{2,1,0:T(8,128)(2,1)}), bf16[1,256,512]{2,1,0:T(8,128)(2,1)}) %reduce-scatter.49.cloned.1.call-update) | async-done | bytes 262160 | tf_op jit(solution)/shard_map/reduce_scatter | solution.py:150
  1010.5 26.3 %reduce-scatter.67.cloned.1.call-done = bf16[1,256,512]{2,1,0:T(8,128)(2,1)} async-done(((bf16[1,1024,512]{2,1,0:T(8,128)(2,1)}), bf16[1,256,512]{2,1,0:T(8,128)(2,1)}) %reduce-scatter.67.cloned.1.call-update) | async-done | bytes 262160 | tf_op jit(solution)/shard_map/reduce_scatter | solution.py:150
  1044.0 24.2 %all-gather.60.cloned.1.call-done = bf16[1,1024,512]{2,1,0:T(8,128)(2,1)} async-done(((bf16[1,256,512]{2,1,0:T(8,128)(2,1)}), bf16[1,1024,512]{2,1,0:T(8,128)(2,1)}) %all-gather.60.cloned.1.call-update) | async-done | bytes 1048592 | tf_op jit(solution)/shard_map/all_gather | solution.py:147
  1081.0 17.7 %reduce-scatter.69.cloned.1.call-done = bf16[1,256,512]{2,1,0:T(8,128)(2,1)} async-done(((bf16[1,1024,512]{2,1,0:T(8,128)(2,1)}), bf16[1,256,512]{2,1,0:T(8,128)(2,1)}) %reduce-scatter.69.cloned.1.call-update) | async-done | bytes 262160 | tf_op jit(solution)/shard_map/reduce_scatter | solution.py:150
  1281.9 319.3 %all-reduce = (f32[1,3,512]{2,1,0:T(4,128)S(1)}, f32[1,3,512]{2,0,1:T(1,128)}) all-reduce(f32[1,3,512]{2,1,0:T(4,128)S(1)} %fusion.470, f32[1,3,512]{2,0,1:T(1,128)S(1)} %broadcast_in_dim.190), channel_id=1, replica_groups=mesh['section'=2,'dp'=16,'tensor'=4] {'dp','tensor'}, use_global_device_ids=true, to_apply=%region_144.145 | all-reduce | flops 3072 | bytes 24576 | tf_op jit(solution)/shard_map/psum | solution.py:388
  (1097 shorter events, 580.2 us)
Async XLA Ops:
  11.1 78.8 %all-gather.22.cloned.1.call-start = ((), (), s32[]{:S(2)}) async-start(), calls=%async_computation.24 | async-start | bytes 1310720 | tf_op jit(solution)/shard_map/all_gather | solution.py:139
  11.9 104.3 %reduce-scatter.37.cloned.1.call-start = ((), (), s32[]{:S(2)}) async-start(), calls=%async_computation.37 | async-start | bytes 1310720 | tf_op jit(solution)/shard_map/reduce_scatter | solution.py:142
  53.8 88.6 %reduce-scatter.31.cloned.1.call-start = ((), (), s32[]{:S(2)}) async-start(), calls=%async_computation.31 | async-start | bytes 1310720 | tf_op jit(solution)/shard_map/reduce_scatter | solution.py:142
  78.5 90.0 %reduce-scatter.25.cloned.1.call-start = ((), (), s32[]{:S(2)}) async-start(), calls=%async_computation.25 | async-start | bytes 1310720 | tf_op jit(solution)/shard_map/reduce_scatter | solution.py:142
  105.1 91.2 %all-gather.24.cloned.1.call-start = ((), (), s32[]{:S(2)}) async-start(), calls=%async_computation.26 | async-start | bytes 1310720 | tf_op jit(solution)/shard_map/all_gather | solution.py:139
  229.2 76.5 %reduce-scatter.29.cloned.1.call-start = ((), (), s32[]{:S(2)}) async-start(), calls=%async_computation.29 | async-start | bytes 1310720 | tf_op jit(solution)/shard_map/reduce_scatter | solution.py:142
  256.7 102.5 %reduce-scatter.33.cloned.1.call-start = ((), (), s32[]{:S(2)}) async-start(), calls=%async_computation.33 | async-start | bytes 1310720 | tf_op jit(solution)/shard_map/reduce_scatter | solution.py:142
  330.6 57.2 %all-gather.32.cloned.1.call-start = ((), (), s32[]{:S(2)}) async-start(), calls=%async_computation.34 | async-start | bytes 1310720 | tf_op jit(solution)/shard_map/all_gather | solution.py:139
  394.7 77.4 %reduce-scatter.43.cloned.1.call-start = ((), (), s32[]{:S(2)}) async-start(), calls=%async_computation.42 | async-start | bytes 1310720 | tf_op jit(solution)/shard_map/reduce_scatter | solution.py:142
  506.1 59.9 %all-gather.42.cloned.1.call-start = ((), (), s32[]{:S(2)}) async-start(), calls=%async_computation.45 | async-start | bytes 1310720 | tf_op jit(solution)/shard_map/all_gather | solution.py:147
  546.9 71.6 %reduce-scatter.53.cloned.1.call-start = ((), (), s32[]{:S(2)}) async-start(), calls=%async_computation.51 | async-start | bytes 1310720 | tf_op jit(solution)/shard_map/reduce_scatter | solution.py:142
  551.2 93.6 %reduce-scatter.47.cloned.1.call-start = ((), (), s32[]{:S(2)}) async-start(), calls=%async_computation.46 | async-start | bytes 1310720 | tf_op jit(solution)/shard_map/reduce_scatter | solution.py:150
  572.4 103.5 %all-gather.48.cloned.1.call-start = ((), (), s32[]{:S(2)}) async-start(), calls=%async_computation.52 | async-start | bytes 1310720 | tf_op jit(solution)/shard_map/all_gather | solution.py:139
  654.8 74.1 %reduce-scatter.55.cloned.1.call-start = ((), (), s32[]{:S(2)}) async-start(), calls=%async_computation.53 | async-start | bytes 1310720 | tf_op jit(solution)/shard_map/reduce_scatter | solution.py:142
  681.1 89.5 %all-gather.50.cloned.1.call-start = ((), (), s32[]{:S(2)}) async-start(), calls=%async_computation.54 | async-start | bytes 1310720 | tf_op jit(solution)/shard_map/all_gather | solution.py:147
  748.7 74.6 %reduce-scatter.57.cloned.1.call-start = ((), (), s32[]{:S(2)}) async-start(), calls=%async_computation.55 | async-start | bytes 1310720 | tf_op jit(solution)/shard_map/reduce_scatter | solution.py:150
  777.1 76.2 %all-gather.52.cloned.1.call-start = ((), (), s32[]{:S(2)}) async-start(), calls=%async_computation.56 | async-start | bytes 1310720 | tf_op jit(solution)/shard_map/all_gather | solution.py:147
  829.1 54.8 %reduce-scatter.59.cloned.1.call-start = ((), (), s32[]{:S(2)}) async-start(), calls=%async_computation.57 | async-start | bytes 1310720 | tf_op jit(solution)/shard_map/reduce_scatter | solution.py:150
  861.0 54.1 %all-gather.56.cloned.1.call-start = ((), (), s32[]{:S(2)}) async-start(), calls=%async_computation.61 | async-start | bytes 1310720 | tf_op jit(solution)/shard_map/all_gather | solution.py:139
  890.1 53.9 %reduce-scatter.65.cloned.1.call-start = ((), (), s32[]{:S(2)}) async-start(), calls=%async_computation.62 | async-start | bytes 1310720 | tf_op jit(solution)/shard_map/reduce_scatter | solution.py:142
  920.2 63.8 %all-gather.58.cloned.1.call-start = ((), (), s32[]{:S(2)}) async-start(), calls=%async_computation.63 | async-start | bytes 1310720 | tf_op jit(solution)/shard_map/all_gather | solution.py:147
  961.1 75.6 %reduce-scatter.67.cloned.1.call-start = ((), (), s32[]{:S(2)}) async-start(), calls=%async_computation.64 | async-start | bytes 1310720 | tf_op jit(solution)/shard_map/reduce_scatter | solution.py:150
  990.5 77.7 %all-gather.60.cloned.1.call-start = ((), (), s32[]{:S(2)}) async-start(), calls=%async_computation.65 | async-start | bytes 1310720 | tf_op jit(solution)/shard_map/all_gather | solution.py:147
  1043.9 54.8 %reduce-scatter.69.cloned.1.call-start = ((), (), s32[]{:S(2)}) async-start(), calls=%async_computation.66 | async-start | bytes 1310720 | tf_op jit(solution)/shard_map/reduce_scatter | solution.py:150
  1075.2 60.6 %all-gather.46.cloned.1.call-start = ((), (), s32[]{:S(2)}) async-start(), calls=%async_computation.49 | async-start | bytes 1310720 | tf_op jit(solution)/shard_map/all_gather | solution.py:147
  1114.3 68.3 %all-gather.38.cloned.1.call-start = ((), (), s32[]{:S(2)}) async-start(), calls=%async_computation.40 | async-start | bytes 1310720 | tf_op jit(solution)/shard_map/all_gather | solution.py:139
  1125.7 83.0 %all-gather.62.cloned.1.call-start = ((), (), s32[]{:S(2)}) async-start(), calls=%async_computation.67 | async-start | bytes 1310720 | tf_op jit(solution)/shard_map/all_gather | solution.py:147
  1135.5 123.6 %reduce-scatter.41.cloned.1.call-start = ((), (), s32[]{:S(2)}) async-start(), calls=%async_computation.41 | async-start | bytes 1310720 | tf_op jit(solution)/shard_map/reduce_scatter | solution.py:142
  1191.0 410.8 %reduce-scatter.51.cloned.1.call-start = ((), (), s32[]{:S(2)}) async-start(), calls=%async_computation.50 | async-start | bytes 1310720 | tf_op jit(solution)/shard_map/reduce_scatter | solution.py:150
  1223.3 380.4 %reduce-scatter.61.cloned.1.call-start = ((), (), s32[]{:S(2)}) async-start(), calls=%async_computation.59 | async-start | bytes 1310720 | tf_op jit(solution)/shard_map/reduce_scatter | solution.py:150
  1237.0 369.6 %reduce-scatter.71.cloned.1.call-start = ((), (), s32[]{:S(2)}) async-start(), calls=%async_computation.68 | async-start | bytes 1310720 | tf_op jit(solution)/shard_map/reduce_scatter | solution.py:150
  1249.0 360.0 %all-reduce.5.cloned.1.call-start = ((), (), s32[]{:S(2)}) async-start(), calls=%async_computation.69 | async-start | bytes 3670016 | tf_op jit(solution)/shard_map/psum | solution.py:382
  (325 other events, 5638.9 us)
Sparse Core Ops, SparseCore 0:
  10.5 26.2 all-gather.33
  39.1 24.2 all-gather.27
  65.6 24.2 all-gather.21
  92.8 23.3 reduce-scatter.36
  172.1 24.1 all-gather.23
  200.8 23.3 reduce-scatter.26
  228.7 24.1 all-gather.25
  255.0 24.2 all-gather.29
  282.3 23.3 reduce-scatter.28
  330.7 28.4 reduce-scatter.32
  363.6 24.0 all-gather.31
  391.6 23.3 reduce-scatter.34
  417.2 24.2 all-gather.35
  448.3 23.7 reduce-scatter.42
  476.7 24.1 all-gather.39
  541.1 24.7 all-gather.41
  651.7 24.1 all-gather.47
  678.0 24.2 all-gather.43
  705.3 23.5 reduce-scatter.54
  743.5 27.0 all-gather.49
  829.2 24.1 all-gather.51
  890.2 24.8 all-gather.55
  920.4 23.5 reduce-scatter.64
  958.5 25.4 all-gather.57
  1044.0 24.1 all-gather.59
  1105.7 24.1 all-gather.45
  1131.4 24.2 all-gather.53
  1158.0 24.4 all-gather.37
  1184.2 24.4 all-gather.61
  1211.7 23.3 reduce-scatter.40
  1263.1 23.7 reduce-scatter.60
  1315.5 144.5 all-reduce.4
  (14 shorter events, 323.4 us)
where the time goes:
time: 1640 us; the launch traced here: 1620 us
  waiting for transfers between devices  780 us (48%)
  blocking collectives  384 us (23%)
  matrix products  222 us (14%)
  other arithmetic  151 us (9%)
  local copies, waits for them, and re-layouts  48.5 us (3%)
  between operations  19.1 us (1%)
  starting transfers between devices  17.4 us (1%)
    psum x1, blocking collectives, shards(): total_gain, total_bias = lax.psum((grad_gain, grad_bias), ('dp', 'tensor'))  319 us
    reduce_scatter x15, waiting for transfers between devices, leave_rows(): lax.psum_scatter(term.astype(jnp.bfloat16), 'tensor', scatter_dimension=1...  270 us
    all_gather x12, waiting for transfers between devices, enter_rows(): return lax.all_gather(row_vals, 'tensor', axis=1, tiled=True)  215 us
    all_gather x9, waiting for transfers between devices, leave_back(): return lax.all_gather(gradient, 'tensor', axis=1, tiled=True)  150 us
    reduce_scatter x9, waiting for transfers between devices, enter_back(): lax.psum_scatter(term.astype(jnp.bfloat16), 'tensor', scatter_dimension=1...  137 us
    dot_general x33, matrix products, project_back(): jnp.einsum('bnk,dk->bnd', gradients, weight, preferred_element_type=jnp.f...  50.5 us
    dot_general x31, matrix products, project(): jnp.einsum('bnd,dk->bnk', row_vals, weight, preferred_element_type=jnp.fl...  50.2 us
    psum x3, blocking collectives, spread_2(): return lax.psum(jnp.where(mine, array, jnp.zeros_like(array)), axis)  36.3 us
  transfers between devices with their start and end apart: 54, of which 44 were waited for; matrix products, arithmetic and copies ran while one was open for 16% of the time, Pallas kernels for 0%

commit v1 on v0

v1 whole, which is shorter than its diff:
```python
import jax
import jax.numpy as jnp
from jax import lax
from jax.experimental import pallas as pl
from jax.experimental.pallas import tpu as pltpu
from jax.sharding import PartitionSpec as P

F32 = jnp.float32
BF = jnp.bfloat16
MESH = pl.DeviceIdType.MESH

MEM = 20
MP = 32
R = 2
T = 256
HALO = 160
D = 512
NT = 4
W_ENC = T + 2 * HALO + MP
W_DEC = T + HALO
MEM_AT = T + 2 * HALO
EPS = 1e-05
FILL = -1e30
SCALE = 0.125

G_DOWN, G_UP, G_CROSS, G_OUT, G_QKV, G_ROWS = 0, 2048, 4096, 5120, 5632, 7168
QKV, OUT, CROSS, UP, DOWN = range(5)
W_ROWS = (512, 128, 512, 512, 512)


def dot(a, b):
    return lax.dot_general(a, b, (((1,), (0,)), ((), ())), preferred_element_type=F32)


def dot_nt(a, b):
    return lax.dot_general(a, b, (((1,), (1,)), ((), ())), preferred_element_type=F32)


def dot_tn(a, b):
    return lax.dot_general(a, b, (((0,), (0,)), ((), ())), preferred_element_type=F32)


def remote(src, dst, send, recv, **device):
    return pltpu.make_async_remote_copy(
        src_ref=src, dst_ref=dst, send_sem=send, recv_sem=recv, device_id=device, device_id_type=MESH
    )


def normed(v):
    c = v - jnp.mean(v, axis=1, keepdims=True)
    rs = lax.rsqrt(jnp.mean(c * c, axis=1, keepdims=True) + EPS)
    return c * rs, rs


def norm_back(xhat, rs, gain, dy):
    dxh = dy * gain
    m1 = jnp.mean(dxh, axis=1, keepdims=True)
    m2 = jnp.mean(dxh * xhat, axis=1, keepdims=True)
    return rs * (dxh - m1 - xhat * m2)


def gelu_both(u):
    k = 0.7978845608028654
    u2 = u * u
    th = jnp.tanh(k * u * (1.0 + 0.044715 * u2))
    half = 0.5 * (1.0 + th)
    grad = half + 0.5 * u * (1.0 - th * th) * (k * (1.0 + 3.0 * 0.044715 * u2))
    return u * half, grad


def layer_kernel(
    lens, x_in, cot_in, wqkv_in, wout_in, wcross_in, wup_in, wdown_in, gain, bias,
    y_out, dx_out, g_out, ng_out,
    x_ext, cotm, cot, wqkv, wout, wcross, wup, wdown,
    kk, vv, kt, vt, qs, pt, ctx, mask, hmask,
    xh1, xh2, xh3, rs1, rs2, rs3, h32, hb, h1b, act, gp, du, d32, dab, dr,
    dkv, dqkv, halo_s, halo_r, memd_s, memd_r,
    ex_o, ex_st, ex_f, ex_m, ex_h, ex_dq, qm,
    kvm, dkvm_s, dkvm_r, kblk, vblk, cpt, cq, cctx,
    mx1, mx2, mx3, mr1, mr2, mr3, mh, mact, mgp, mc, mm, mst, md,
    lsem, wsend, wrecv, xsend, xrecv, msend, mrecv, esend, erecv, ksend, krecv, dsend, drecv,
    hsend, hrecv, gsend, grecv, qsend, qrecv,
):
    sec = lax.axis_index("section")
    dp = lax.axis_index("dp")
    t = lax.axis_index("tensor")
    core = lax.rem(dp, 2)
    sib = dp + 1 - 2 * core
    is_enc = sec == 0
    is_dec = sec == 1
    left = lax.rem(t + 3, NT)
    right = lax.rem(t + 1, NT)
    opp = lax.rem(t + 2, NT)
    other = 1 - sec

    ins = (wqkv_in, wout_in, wcross_in, wup_in, wdown_in)
    ws = (wqkv, wout, wcross, wup, wdown)

    def part(i, ref, start, n):
        if i in (QKV, CROSS):
            return ref.at[:, pl.ds(start, n), :]
        return ref.at[pl.ds(start, n), :]

    def slot(i, a, start, n):
        if i in (QKV, CROSS):
            return ws[i].at[a, :, pl.ds(start, n), :]
        return ws[i].at[a, pl.ds(start, n), :]

    barrier = pltpu.get_barrier_semaphore()
    for off in (1, 2, 3):
        pl.semaphore_signal(barrier, inc=1, device_id={"tensor": lax.rem(t + off, NT)}, device_id_type=MESH)
    pl.semaphore_signal(barrier, inc=1, device_id={"dp": sib}, device_id_type=MESH)
    for b in range(NT):
        pl.semaphore_signal(barrier, inc=1, device_id={"section": other, "tensor": b}, device_id_type=MESH)

    locals_ = [
        pltpu.make_async_copy(x_in, x_ext.at[:, pl.ds(0, T), :], lsem.at[0]),
        pltpu.make_async_copy(cot_in, cot, lsem.at[1]),
    ]
    for i in range(5):
        locals_.append(pltpu.make_async_copy(ins[i], ws[i].at[t], lsem.at[2 + i]))
    for c in locals_:
        c.start()

    pl.semaphore_wait(barrier, 8)

    x_right = remote(x_in.at[:, pl.ds(T - HALO, HALO), :], x_ext.at[:, pl.ds(T, HALO), :],
                     xsend.at[0], xrecv.at[0], tensor=right)
    x_left = remote(x_in.at[:, pl.ds(0, HALO), :], x_ext.at[:, pl.ds(T + HALO, HALO), :],
                    xsend.at[1], xrecv.at[1], tensor=left)
    x_right.start()

    mem_copies = []
    for off in (1, 2, 3):
        to = lax.rem(t + off, NT)
        mem_copies.append(remote(x_in.at[:, pl.ds(0, MP), :], x_ext.at[:, pl.ds(MEM_AT, MP), :],
                                 msend.at[0, off - 1], mrecv.at[0], tensor=to))
        mem_copies.append(remote(cot_in.at[:, pl.ds(0, MP), :], cotm, msend.at[1, off - 1], mrecv.at[1], tensor=to))
    mem_local = [
        pltpu.make_async_copy(x_in.at[:, pl.ds(0, MP), :], x_ext.at[:, pl.ds(MEM_AT, MP), :], lsem.at[7]),
        pltpu.make_async_copy(cot_in.at[:, pl.ds(0, MP), :], cotm, lsem.at[8]),
    ]

    @pl.when(is_enc)
    def _():
        x_left.start()

        @pl.when(t == 0)
        def _():
            for c in mem_copies + mem_local:
                c.start()

    def w_copies(i):
        rows = W_ROWS[i]
        hf, qt = rows // 2, rows // 4
        mine = core * hf
        y_right = remote(part(i, ins[i], mine, hf), slot(i, t, mine, hf), wsend.at[i, 0], wrecv.at[i, 0], tensor=right)
        y_left = remote(part(i, ins[i], mine, hf), slot(i, t, mine, hf), wsend.at[i, 1], wrecv.at[i, 1], tensor=left)
        on_right = remote(slot(i, left, mine, qt), slot(i, left, mine, qt), wsend.at[i, 2], wrecv.at[i, 2], tensor=right)
        on_left = remote(slot(i, right, mine + qt, qt), slot(i, right, mine + qt, qt), wsend.at[i, 3], wrecv.at[i, 3],
                         tensor=left)
        s_left = remote(slot(i, left, mine, hf), slot(i, left, mine, hf), wsend.at[i, 4], wrecv.at[i, 4], dp=sib)
        s_right = remote(slot(i, right, mine, hf), slot(i, right, mine, hf), wsend.at[i, 5], wrecv.at[i, 5], dp=sib)
        s_opp = remote(slot(i, opp, mine, hf), slot(i, opp, mine, hf), wsend.at[i, 6], wrecv.at[i, 6], dp=sib)
        return y_right, y_left, on_right, on_left, s_left, s_right, s_opp

    copies = [w_copies(i) for i in range(5)]

    def send_first(i):
        copies[i][0].start()
        copies[i][1].start()

    def send_on(i):
        y_right, y_left, on_right, on_left, s_left, s_right, s_opp = copies[i]
        y_right.wait_recv()
        on_right.start()
        s_left.start()
        y_left.wait_recv()
        on_left.start()
        s_right.start()

    def send_opp(i):
        copies[i][2].wait_recv()
        copies[i][3].wait_recv()
        copies[i][6].start()

    def ready(i, rel):
        copies[i][4 + rel].wait_recv()

    send_first(QKV)
    send_first(OUT)

    lane = lax.broadcasted_iota(jnp.int32, (T, 128), 1)
    hmask[0] = jnp.where(lane < 64, 1.0, 0.0).astype(BF)
    hmask[1] = jnp.where(lane < 64, 0.0, 1.0).astype(BF)

    def segments(pos, r):
        off = pos - MEM
        seg = jnp.where(off >= 0, 1, 0)
        end = jnp.int32(0)
        for k in range(16):
            end = end + lens[r, k]
            seg = seg + jnp.where(off >= end, 1, 0)
        return seg

    def make_masks(width, encoder):
        for r in range(R):
            for half in range(2):
                i = lax.broadcasted_iota(jnp.int32, (width, 128), 0)
                pos = jnp.where(i < T, i, jnp.where(i < T + HALO, i - T - HALO, i - HALO)) + t * T
                qpos = lax.broadcasted_iota(jnp.int32, (8, 128), 1) + (t * T + half * 128)
                ks = segments(pos, r)
                q_seg = segments(qpos, r)[0:1]
                same = ks == q_seg
                if encoder:
                    ok = jnp.logical_or(jnp.logical_and(i < MEM_AT, jnp.logical_and(same, ks > 0)),
                                        jnp.logical_and(i >= MEM_AT, i < MEM_AT + MEM))
                else:
                    ok = jnp.logical_and(same, jnp.logical_and(pos <= qpos[0:1], pos >= 0))
                mask[r, 0:width, half * 128:half * 128 + 128] = jnp.where(ok, 0.0, FILL)

    @pl.when(is_enc)
    def _():
        make_masks(W_ENC, True)

    @pl.when(is_dec)
    def _():
        make_masks(W_DEC, False)

    locals_[0].wait()
    x_right.wait_recv()

    @pl.when(is_enc)
    def _():
        x_left.wait_recv()

        @pl.when(t == 0)
        def _():
            for c in mem_local:
                c.wait()

        @pl.when(t > 0)
        def _():
            mem_copies[0].wait_recv()
            mem_copies[1].wait_recv()

    for c in locals_[1:]:
        c.wait()

    def shard_at(step):
        return lax.rem(t + jnp.where(step == 0, 0, jnp.where(step == 1, 3, step - 1)), NT)

    lane_m = lax.broadcasted_iota(jnp.int32, (MP, 128), 1)
    low_m = lane_m < 64

    def project(a, width, encoder):
        wkv = jnp.concatenate([wqkv[a, 1], wqkv[a, 2]], axis=1)
        for r in range(R):
            kv = dot(x_ext[r, 0:width], wkv)
            k32, v32 = kv[:, 0:128], kv[:, 128:256]
            kk[a, r, 0:width] = k32.astype(BF)
            vv[a, r, 0:width] = v32.astype(BF)
            kt[a, r, :, 0:width] = k32.T.astype(BF)
            vt[a, r, :, 0:width] = v32.T.astype(BF)
            q = dot(x_ext[r, 0:T], wqkv[a, 0]).astype(BF)
            qs[a, r] = (q.astype(F32) * SCALE).astype(BF)
            if encoder:
                m32 = dot(x_ext[r, MEM_AT:MEM_AT + MP], wqkv[a, 0]).astype(BF).astype(F32) * SCALE
                lhs = jnp.concatenate([jnp.where(low_m, m32, 0.0), jnp.where(low_m, 0.0, m32)], axis=0).astype(BF)
                qm[a, r] = lhs
                s = dot_nt(lhs, k32[0:T].astype(BF))
                top = jnp.max(s, axis=1, keepdims=True)
                p = jnp.exp(s - top)
                total = jnp.sum(p, axis=1, keepdims=True)
                o = dot(p.astype(BF), v32[0:T].astype(BF)) / total
                ex_o[t, a, r * MP:r * MP + MP] = jnp.where(low_m, o[0:MP], o[MP:2 * MP]).astype(BF)
                st = ex_st[t, r * MP:r * MP + MP]
                st = jnp.where(lane_m == 2 * a, top[0:MP], st)
                st = jnp.where(lane_m == 2 * a + 1, top[MP:2 * MP], st)
                st = jnp.where(lane_m == 2 * a + 8, total[0:MP], st)
                st = jnp.where(lane_m == 2 * a + 9, total[MP:2 * MP], st)
                ex_st[t, r * MP:r * MP + MP] = st

    ex_st[t] = jnp.zeros((R * MP, 128), F32)

    @pl.loop(0, NT)
    def _(step):
        @pl.when(step == 1)
        def _():
            send_on(QKV)
            send_on(OUT)

            @pl.when(is_dec)
            def _():
                send_first(CROSS)

            send_first(UP)
            send_first(DOWN)
            ready(QKV, 0)

        @pl.when(step == 2)
        def _():
            ready(QKV, 1)

        @pl.when(step == 3)
        def _():
            send_opp(QKV)
            send_opp(OUT)
            ready(QKV, 2)

        a = shard_at(step)

        @pl.when(is_enc)
        def _():
            project(a, W_ENC, True)

        @pl.when(is_dec)
        def _():
            project(a, W_DEC, False)

    def ex_copies(e, buf):
        out = []
        for off in (1, 2, 3):
            out.append(remote(buf.at[t], buf.at[t], esend.at[e, off - 1], erecv.at[e, off - 1],
                              tensor=lax.rem(t + off, NT)))
        return out

    exchanges = [ex_copies(e, buf) for e, buf in enumerate((ex_o, ex_st, ex_f, ex_m, ex_h))]

    def ex_start(e):
        for c in exchanges[e]:
            c.start()

    def ex_wait(e):
        for c in exchanges[e]:
            c.wait_recv()

    @pl.when(is_enc)
    def _():
        ex_start(0)
        ex_start(1)

    def attend(a, r, width):
        tops = []
        for h in range(2):
            s = dot_nt(kk[a, r, 0:width], qs[a, r] * hmask[h]) + mask[r, 0:width]
            p = jnp.exp(s - jnp.max(s, axis=0, keepdims=True))
            p = (p * (1.0 / jnp.sum(p, axis=0, keepdims=True))).astype(BF)
            pt[a, r, h, 0:width] = p
            tops.append(dot(vt[a, r, h * 64:h * 64 + 64, 0:width], p))
        ctx[r, a] = jnp.concatenate(tops, axis=0).T.astype(BF)

    @pl.loop(0, NT * R)
    def _(i):
        a = shard_at(lax.div(i, 2))
        r = lax.rem(i, 2)

        @pl.when(is_enc)
        def _():
            attend(a, r, W_ENC)

        @pl.when(is_dec)
        def _():
            attend(a, r, W_DEC)

    for rel in range(3):
        ready(OUT, rel)

    def wide(ref, r):
        return jnp.concatenate([ref[r, a] for a in range(NT)], axis=1)

    w_out_full = wout[...].reshape(D, D)

    @pl.loop(0, R)
    def _(r):
        a0 = x_ext[r, 0:T].astype(F32) + dot(wide(ctx, r), w_out_full)
        xh, rs = normed(a0)
        xh1[r] = xh
        rs1[r] = rs
        h = xh * gain[0:1] + bias[0:1]
        h32[r] = h
        hb[r] = h.astype(BF)

    def mem_combine():
        for r in range(R):
            rows = slice(r * MP, r * MP + MP)
            sts = [ex_st[s, rows] for s in range(NT)]
            top = jnp.maximum(jnp.maximum(sts[0], sts[1]), jnp.maximum(sts[2], sts[3]))
            ws_ = [pltpu.roll(sts[s], 120, 1) * jnp.exp(sts[s] - top) for s in range(NT)]
            total = ws_[0] + ws_[1] + ws_[2] + ws_[3]
            inv = 1.0 / jnp.where(lane_m < 8, total, 1.0)
            mst[0, rows] = jnp.where(lane_m < 8, top + jnp.log(jnp.where(lane_m < 8, total, 1.0)), 0.0)
            for a in range(NT):
                acc = jnp.zeros((MP, 128), F32)
                for s in range(NT):
                    w = ws_[s] * inv
                    wide_w = jnp.where(low_m, w[:, 2 * a:2 * a + 1], w[:, 2 * a + 1:2 * a + 2])
                    acc = acc + wide_w * ex_o[s, a, rows].astype(F32)
                mc[rows, a * 128:a * 128 + 128] = acc

    def mem_first():
        mem_combine()
        xm = jnp.concatenate([x_ext[r, MEM_AT:MEM_AT + MP] for r in range(R)], axis=0).astype(F32)
        xh, rs = normed(xm + dot(mc[...].astype(BF), w_out_full))
        mx1[...] = xh
        mr1[...] = rs
        h = xh * gain[0:1] + bias[0:1]
        mh[...] = h
        av, gv = gelu_both(dot(h.astype(BF), wup[t]))
        mact[...] = av.astype(BF)
        mgp[...] = gv
        ex_f[t] = dot(av.astype(BF), wdown[t]).astype(BF)
        ex_start(2)

    kv_copies = [remote(kvm.at[t], kvm.at[t], ksend.at[b], krecv.at[t], section=other, tensor=b) for b in range(NT)]

    def mem_second():
        ex_wait(2)
        third = mh[...]
        for s in range(NT):
            third = third + ex_f[s].astype(F32)
        xh, rs = normed(third)
        mx2[...] = xh
        mr2[...] = rs
        y = xh * gain[1:2] + bias[1:2]
        md[...] = y
        xh, rs = normed(y)
        mx3[...] = xh
        mr3[...] = rs
        m = (xh * gain[2:3] + bias[2:3]).astype(BF)
        mm[...] = m
        kvm[t, 0] = dot(m, wcross[t, 0]).astype(BF)
        kvm[t, 1] = dot(m, wcross[t, 1]).astype(BF)
        for c in kv_copies:
            c.start()

    @pl.when(is_enc)
    def _():
        ex_wait(0)
        ex_wait(1)
        mem_first()

    @pl.when(is_dec)
    def _():
        send_on(CROSS)

    send_on(UP)
    send_on(DOWN)

    @pl.when(is_enc)
    def _():
        mem_second()

    @pl.when(is_dec)
    def _():
        send_opp(CROSS)

    send_opp(UP)
    send_opp(DOWN)

    pad_mask = jnp.where(
        lax.rem(lax.broadcasted_iota(jnp.int32, (256, T), 0), MP) < MEM, 0.0, FILL)

    def full_cross(j):
        return jnp.concatenate([wcross[a, j] for a in range(NT)], axis=1)

    def cross_forward():
        for rel in range(3):
            ready(CROSS, rel)
        for b in range(NT):
            remote(kvm.at[b], kvm.at[b], ksend.at[b], krecv.at[b], section=other, tensor=b).wait_recv()
        kblk[...] = jnp.zeros(kblk.shape, BF)
        vblk[...] = jnp.zeros(vblk.shape, BF)
        for r in range(R):
            for a in range(NT):
                for h in range(2):
                    at = slice(a * 64 + h * MP, a * 64 + h * MP + MP)
                    kblk[r, at, a * 128:a * 128 + 128] = kvm[a, 0, r * MP:r * MP + MP] * hmask[h, 0:MP]
                    vblk[r, at, a * 128:a * 128 + 128] = kvm[a, 1, r * MP:r * MP + MP] * hmask[h, 0:MP]
        wc0 = full_cross(0)
        wc1 = full_cross(1)

        @pl.loop(0, R)
        def _(r):
            h1b[r] = hb[r]
            q = dot(hb[r], wc0).astype(BF)
            q = (q.astype(F32) * SCALE).astype(BF)
            cq[r] = q
            s = dot_nt(kblk[r], q) + pad_mask
            s = s.reshape(8, MP, T)
            p = jnp.exp(s - jnp.max(s, axis=1, keepdims=True))
            p = p * (1.0 / jnp.sum(p, axis=1, keepdims=True))
            p = p.reshape(256, T).astype(BF)
            cpt[r] = p
            c = dot_tn(p, vblk[r]).astype(BF)
            cctx[r] = c
            xh, rs = normed(h32[r] + dot_nt(c, wc1))
            xh2[r] = xh
            rs2[r] = rs
            h = xh * gain[1:2] + bias[1:2]
            h32[r] = h
            hb[r] = h.astype(BF)

    @pl.when(is_dec)
    def _():
        cross_forward()

    for rel in range(3):
        ready(UP, rel)

    @pl.loop(0, NT * R)
    def _(i):
        a = lax.div(i, 2)
        r = lax.rem(i, 2)
        av, gv = gelu_both(dot(hb[r], wup[a]))
        act[r, a] = av.astype(BF)
        gp[r, a] = gv.astype(BF)

    for rel in range(3):
        ready(DOWN, rel)

    last = jnp.where(is_enc, 1, 2)
    g_last = jnp.where(is_enc, gain[1:2], gain[2:3])
    b_last = jnp.where(is_enc, bias[1:2], bias[2:3])
    ng_out[...] = jnp.zeros(ng_out.shape, F32)

    def add_norm(at, xh, dy):
        ng_out[pl.ds(at, 1)] += jnp.sum(dy * xh, axis=0, keepdims=True)
        ng_out[pl.ds(at + 3, 1)] += jnp.sum(dy, axis=0, keepdims=True)

    row_i = lax.broadcasted_iota(jnp.int32, (T, D), 0)
    is_mem_row = jnp.logical_and(row_i < MEM, jnp.logical_and(is_enc, t == 0))

    @pl.loop(0, R)
    def _(r):
        third = h32[r]
        for a in range(NT):
            third = third + dot(act[r, a], wdown[a])
        xh, rs = normed(third)
        y_out[r] = xh * g_last + b_last
        dy = jnp.where(is_mem_row, 0.0, cot[r])
        d3 = norm_back(xh, rs, g_last, dy)
        ng_out[pl.ds(last, 1)] += jnp.sum(dy * xh, axis=0, keepdims=True)
        ng_out[pl.ds(last + 3, 1)] += jnp.sum(dy, axis=0, keepdims=True)
        d32[r] = d3
        dab[r] = d3.astype(BF)

    @pl.when(jnp.logical_and(is_enc, t == 0))
    def _():
        for r in range(R):
            y_out[r, 0:24] = jnp.where(
                lax.broadcasted_iota(jnp.int32, (24, D), 0) < MEM, md[r * MP:r * MP + 24], y_out[r, 0:24])

    @pl.loop(0, NT)
    def _(a):
        for r in range(R):
            du[r, a] = (dot_nt(dab[r], wdown[a]) * gp[r, a].astype(F32)).astype(BF)
        wd = dot_tn(act[0, a], dab[0]) + dot_tn(act[1, a], dab[1])
        wu = dot_tn(hb[0], du[0, a]) + dot_tn(hb[1], du[1, a])
        for j in range(4):
            g_out[a, G_DOWN + D * j:G_DOWN + D * (j + 1)] = wd[:, 128 * j:128 * j + 128].astype(BF)
            g_out[a, G_UP + D * j:G_UP + D * (j + 1)] = wu[:, 128 * j:128 * j + 128].astype(BF)

    @pl.loop(0, R)
    def _(r):
        d = d32[r]
        for a in range(NT):
            d = d + dot_nt(du[r, a], wup[a])
        d32[r] = d

    dkv_copies = [
        remote(dkvm_s.at[b], dkvm_r.at[t], dsend.at[b], drecv.at[t], section=other, tensor=b) for b in range(NT)
    ]

    def cross_backward():
        wc0 = full_cross(0)
        wc1 = full_cross(1)

        @pl.loop(0, R)
        def _(r):
            dy = d32[r]
            add_norm(1, xh2[r], dy)
            d2 = norm_back(xh2[r], rs2[r], gain[1:2], dy)
            d32[r] = d2
            dcb = d2.astype(BF)
            dab[r] = dcb
            dc = dot(dcb, wc1).astype(BF)
            p = cpt[r].astype(F32).reshape(8, MP, T)
            dp_ = dot_nt(vblk[r], dc).reshape(8, MP, T)
            ds = p * (dp_ - jnp.sum(p * dp_, axis=1, keepdims=True))
            ds = ds.reshape(256, T).astype(BF)
            dk = dot(ds, cq[r])
            dv = dot(cpt[r], dc)
            rows = pl.ds(pl.multiple_of(r * MP, MP), MP)
            for a in range(NT):
                for j, val in ((0, dk), (1, dv)):
                    dkvm_s[a, j, rows] = jnp.where(
                        low_m, val[64 * a:64 * a + MP, 128 * a:128 * a + 128],
                        val[64 * a + MP:64 * a + 2 * MP, 128 * a:128 * a + 128])
            dq = (dot_tn(ds, kblk[r]) * SCALE).astype(BF)
            cq[r] = dq

        for c in dkv_copies:
            c.start()

        gq = dot_tn(h1b[0], cq[0]) + dot_tn(h1b[1], cq[1])
        go = dot_tn(dab[0], cctx[0]) + dot_tn(dab[1], cctx[1])
        for a in range(NT):
            g_out[a, G_CROSS:G_CROSS + D] = gq[:, 128 * a:128 * a + 128].astype(BF)
            g_out[a, G_CROSS + D:G_CROSS + 2 * D] = go[:, 128 * a:128 * a + 128].astype(BF)

        @pl.loop(0, R)
        def _(r):
            d32[r] += dot_nt(cq[r], wc0)

    @pl.when(is_dec)
    def _():
        cross_backward()

    @pl.loop(0, R)
    def _(r):
        dy = d32[r]
        add_norm(0, xh1[r], dy)
        d1 = norm_back(xh1[r], rs1[r], gain[0:1], dy)
        dx_out[r] = d1
        db = d1.astype(BF)
        dab[r] = db
        drr = dot_nt(db, w_out_full).astype(BF)
        for a in range(NT):
            dr[r, a] = drr[:, 128 * a:128 * a + 128]

    def attend_back(a, r, width, encoder):
        dk = jnp.zeros((width, 128), F32)
        dv = jnp.zeros((width, 128), F32)
        dqs = []
        for h in range(2):
            q_h = qs[a, r] * hmask[h]
            dr_h = dr[r, a] * hmask[h]
            pb = pt[a, r, h, 0:width]
            p = pb.astype(F32)
            dp_ = dot_nt(vv[a, r, 0:width], dr_h)
            ds = (p * (dp_ - jnp.sum(p * dp_, axis=0, keepdims=True))).astype(BF)
            dqs.append(dot(kt[a, r, h * 64:h * 64 + 64, 0:width], ds))
            dk = dk + dot(ds, q_h)
            dv = dv + dot(pb, dr_h)
        dqkv[r, a, :, 0:128] = (jnp.concatenate(dqs, axis=0).T * SCALE).astype(BF)
        for j, val in ((0, dk), (1, dv)):
            dkv[a, r, j] = val[0:T]
            halo_s[0, a, r, j] = val[T:T + HALO].astype(BF)
            if encoder:
                halo_s[1, a, r, j] = val[T + HALO:T + 2 * HALO].astype(BF)
                memd_s[a, r, j] = val[MEM_AT:MEM_AT + MP].astype(BF)

    def halo_copies(a):
        return (remote(halo_s.at[0, a], halo_r.at[0, a], hsend.at[0, a], hrecv.at[0, a], tensor=left),
                remote(halo_s.at[1, a], halo_r.at[1, a], hsend.at[1, a], hrecv.at[1, a], tensor=right))

    @pl.loop(0, NT)
    def _(a):
        for r in range(R):
            @pl.when(is_enc)
            def _():
                attend_back(a, r, W_ENC, True)

            @pl.when(is_dec)
            def _():
                attend_back(a, r, W_DEC, False)

        to_left, to_right = halo_copies(a)
        to_left.start()

        @pl.when(is_enc)
        def _():
            to_right.start()

    to_first = remote(memd_s, memd_r.at[t], gsend.at[0], grecv.at[t], tensor=0)

    @pl.when(jnp.logical_and(is_enc, t > 0))
    def _():
        to_first.start()

    def out_grad():
        wo = dot_tn(wide(ctx, 0), dab[0]) + dot_tn(wide(ctx, 1), dab[1])
        for a in range(NT):
            for j in range(4):
                g_out[a, G_OUT + 128 * j:G_OUT + 128 * j + 128] = (
                    wo[128 * a:128 * a + 128, 128 * j:128 * j + 128].astype(BF))

    out_grad()

    first = jnp.where(t == 0, 1.0, 0.0)
    dq_copy = remote(ex_dq.at[t], ex_dq.at[t], qsend.at[0], qrecv.at[t], tensor=0)

    def add_g(start, val):
        n = val.shape[0]
        g_out[t, start:start + n] = (g_out[t, start:start + n].astype(F32) + val).astype(BF)

    def add_norm_m(at, xh, dy):
        ng_out[at:at + 1] += first * jnp.sum(dy * xh, axis=0, keepdims=True)
        ng_out[at + 3:at + 4] += first * jnp.sum(dy, axis=0, keepdims=True)

    def mem_backward():
        for b in range(NT):
            remote(dkvm_s.at[b], dkvm_r.at[b], dsend.at[b], drecv.at[b], section=other, tensor=b).wait_recv()
        grads = []
        for j in range(2):
            tot = dkvm_r[0, j] + dkvm_r[1, j] + dkvm_r[2, j] + dkvm_r[3, j]
            grads.append(tot.astype(BF))
        ex_m[t] = (dot_nt(grads[0], wcross[t, 0]) + dot_nt(grads[1], wcross[t, 1])).astype(BF)
        ex_start(3)
        for a in range(NT):
            g_out[a, G_CROSS:G_CROSS + 2 * D] = jnp.zeros((2 * D, 128), BF)
        for j in range(2):
            g_out[t, G_CROSS + D * j:G_CROSS + D * j + D] = dot_tn(mm[...], grads[j]).astype(BF)
        ex_wait(3)
        dm = ex_m[0].astype(F32)
        for s in range(1, NT):
            dm = dm + ex_m[s].astype(F32)
        add_norm_m(2, mx3[...], dm)
        rows_m = lax.broadcasted_iota(jnp.int32, (R * MP, D), 0)
        cm = jnp.concatenate([cotm[0], cotm[1]], axis=0)
        cm = jnp.where(lax.rem(rows_m, MP) < MEM, cm, 0.0)
        dy = cm + norm_back(mx3[...], mr3[...], gain[2:3], dm)
        add_norm_m(1, mx2[...], dy)
        d3 = norm_back(mx2[...], mr2[...], gain[1:2], dy)
        d3b = d3.astype(BF)
        dum = (dot_nt(d3b, wdown[t]) * mgp[...]).astype(BF)
        ex_h[t] = dot_nt(dum, wup[t]).astype(BF)
        ex_start(4)
        wd = dot_tn(mact[...], d3b)
        wu = dot_tn(mh[...].astype(BF), dum)
        for j in range(4):
            add_g(G_DOWN + D * j, wd[:, 128 * j:128 * j + 128])
            add_g(G_UP + D * j, wu[:, 128 * j:128 * j + 128])
        ex_wait(4)
        d2 = d3
        for s in range(NT):
            d2 = d2 + ex_h[s].astype(F32)
        add_norm_m(0, mx1[...], d2)
        d1 = norm_back(mx1[...], mr1[...], gain[0:1], d2)
        md[...] = d1
        d1b = d1.astype(BF)
        drm = dot_nt(d1b, w_out_full).astype(BF).astype(F32)
        prod = drm * mc[...]
        for r in range(R):
            acc = jnp.zeros((MP, 128), F32)
            for hh in range(8):
                part_ = prod[r * MP:r * MP + MP, (hh // 2) * 128:(hh // 2) * 128 + 128]
                part_ = jnp.where(low_m if hh % 2 == 0 else jnp.logical_not(low_m), part_, 0.0)
                acc = jnp.where(lane_m == hh, jnp.sum(part_, axis=1, keepdims=True), acc)
            mst[1, r * MP:r * MP + MP] = acc
        for a in range(NT):
            @pl.when(t == a)
            def _():
                wo = dot_tn(mc[:, 128 * a:128 * a + 128].astype(BF), d1b)
                for j in range(4):
                    add_g(G_OUT + 128 * j, wo[:, 128 * j:128 * j + 128])
        for a in range(NT):
            for r in range(R):
                rows = slice(r * MP, r * MP + MP)
                lse = mst[0, rows]
                dlt = mst[1, rows]
                lse = jnp.concatenate([lse[:, 2 * a:2 * a + 1], lse[:, 2 * a + 1:2 * a + 2]], axis=0)
                dlt = jnp.concatenate([dlt[:, 2 * a:2 * a + 1], dlt[:, 2 * a + 1:2 * a + 2]], axis=0)
                lhs = qm[a, r]
                ko, vo = kk[a, r, 0:T], vv[a, r, 0:T]
                p = jnp.exp(dot_nt(lhs, ko) - lse)
                dra = drm[rows, 128 * a:128 * a + 128]
                dra = jnp.concatenate([jnp.where(low_m, dra, 0.0), jnp.where(low_m, 0.0, dra)], axis=0).astype(BF)
                ds = (p * (dot_nt(dra, vo) - dlt)).astype(BF)
                dq = dot(ds, ko)
                ex_dq[t, a, rows] = (jnp.where(low_m, dq[0:MP], dq[MP:2 * MP]) * SCALE).astype(BF)
                dkv[a, r, 0] += dot_tn(ds, lhs)
                dkv[a, r, 1] += dot_tn(p.astype(BF), dra)

        @pl.when(t > 0)
        def _():
            dq_copy.start()

        @pl.when(t == 0)
        def _():
            for r in range(R):
                dx_out[r, 0:MP] += md[r * MP:r * MP + MP]
            for s in range(1, NT):
                remote(memd_s, memd_r.at[s], gsend.at[0], grecv.at[s], tensor=0).wait_recv()
                remote(ex_dq.at[s], ex_dq.at[s], qsend.at[0], qrecv.at[s], tensor=0).wait_recv()
            for a in range(NT):
                for r in range(R):
                    rows = slice(r * MP, r * MP + MP)
                    for j in range(2):
                        tot = memd_s[a, r, j].astype(F32)
                        for s in range(1, NT):
                            tot = tot + memd_r[s, a, r, j].astype(F32)
                        dkv[a, r, j, 0:MP] += tot
                    tot = ex_dq[0, a, rows].astype(F32)
                    for s in range(1, NT):
                        tot = tot + ex_dq[s, a, rows].astype(F32)
                    dqkv[r, a, 0:MP, 0:128] = (dqkv[r, a, 0:MP, 0:128].astype(F32) + tot).astype(BF)

    @pl.when(is_enc)
    def _():
        mem_backward()

    @pl.loop(0, NT)
    def _(a):
        to_left, to_right = halo_copies(a)
        to_left.wait_recv()

        @pl.when(is_enc)
        def _():
            to_right.wait_recv()

        for r in range(R):
            for j in range(2):
                dkv[a, r, j, T - HALO:T] += halo_r[0, a, r, j].astype(F32)

                @pl.when(is_enc)
                def _():
                    dkv[a, r, j, 0:HALO] += halo_r[1, a, r, j].astype(F32)

                dqkv[r, a, :, 128 * (j + 1):128 * (j + 2)] = dkv[a, r, j].astype(BF)
        gw = dot_tn(x_ext[0, 0:T], dqkv[0, a]) + dot_tn(x_ext[1, 0:T], dqkv[1, a])
        for j in range(3):
            g_out[a, G_QKV + D * j:G_QKV + D * j + D] = gw[:, 128 * j:128 * j + 128].astype(BF)
        wfull = jnp.concatenate([wqkv[a, j] for j in range(3)], axis=1)
        for r in range(R):
            dx_out[r] += dot_nt(dqkv[r, a], wfull)

    for i in range(5):
        def drain(i=i):
            for c in copies[i]:
                c.wait_send()
        if i == CROSS:
            pl.when(is_dec)(drain)
        else:
            drain()
    x_right.wait_send()
    for a in range(NT):
        halo_copies(a)[0].wait_send()

    @pl.when(is_dec)
    def _():
        for c in dkv_copies:
            c.wait_send()

    @pl.when(is_enc)
    def _():
        x_left.wait_send()
        for a in range(NT):
            halo_copies(a)[1].wait_send()
        for e in range(5):
            for c in exchanges[e]:
                c.wait_send()
        for c in kv_copies:
            c.wait_send()

        @pl.when(t == 0)
        def _():
            for c in mem_copies:
                c.wait_send()

        @pl.when(t > 0)
        def _():
            to_first.wait_send()
            dq_copy.wait_send()


def layer_call(lens, x, cot, wqkv, wout, wcross, wup, wdown, gain, bias):
    any_ = pl.BlockSpec(memory_space=pl.ANY)
    vmem = pl.BlockSpec(memory_space=pltpu.VMEM)
    M = R * MP
    W = W_ENC
    V = pltpu.VMEM
    S = pltpu.SemaphoreType.DMA
    scratch = [
        V((R, W, D), BF), V((R, MP, D), F32), V((R, T, D), F32),
        V((NT, 3, D, 128), BF), V((NT, 128, D), BF), V((NT, 2, D, 128), BF), V((NT, D, D), BF), V((NT, D, D), BF),
        V((NT, R, W, 128), BF), V((NT, R, W, 128), BF), V((NT, R, 128, W), BF), V((NT, R, 128, W), BF),
        V((NT, R, T, 128), BF), V((NT, R, 2, W, T), BF), V((R, NT, T, 128), BF), V((R, W, T), F32), V((2, T, 128), BF),
        V((R, T, D), F32), V((R, T, D), F32), V((8, 128), F32),
        V((R, T, 1), F32), V((R, T, 1), F32), V((8, 128), F32),
        V((R, T, D), F32), V((R, T, D), BF), V((R, T, D), BF),
        V((R, NT, T, D), BF), V((R, NT, T, D), BF), V((R, NT, T, D), BF),
        V((R, T, D), F32), V((R, T, D), BF), V((R, NT, T, 128), BF),
        V((NT, R, 2, T, 128), F32), V((R, NT, T, 384), BF), V((2, NT, R, 2, HALO, 128), BF),
        V((2, NT, R, 2, HALO, 128), BF), V((NT, R, 2, MP, 128), BF), V((NT, NT, R, 2, MP, 128), BF),
        V((NT, NT, M, 128), BF), V((NT, M, 128), F32), V((NT, M, D), BF), V((NT, M, D), BF), V((NT, M, D), BF),
        V((NT, NT, M, 128), BF), V((NT, R, 2 * MP, 128), BF),
        V((NT, 2, M, 128), BF), V((NT, 2, M, 128), F32), V((NT, 2, M, 128), F32),
        V((R, 256, D), BF), V((R, 256, D), BF), V((R, 256, T), BF), V((R, T, D), BF), V((R, T, D), BF),
        V((M, D), F32), V((M, D), F32), V((M, D), F32), V((M, 1), F32), V((M, 1), F32), V((M, 1), F32),
        V((M, D), F32), V((M, D), BF), V((M, D), F32), V((M, D), F32), V((M, D), BF), V((2, M, 128), F32),
        V((M, D), F32),
        S((9,)), S((5, 7)), S((5, 7)), S((2,)), S((2,)), S((2, 3)), S((2,)), S((5, 3)), S((5, 3)),
        S((NT,)), S((NT,)), S((NT,)), S((NT,)), S((2, NT)), S((2, NT)), S((1,)), S((NT,)), S((1,)), S((NT,)),
    ]
    return pl.pallas_call(
        layer_kernel,
        out_shape=(
            jax.ShapeDtypeStruct((R, T, D), F32),
            jax.ShapeDtypeStruct((R, T, D), F32),
            jax.ShapeDtypeStruct((NT, G_ROWS, 128), BF),
            jax.ShapeDtypeStruct((8, D), F32),
        ),
        in_specs=[pl.BlockSpec(memory_space=pltpu.SMEM)] + [any_] * 7 + [vmem] * 2,
        out_specs=(vmem,) * 4,
        scratch_shapes=scratch,
        compiler_params=pltpu.CompilerParams(
            collective_id=0, has_side_effects=True, vmem_limit_bytes=60 * 1024 * 1024
        ),
        name="layers",
    )(lens, x, cot, wqkv, wout, wcross, wup, wdown, gain, bias)


CHUNKS = ((G_DOWN, 2048), (G_UP, 2048), (G_CROSS, 1024), (G_OUT, 2048))
HALF = G_ROWS // 2


def reduce_kernel(
    chips, g, ng, o_qkv, o_out, o_cross, o_up, o_down, o_gain, o_bias,
    r1, h, r2, y, r3, full, ny, nc, nx,
    s1, q1, s2, q2, s3, q3, s4, q4, s5, q5, ns, nq,
):
    dp = lax.axis_index("dp")
    t = lax.axis_index("tensor")
    core = lax.rem(dp, 2)
    chip = lax.div(dp, 2)
    sib = dp + 1 - 2 * core

    def chip_at(off):
        return lax.rem(chip + off, chips)

    barrier = pltpu.get_barrier_semaphore()
    for off in (1, 2, 3):
        pl.semaphore_signal(barrier, inc=1, device_id={"tensor": lax.rem(t + off, NT)}, device_id_type=MESH)
    pl.semaphore_signal(barrier, inc=1, device_id={"dp": sib}, device_id_type=MESH)
    for off in range(1, chips):
        pl.semaphore_signal(barrier, inc=1, device_id={"dp": chip_at(off) * 2 + core}, device_id_type=MESH)
    pl.semaphore_wait(barrier, 4 + chips - 1)

    def at(k):
        return CHUNKS[k][0] // 2, CHUNKS[k][1] // 2

    def piece(k):
        return CHUNKS[k][1] // 2 // chips

    def c1(k):
        start, n = CHUNKS[k]
        lo, hf = at(k)
        return [remote(g.at[:, pl.ds(start + (1 - core) * hf, hf), :], r1.at[:, pl.ds(lo, hf), :],
                       s1.at[k], q1.at[k], dp=sib)]

    def c2(k):
        lo, hf = at(k)
        out = []
        for off in (1, 2, 3):
            to = lax.rem(t + off, NT)
            out.append(remote(h.at[to, pl.ds(lo, hf), :], r2.at[off - 1, pl.ds(lo, hf), :],
                              s2.at[k, off - 1], q2.at[k, off - 1], tensor=to))
        return out

    def c3(k):
        lo, hf = at(k)
        n = piece(k)
        out = []
        for off in range(1, chips):
            to = chip_at(off)
            out.append(remote(y.at[pl.ds(lo + to * n, n), :], r3.at[off - 1, pl.ds(lo // chips, n), :],
                              s3.at[k, off - 1], q3.at[k, off - 1], dp=to * 2 + core))
        return out

    def c4(k):
        start, _ = CHUNKS[k]
        lo, hf = at(k)
        n = piece(k)
        mine = full.at[pl.ds(start + core * hf + chip * n, n), :]
        out = []
        for off in range(1, chips):
            out.append(remote(mine, mine, s4.at[k, off - 1], q4.at[k, off - 1], dp=chip_at(off) * 2 + core))
        return out

    def c5(k):
        start, _ = CHUNKS[k]
        lo, hf = at(k)
        mine = full.at[pl.ds(start + core * hf, hf), :]
        return [remote(mine, mine, s5.at[k], q5.at[k], dp=sib)]

    def go(copies):
        for c in copies:
            c.start()

    def come(copies):
        for c in copies:
            c.wait_recv()

    def gone(copies):
        for c in copies:
            c.wait_send()

    def stage(k, step):
        start, _ = CHUNKS[k]
        lo, hf = at(k)
        n = piece(k)
        if step == 0:
            go(c1(k))
        if step == 1:
            come(c1(k))
            for a in range(NT):
                h[a, lo:lo + hf] = (g[a, pl.ds(start + core * hf, hf)].astype(F32)
                                    + r1[a, lo:lo + hf].astype(F32)).astype(BF)
            go(c2(k))
        if step == 2:
            come(c2(k))
            tot = h[t, lo:lo + hf].astype(F32)
            for o in range(3):
                tot = tot + r2[o, lo:lo + hf].astype(F32)
            y[lo:lo + hf] = tot.astype(BF)
            go(c3(k))
        if step == 3:
            come(c3(k))
            tot = y[pl.ds(lo + chip * n, n)].astype(F32)
            for o in range(chips - 1):
                tot = tot + r3[o, lo // chips:lo // chips + n].astype(F32)
            full[pl.ds(start + core * hf + chip * n, n)] = tot.astype(BF)
            go(c4(k))
        if step == 4:
            come(c4(k))
            go(c5(k))
        if step == 5:
            come(c5(k))

    ny[t] = ng[...]
    n1 = [remote(ny.at[t], ny.at[t], ns.at[o - 1], nq.at[o - 1], tensor=lax.rem(t + o, NT)) for o in (1, 2, 3)]
    n2 = [remote(nc.at[0], nc.at[1], ns.at[3], nq.at[3], dp=sib)]
    n3 = [remote(nx.at[chip], nx.at[chip], ns.at[3 + o], nq.at[3 + o], dp=chip_at(o) * 2 + core)
          for o in range(1, chips)]
    go(n1)

    for tick in range(len(CHUNKS) + 5):
        for k in range(len(CHUNKS)):
            if 0 <= tick - k < 6:
                stage(k, tick - k)
        if tick == 1:
            come(n1)
            nc[0] = ny[0] + ny[1] + ny[2] + ny[3]
            go(n2)
        if tick == 2:
            come(n2)
            nx[chip] = nc[0] + nc[1]
            go(n3)
        if tick == 4:
            come(n3)
            tot = nx[0]
            for o in range(1, chips):
                tot = tot + nx[o]
            o_gain[...] = tot[0:3]
            o_bias[...] = tot[3:6]

    for j in range(3):
        o_qkv[j] = full[G_QKV + D * j:G_QKV + D * j + D].astype(F32)
    for j in range(2):
        o_cross[j] = full[G_CROSS + D * j:G_CROSS + D * j + D].astype(F32)
    for j in range(4):
        cols = slice(128 * j, 128 * j + 128)
        o_out[:, cols] = full[G_OUT + 128 * j:G_OUT + 128 * j + 128].astype(F32)
        o_up[:, cols] = full[G_UP + D * j:G_UP + D * j + D].astype(F32)
        o_down[:, cols] = full[G_DOWN + D * j:G_DOWN + D * j + D].astype(F32)

    for k in range(len(CHUNKS)):
        for c in (c1, c2, c3, c4, c5):
            gone(c(k))
    gone(n1)
    gone(n2)
    gone(n3)


def reduce_call(chips, g, ng):
    vmem = pl.BlockSpec(memory_space=pltpu.VMEM)
    V = pltpu.VMEM
    S = pltpu.SemaphoreType.DMA
    K = len(CHUNKS)
    o = max(chips - 1, 1)
    scratch = [
        V((NT, HALF, 128), BF), V((NT, HALF, 128), BF), V((3, HALF, 128), BF), V((HALF, 128), BF),
        V((o, HALF // chips, 128), BF), V((G_ROWS, 128), BF), V((NT, 8, D), F32), V((2, 8, D), F32),
        V((chips, 8, D), F32),
        S((K,)), S((K,)), S((K, 3)), S((K, 3)), S((K, o)), S((K, o)), S((K, o)), S((K, o)), S((K,)), S((K,)),
        S((4 + o,)), S((4 + o,)),
    ]

    def kernel(*refs):
        reduce_kernel(chips, *refs)

    return pl.pallas_call(
        kernel,
        out_shape=tuple(
            jax.ShapeDtypeStruct(s, F32)
            for s in ((3, D, 128), (128, D), (2, D, 128), (D, D), (D, D), (3, D), (3, D))
        ),
        in_specs=[vmem] * 2,
        out_specs=(vmem,) * 7,
        scratch_shapes=scratch,
        compiler_params=pltpu.CompilerParams(
            collective_id=1, has_side_effects=True, vmem_limit_bytes=60 * 1024 * 1024
        ),
        name="reduce",
    )(g, ng)


def solution(mesh):
    chips = mesh.shape["dp"] // 2

    def shards(inputs, lengths, w_qkv, w_out, w_cross, w_up, w_down, norm_gain, norm_bias, cotangent):
        y, dx, g, ng = layer_call(
            lengths, inputs[0], cotangent[0], w_qkv[0], w_out[0], w_cross[0], w_up[0], w_down[0],
            norm_gain[0], norm_bias[0])
        rest = reduce_call(chips, g, ng)
        return (y[None], dx[None]) + tuple(v[None] for v in rest)

    return jax.shard_map(
        shards,
        mesh=mesh,
        in_specs=(
            P("section", "dp", "tensor", None),
            P("dp", None),
            P("section", None, None, "tensor"),
            P("section", "tensor", None),
            P("section", None, None, "tensor"),
            P("section", None, "tensor"),
            P("section", "tensor", None),
            P("section", None, None),
            P("section", None, None),
            P("section", "dp", "tensor", None),
        ),
        out_specs=(
            P("section", "dp", "tensor", None),
            P("section", "dp", "tensor", None),
            P("section", None, None, "tensor"),
            P("section", "tensor", None),
            P("section", None, None, "tensor"),
            P("section", None, "tensor"),
            P("section", "tensor", None),
            P("section", None, None),
            P("section", None, None),
        ),
        check_vma=False,
    )
```

time: 1640 us -> 214 us (0.13)
  waiting for transfers between devices: 780 us -> 0 us
  blocking collectives: 384 us -> 0 us
  matrix products: 222 us -> 0 us
  Pallas kernels: 0 us -> 199 us
  other arithmetic: 151 us -> 0 us
  local copies, waits for them, and re-layouts: 48.5 us -> 13.5 us
  between operations: 19.1 us -> 0.7 us
  starting transfers between devices: 17.4 us -> 0 us
    reduce_scatter x24 -> x0, waiting for transfers between devices: 407 us -> none  [the longest x15 270 us: leave_rows(): lax.psum_scatter(term.astype(jnp.bfloat16), 'tensor', scatter_dimension=1...]
    psum x6 -> x0, blocking collectives: 384 us -> none  [the longest x1 319 us: shards(): total_gain, total_bias = lax.psum((grad_gain, grad_bias), ('dp', 'tensor'))]
    all_gather x21 -> x0, waiting for transfers between devices: 365 us -> none  [the longest x12 215 us: enter_rows(): return lax.all_gather(row_vals, 'tensor', axis=1, tiled=True)]
    dot_general x130 -> x0, matrix products: 205 us -> none  [the longest x33 50.5 us: project_back(): jnp.einsum('bnk,dk->bnd', gradients, weight, preferred_element_type=jnp.f...]
    pallas_call x0 -> x2, Pallas kernels: none -> 199 us  [the longest x1 121 us: layer_call(): pl.pallas_call(layer_kernel, out_shape=(jax.ShapeDtypeStruct((R, T, D), F...]
    reduce_sum x51 -> x0, other arithmetic: 59.7 us -> none  [the longest x11 24.2 us: layer_norm(): return centred * lax.rsqrt(spread + NORM_EPS) * gain_vec + bias_vec]
    convert_element_type x23 -> x0, other arithmetic: 35.1 us -> none  [the longest x5 14 us: attention_back(): d_scores = (attn_probs * (d_probs - centre)).astype(jnp.bfloat16)]
    select_n x20 -> x0, other arithmetic: 26.1 us -> none  [the longest x3 7.62 us: allowed_mask(): return jnp.where(decoder_side, causal, open_mask)]
  transfers between devices with their start and end apart: 54 -> 0, of which waited for: 44 -> 0; matrix products, arithmetic and copies ran while one was open for 16% -> 0% of each run, Pallas kernels for 0% -> 0%
where the time goes in v1:
time: 214 us; the launch traced here: 213 us
  Pallas kernels  199 us (93%)
  local copies, waits for them, and re-layouts  13.5 us (6%)
    pallas_call x1, Pallas kernels, layer_call(): pl.pallas_call(layer_kernel, out_shape=(jax.ShapeDtypeStruct((R, T, D), F...  121 us
    pallas_call x1, Pallas kernels, reduce_call(): pl.pallas_call(kernel, out_shape=tuple((jax.ShapeDtypeStruct(s, F32) for...  77.8 us
    unnamed x18, local copies, waits for them, and re-layouts  13.5 us

profile of v1, /device:TPU:1, one launch (start us, length us, event | category | flops | bytes accessed | tf_op | source)
XLA Modules:
  0.0 213.5 jit_solution(2879572699100109493)
XLA Ops:
  0.6 1.3 copy_bitcast_fusion
  2.0 121.4 %layers.1 = (f32[2,256,512]{2,1,0:T(8,128)}, f32[2,256,512]{2,1,0:T(8,128)}, bf16[4,7168,128]{2,1,0:T(8,128)(2,1)}, f32[8,512]{1,0:T(8,128)}) custom-call(s32[2,16]{1,0:T(2,128)} %lens.1, bf16[2,256,512]{2,1,0:T(8,128)(2,1)} %bitcast.26, f32[2,256,512]{2,1,0:T(8,128)} %bitcast.20, bf16[3,512,128]{2,1,0:T(8,128)(2,1)} %bitcast.30, bf16[128,512]{1,0:T(8,128)(2,1)} %bitcast.33, ...), custom_call_target="tpu_custom_call" | custom-call | tf_op jit(solution)/shard_map/layers/pallas_call | solution.py:897
  123.4 0.0 copy-start.1
  123.4 0.0 copy-start
  123.4 77.8 %reduce.1 = (f32[3,512,128]{2,1,0:T(8,128)}, f32[128,512]{1,0:T(8,128)}, f32[2,512,128]{2,1,0:T(8,128)}, f32[512,512]{1,0:T(8,128)}, f32[512,512]{1,0:T(8,128)}, /*index=5*/f32[3,512]{1,0:T(4,128)}, f32[3,512]{1,0:T(4,128)}) custom-call(bf16[4,7168,128]{2,1,0:T(8,128)(2,1)} %get-tuple-element.22.refs_0_, f32[8,512]{1,0:T(8,128)} %get-tuple-element.23.refs_1_), custom_call_target="tpu_custom_call" | custom-call | tf_op jit(solution)/shard_map/reduce/pallas_call | solution.py:1094
  201.2 0.0 copy-start.3
  201.2 0.0 copy-start.2
  201.3 1.4 copy.19
  202.7 1.3 copy.20
  204.0 0.0 copy-done.1
  204.0 1.0 copy.32
  205.0 0.0 copy-done
  205.0 1.0 copy.33
  205.9 2.1 copy.34
  208.0 1.7 copy.35
  209.7 1.9 copy.36
  211.5 0.0 copy-done.3
  211.5 1.0 copy.37
  212.5 0.0 copy-done.2
  212.5 1.0 copy.38
Async XLA Ops:
  123.4 80.6 %copy-start.1 = (f32[2,256,512]{2,1,0:T(8,128)S(1)}, f32[2,256,512]{2,1,0:T(8,128)}, u32[]{:S(2)}) copy-start(f32[2,256,512]{2,1,0:T(8,128)} %get-tuple-element.20) | copy-start | bytes 3145732
  123.4 81.6 %copy-start = (f32[2,256,512]{2,1,0:T(8,128)S(1)}, f32[2,256,512]{2,1,0:T(8,128)}, u32[]{:S(2)}) copy-start(f32[2,256,512]{2,1,0:T(8,128)} %get-tuple-element.21) | copy-start | bytes 3145732
  201.2 10.3 %copy-start.3 = (f32[512,512]{1,0:T(8,128)S(1)}, f32[512,512]{1,0:T(8,128)}, u32[]{:S(2)}) copy-start(f32[512,512]{1,0:T(8,128)} %get-tuple-element.27) | copy-start | bytes 3145732
  201.2 11.3 %copy-start.2 = (f32[512,512]{1,0:T(8,128)S(1)}, f32[512,512]{1,0:T(8,128)}, u32[]{:S(2)}) copy-start(f32[512,512]{1,0:T(8,128)} %get-tuple-element.28) | copy-start | bytes 3145732

commit v2 on v1

v2 whole, which is shorter than its diff:
```python
import jax
import jax.numpy as jnp
from jax import lax
from jax.experimental import pallas as pl
from jax.experimental.pallas import tpu as pltpu
from jax.sharding import PartitionSpec as P

F32 = jnp.float32
BF = jnp.bfloat16
MESH = pl.DeviceIdType.MESH
VMEM_BYTES = 62 * 1024 * 1024

MEM = 20
MP = 32
R = 2
T = 256
HALO = 160
D = 512
NT = 4
W_ENC = T + 2 * HALO + MP
W_DEC = T + HALO
MEM_AT = T + 2 * HALO
EPS = 1e-05
FILL = -1e30
SCALE = 0.125

G_DOWN, G_UP, G_CROSS, G_OUT, G_QKV, G_ROWS = 0, 2048, 4096, 5120, 5632, 7168
CHUNKS = ((G_DOWN, 2048), (G_UP, 2048), (G_CROSS, 1024), (G_OUT, 512), (G_QKV, 1536))
C_DOWN, C_UP, C_CROSS, C_OUT, C_QKV = range(5)
LATE = G_CROSS // 2
HALF = G_ROWS // 2
QKV, OUT, CROSS, UP, DOWN = range(5)
W_ROWS = (512, 128, 512, 512, 512)


def dot(a, b):
    return lax.dot_general(a, b, (((1,), (0,)), ((), ())), preferred_element_type=F32)


def dot_nt(a, b):
    return lax.dot_general(a, b, (((1,), (1,)), ((), ())), preferred_element_type=F32)


def dot_tn(a, b):
    return lax.dot_general(a, b, (((0,), (0,)), ((), ())), preferred_element_type=F32)


def remote(src, dst, send, recv, **device):
    return pltpu.make_async_remote_copy(
        src_ref=src, dst_ref=dst, send_sem=send, recv_sem=recv, device_id=device, device_id_type=MESH
    )


def normed(v):
    c = v - jnp.mean(v, axis=1, keepdims=True)
    rs = lax.rsqrt(jnp.mean(c * c, axis=1, keepdims=True) + EPS)
    return c * rs, rs


def norm_back(xhat, rs, gain, dy):
    dxh = dy * gain
    m1 = jnp.mean(dxh, axis=1, keepdims=True)
    m2 = jnp.mean(dxh * xhat, axis=1, keepdims=True)
    return rs * (dxh - m1 - xhat * m2)


def gelu_both(u):
    k = 0.7978845608028654
    u2 = u * u
    th = jnp.tanh(k * u * (1.0 + 0.044715 * u2))
    half = 0.5 * (1.0 + th)
    grad = half + 0.5 * u * (1.0 - th * th) * (k * (1.0 + 3.0 * 0.044715 * u2))
    return u * half, grad


def layer_kernel(chips, names, *refs):
    (lens, x_in, cot_in, wqkv_in, wout_in, wcross_in, wup_in, wdown_in, gain, bias,
     y_out, dx_out, full, ng_tot) = refs[:14]
    m = dict(zip(names, refs[14:]))
    x_ext, cotm, d32, wqkv, wout, wcross, wup, wdown = (
        m[n] for n in ("x_ext", "cotm", "d32", "wqkv", "wout", "wcross", "wup", "wdown"))
    kk, vv, vt, qs, pt, ctx, mask, hmask = (m[n] for n in ("kk", "vv", "vt", "qs", "pt", "ctx", "mask", "hmask"))
    xh1, xh2, rs1, rs2, h32, hb, h1b, act, gp, dab, dr = (
        m[n] for n in ("xh1", "xh2", "rs1", "rs2", "h32", "hb", "h1b", "act", "gp", "dab", "dr"))
    dkv, halo_s, halo_r, memd_s, memd_r = (m[n] for n in ("dkv", "halo_s", "halo_r", "memd_s", "memd_r"))
    ex_o, ex_st, ex_f, ex_m, ex_h, ex_dq, qm = (
        m[n] for n in ("ex_o", "ex_st", "ex_f", "ex_m", "ex_h", "ex_dq", "qm"))
    kvm, dkvm_s, dkvm_r, kblk, vblk, cpt, cq, cctx = (
        m[n] for n in ("kvm", "dkvm_s", "dkvm_r", "kblk", "vblk", "cpt", "cq", "cctx"))
    mx1, mx2, mx3, mr1, mr2, mr3, mh, mact, mgp, mc, mm, mst, md = (
        m[n] for n in ("mx1", "mx2", "mx3", "mr1", "mr2", "mr3", "mh", "mact", "mgp", "mc", "mm", "mst", "md"))
    g, r1, r2, r3, rx, ry, ysum, ng, ny, nc, nx = (
        m[n] for n in ("g", "r1", "r2", "r3", "rx", "ry", "ysum", "ng", "ny", "nc", "nx"))
    (lsem, wsend, wrecv, xsend, xrecv, msend, mrecv, esend, erecv, ksend, krecv, dsend, drecv,
     hsend, hrecv, gsend, grecv, qsend, qrecv) = (
        m[n] for n in ("lsem", "wsend", "wrecv", "xsend", "xrecv", "msend", "mrecv", "esend", "erecv", "ksend",
                       "krecv", "dsend", "drecv", "hsend", "hrecv", "gsend", "grecv", "qsend", "qrecv"))
    s1, q1, s2, q2, s3, q3, s4, q4, s5, q5, ns, nq = (
        m[n] for n in ("s1", "q1", "s2", "q2", "s3", "q3", "s4", "q4", "s5", "q5", "ns", "nq"))

    def g_row(i):
        return gain[0, i:i + 1]

    def b_row(i):
        return bias[0, i:i + 1]

    sec = lax.axis_index("section")
    dp = lax.axis_index("dp")
    t = lax.axis_index("tensor")
    core = lax.rem(dp, 2)
    chip = lax.div(dp, 2)
    sib = dp + 1 - 2 * core
    is_enc = sec == 0
    is_dec = sec == 1
    left = lax.rem(t + 3, NT)
    right = lax.rem(t + 1, NT)
    opp = lax.rem(t + 2, NT)
    other = 1 - sec

    def chip_at(off):
        return lax.rem(chip + off, chips)

    ins = (wqkv_in, wout_in, wcross_in, wup_in, wdown_in)
    ws = (wqkv, wout, wcross, wup, wdown)

    def part(i, ref, start, n):
        if i in (QKV, CROSS):
            return ref.at[:, pl.ds(start, n), :]
        return ref.at[pl.ds(start, n), :]

    def slot(i, a, start, n):
        if i in (QKV, CROSS):
            return ws[i].at[a, :, pl.ds(start, n), :]
        return ws[i].at[a, pl.ds(start, n), :]

    barrier = pltpu.get_barrier_semaphore()
    for off in (1, 2, 3):
        pl.semaphore_signal(barrier, inc=1, device_id={"tensor": lax.rem(t + off, NT)}, device_id_type=MESH)
    pl.semaphore_signal(barrier, inc=1, device_id={"dp": sib}, device_id_type=MESH)
    for b in range(NT):
        pl.semaphore_signal(barrier, inc=1, device_id={"section": other, "tensor": b}, device_id_type=MESH)
    for off in range(1, chips):
        pl.semaphore_signal(barrier, inc=1, device_id={"dp": chip_at(off) * 2 + core}, device_id_type=MESH)

    locals_ = [
        pltpu.make_async_copy(x_in, x_ext.at[:, pl.ds(0, T), :], lsem.at[0]),
        pltpu.make_async_copy(cot_in, d32, lsem.at[1]),
    ]
    for i in range(5):
        locals_.append(pltpu.make_async_copy(ins[i], ws[i].at[t], lsem.at[2 + i]))
    for c in locals_:
        c.start()

    pl.semaphore_wait(barrier, 8 + chips - 1)

    x_right = remote(x_in.at[:, pl.ds(T - HALO, HALO), :], x_ext.at[:, pl.ds(T, HALO), :],
                     xsend.at[0], xrecv.at[0], tensor=right)
    x_left = remote(x_in.at[:, pl.ds(0, HALO), :], x_ext.at[:, pl.ds(T + HALO, HALO), :],
                    xsend.at[1], xrecv.at[1], tensor=left)
    x_right.start()

    mem_x, mem_c = [], []
    for off in (1, 2, 3):
        to = lax.rem(t + off, NT)
        mem_x.append(remote(x_in.at[:, pl.ds(0, MP), :], x_ext.at[:, pl.ds(MEM_AT, MP), :],
                            msend.at[0, off - 1], mrecv.at[0], tensor=to))
        mem_c.append(remote(cot_in.at[:, pl.ds(0, MP), :], cotm, msend.at[1, off - 1], mrecv.at[1], tensor=to))
    mem_local = [
        pltpu.make_async_copy(x_in.at[:, pl.ds(0, MP), :], x_ext.at[:, pl.ds(MEM_AT, MP), :], lsem.at[7]),
        pltpu.make_async_copy(cot_in.at[:, pl.ds(0, MP), :], cotm, lsem.at[8]),
    ]

    @pl.when(is_enc)
    def _():
        x_left.start()

        @pl.when(t == 0)
        def _():
            for c in mem_x + mem_local:
                c.start()

    def w_copies(i):
        rows = W_ROWS[i]
        hf, qt = rows // 2, rows // 4
        mine = core * hf
        y_right = remote(part(i, ins[i], mine, hf), slot(i, t, mine, hf), wsend.at[i, 0], wrecv.at[i, 0], tensor=right)
        y_left = remote(part(i, ins[i], mine, hf), slot(i, t, mine, hf), wsend.at[i, 1], wrecv.at[i, 1], tensor=left)
        on_right = remote(slot(i, left, mine, qt), slot(i, left, mine, qt), wsend.at[i, 2], wrecv.at[i, 2], tensor=right)
        on_left = remote(slot(i, right, mine + qt, qt), slot(i, right, mine + qt, qt), wsend.at[i, 3], wrecv.at[i, 3],
                         tensor=left)
        s_left = remote(slot(i, left, mine, hf), slot(i, left, mine, hf), wsend.at[i, 4], wrecv.at[i, 4], dp=sib)
        s_right = remote(slot(i, right, mine, hf), slot(i, right, mine, hf), wsend.at[i, 5], wrecv.at[i, 5], dp=sib)
        s_opp = remote(slot(i, opp, mine, hf), slot(i, opp, mine, hf), wsend.at[i, 6], wrecv.at[i, 6], dp=sib)
        return y_right, y_left, on_right, on_left, s_left, s_right, s_opp

    copies = [w_copies(i) for i in range(5)]

    def send_first(i):
        copies[i][0].start()
        copies[i][1].start()

    def send_on(i):
        y_right, y_left, on_right, on_left, s_left, s_right, s_opp = copies[i]
        y_right.wait_recv()
        on_right.start()
        s_left.start()
        y_left.wait_recv()
        on_left.start()
        s_right.start()

    def send_opp(i):
        copies[i][2].wait_recv()
        copies[i][3].wait_recv()
        copies[i][6].start()

    def ready(i, rel):
        copies[i][4 + rel].wait_recv()

    send_first(QKV)
    send_first(OUT)

    lane = lax.broadcasted_iota(jnp.int32, (T, 128), 1)
    hmask[0] = jnp.where(lane < 64, 1.0, 0.0).astype(BF)
    hmask[1] = jnp.where(lane < 64, 0.0, 1.0).astype(BF)

    def segments(pos, r):
        off = pos - MEM
        seg = jnp.where(off >= 0, 1, 0)
        end = jnp.int32(0)
        for k in range(16):
            end = end + lens[r, k]
            seg = seg + jnp.where(off >= end, 1, 0)
        return seg

    def make_masks(width, encoder):
        for r in range(R):
            i = lax.broadcasted_iota(jnp.int32, (width, 128), 0)
            pos = jnp.where(i < T, i, jnp.where(i < T + HALO, i - T - HALO, i - HALO)) + t * T
            ks = segments(pos, r)
            for half in range(2):
                qpos = lax.broadcasted_iota(jnp.int32, (8, 128), 1) + (t * T + half * 128)
                q_seg = segments(qpos, r)[0:1]
                same = ks == q_seg
                if encoder:
                    ok = jnp.logical_or(jnp.logical_and(i < MEM_AT, jnp.logical_and(same, ks > 0)),
                                        jnp.logical_and(i >= MEM_AT, i < MEM_AT + MEM))
                else:
                    ok = jnp.logical_and(same, jnp.logical_and(pos <= qpos[0:1], pos >= 0))
                mask[r, 0:width, half * 128:half * 128 + 128] = jnp.where(ok, 0.0, FILL)

    @pl.when(is_enc)
    def _():
        make_masks(W_ENC, True)

    @pl.when(is_dec)
    def _():
        make_masks(W_DEC, False)

    ex_st[t] = jnp.zeros((R * MP, 128), F32)
    ng[...] = jnp.zeros(ng.shape, F32)

    locals_[0].wait()
    locals_[2 + QKV].wait()
    x_right.wait_recv()

    @pl.when(is_enc)
    def _():
        x_left.wait_recv()

        @pl.when(t == 0)
        def _():
            mem_local[0].wait()

        @pl.when(t > 0)
        def _():
            mem_x[0].wait_recv()

    def shard_at(step):
        return lax.rem(t + jnp.where(step == 0, 0, jnp.where(step == 1, 3, step - 1)), NT)

    lane_m = lax.broadcasted_iota(jnp.int32, (MP, 128), 1)
    low_m = lane_m < 64

    def project(a, width, encoder):
        wkv = jnp.concatenate([wqkv[a, 1], wqkv[a, 2]], axis=1)
        for r in range(R):
            kv = dot(x_ext[r, 0:width], wkv)
            k32, v32 = kv[:, 0:128], kv[:, 128:256]
            kk[a, r, 0:width] = k32.astype(BF)
            vv[a, r, 0:width] = v32.astype(BF)
            vt[a, r, :, 0:width] = v32.T.astype(BF)
            q = dot(x_ext[r, 0:T], wqkv[a, 0]).astype(BF)
            qs[a, r] = (q.astype(F32) * SCALE).astype(BF)
            if encoder:
                m32 = dot(x_ext[r, MEM_AT:MEM_AT + MP], wqkv[a, 0]).astype(BF).astype(F32) * SCALE
                lhs = jnp.concatenate([jnp.where(low_m, m32, 0.0), jnp.where(low_m, 0.0, m32)], axis=0).astype(BF)
                qm[a, r] = lhs
                s = dot_nt(lhs, k32[0:T].astype(BF))
                top = jnp.max(s, axis=1, keepdims=True)
                p = jnp.exp(s - top)
                total = jnp.sum(p, axis=1, keepdims=True)
                o = dot(p.astype(BF), v32[0:T].astype(BF)) / total
                ex_o[t, a, r * MP:r * MP + MP] = jnp.where(low_m, o[0:MP], o[MP:2 * MP]).astype(BF)
                st = ex_st[t, r * MP:r * MP + MP]
                st = jnp.where(lane_m == 2 * a, top[0:MP], st)
                st = jnp.where(lane_m == 2 * a + 1, top[MP:2 * MP], st)
                st = jnp.where(lane_m == 2 * a + 8, total[0:MP], st)
                st = jnp.where(lane_m == 2 * a + 9, total[MP:2 * MP], st)
                ex_st[t, r * MP:r * MP + MP] = st

    def ex_copies(e, buf):
        out = []
        for off in (1, 2, 3):
            out.append(remote(buf.at[t], buf.at[t], esend.at[e, off - 1], erecv.at[e, off - 1],
                              tensor=lax.rem(t + off, NT)))
        return out

    exchanges = [ex_copies(e, buf) for e, buf in enumerate((ex_o, ex_st, ex_f, ex_m, ex_h))]

    def ex_start(e):
        for c in exchanges[e]:
            c.start()

    def ex_wait(e):
        for c in exchanges[e]:
            c.wait_recv()

    def wide(ref, r):
        return jnp.concatenate([ref[r, a] for a in range(NT)], axis=1)

    def w_out_full():
        return wout[...].reshape(D, D)

    def mem_combine():
        for r in range(R):
            rows = slice(r * MP, r * MP + MP)
            sts = [ex_st[s, rows] for s in range(NT)]
            top = jnp.maximum(jnp.maximum(sts[0], sts[1]), jnp.maximum(sts[2], sts[3]))
            wts = [pltpu.roll(sts[s], 120, 1) * jnp.exp(sts[s] - top) for s in range(NT)]
            total = wts[0] + wts[1] + wts[2] + wts[3]
            total = jnp.where(lane_m < 8, total, 1.0)
            inv = 1.0 / total
            mst[0, rows] = jnp.where(lane_m < 8, top + jnp.log(total), 0.0)
            for a in range(NT):
                acc = jnp.zeros((MP, 128), F32)
                for s in range(NT):
                    w = wts[s] * inv
                    wide_w = jnp.where(low_m, w[:, 2 * a:2 * a + 1], w[:, 2 * a + 1:2 * a + 2])
                    acc = acc + wide_w * ex_o[s, a, rows].astype(F32)
                mc[rows, a * 128:a * 128 + 128] = acc

    def mem_first():
        mem_combine()
        xm = jnp.concatenate([x_ext[r, MEM_AT:MEM_AT + MP] for r in range(R)], axis=0).astype(F32)
        xh, rs = normed(xm + dot(mc[...].astype(BF), w_out_full()))
        mx1[...] = xh
        mr1[...] = rs
        h = xh * g_row(0) + b_row(0)
        mh[...] = h
        av, gv = gelu_both(dot(h.astype(BF), wup[t]))
        mact[...] = av.astype(BF)
        mgp[...] = gv
        ex_f[t] = dot(av.astype(BF), wdown[t]).astype(BF)
        ex_start(2)

    kv_copies = [remote(kvm.at[t], kvm.at[t], ksend.at[b], krecv.at[t], section=other, tensor=b) for b in range(NT)]

    def mem_second():
        third = mh[...]
        for s in range(NT):
            third = third + ex_f[s].astype(F32)
        xh, rs = normed(third)
        mx2[...] = xh
        mr2[...] = rs
        y = xh * g_row(1) + b_row(1)
        md[...] = y
        xh, rs = normed(y)
        mx3[...] = xh
        mr3[...] = rs
        mv = (xh * g_row(2) + b_row(2)).astype(BF)
        mm[...] = mv
        kvm[t, 0] = dot(mv, wcross[t, 0]).astype(BF)
        kvm[t, 1] = dot(mv, wcross[t, 1]).astype(BF)
        for c in kv_copies:
            c.start()

    def attend(a, r, width):
        tops = []
        for h in range(2):
            s = dot_nt(kk[a, r, 0:width], qs[a, r] * hmask[h]) + mask[r, 0:width]
            p = jnp.exp(s - jnp.max(s, axis=0, keepdims=True))
            p = (p * (1.0 / jnp.sum(p, axis=0, keepdims=True))).astype(BF)
            pt[a, r, h, 0:width] = p
            tops.append(dot(vt[a, r, h * 64:h * 64 + 64, 0:width], p))
        ctx[r, a] = jnp.concatenate(tops, axis=0).T.astype(BF)

    @pl.loop(0, NT * R)
    def _(i):
        @pl.when(i == 1)
        def _():
            send_on(QKV)

            @pl.when(is_dec)
            def _():
                send_first(CROSS)

            send_first(UP)
            send_first(DOWN)
            ready(QKV, 0)
            ready(QKV, 1)

        @pl.when(i == 2)
        def _():
            send_opp(QKV)
            ready(QKV, 2)
            send_on(OUT)

        step_from = jnp.where(i == 0, 0, jnp.where(i == 1, 1, jnp.where(i == 2, 3, 4)))
        step_to = jnp.where(i == 0, 1, jnp.where(i == 1, 3, 4))

        @pl.loop(step_from, step_to)
        def _(step):
            @pl.when(is_enc)
            def _():
                project(shard_at(step), W_ENC, True)

            @pl.when(is_dec)
            def _():
                project(shard_at(step), W_DEC, False)

        @pl.when(i == 2)
        def _():
            @pl.when(is_enc)
            def _():
                ex_start(0)
                ex_start(1)

        @pl.when(i == 4)
        def _():
            send_opp(OUT)
            locals_[2 + OUT].wait()
            for rel in range(3):
                ready(OUT, rel)

            @pl.when(is_dec)
            def _():
                send_on(CROSS)

            @pl.when(is_enc)
            def _():
                locals_[2 + UP].wait()
                locals_[2 + DOWN].wait()
                ex_wait(0)
                ex_wait(1)
                mem_first()

        @pl.when(i == 6)
        def _():
            send_on(UP)

            @pl.when(is_enc)
            def _():
                locals_[2 + CROSS].wait()
                ex_wait(2)
                mem_second()

        a = shard_at(lax.div(i, 2))
        r = lax.rem(i, 2)

        @pl.when(is_enc)
        def _():
            attend(a, r, W_ENC)

        @pl.when(is_dec)
        def _():
            attend(a, r, W_DEC)

    @pl.when(is_dec)
    def _():
        send_opp(CROSS)
        locals_[2 + CROSS].wait()
        locals_[2 + UP].wait()
        locals_[2 + DOWN].wait()

    send_on(DOWN)

    @pl.when(jnp.logical_and(is_enc, t == 0))
    def _():
        for c in mem_c:
            c.start()

    @pl.loop(0, R)
    def _(r):
        a0 = x_ext[r, 0:T].astype(F32) + dot(wide(ctx, r), w_out_full())
        xh, rs = normed(a0)
        xh1[r] = xh
        rs1[r] = rs
        h = xh * g_row(0) + b_row(0)
        h32[r] = h
        hb[r] = h.astype(BF)

    send_opp(UP)

    pad_mask = jnp.where(
        lax.rem(lax.broadcasted_iota(jnp.int32, (256, T), 0), MP) < MEM, 0.0, FILL)

    def full_cross(j):
        return jnp.concatenate([wcross[a, j] for a in range(NT)], axis=1)

    def cross_forward():
        for rel in range(3):
            ready(CROSS, rel)
        wc0 = full_cross(0)
        wc1 = full_cross(1)
        kblk[...] = jnp.zeros(kblk.shape, BF)
        vblk[...] = jnp.zeros(vblk.shape, BF)

        @pl.loop(0, R)
        def _(r):
            h1b[r] = hb[r]
            q = dot(hb[r], wc0).astype(BF)
            cq[r] = (q.astype(F32) * SCALE).astype(BF)

        for b in range(NT):
            remote(kvm.at[b], kvm.at[b], ksend.at[b], krecv.at[b], section=other, tensor=b).wait_recv()
        for r in range(R):
            for a in range(NT):
                for h in range(2):
                    at = slice(a * 64 + h * MP, a * 64 + h * MP + MP)
                    kblk[r, at, a * 128:a * 128 + 128] = kvm[a, 0, r * MP:r * MP + MP] * hmask[h, 0:MP]
                    vblk[r, at, a * 128:a * 128 + 128] = kvm[a, 1, r * MP:r * MP + MP] * hmask[h, 0:MP]

        @pl.loop(0, R)
        def _(r):
            s = dot_nt(kblk[r], cq[r]) + pad_mask
            s = s.reshape(8, MP, T)
            p = jnp.exp(s - jnp.max(s, axis=1, keepdims=True))
            p = p * (1.0 / jnp.sum(p, axis=1, keepdims=True))
            p = p.reshape(256, T).astype(BF)
            cpt[r] = p
            c = dot_tn(p, vblk[r]).astype(BF)
            cctx[r] = c
            xh, rs = normed(h32[r] + dot_nt(c, wc1))
            xh2[r] = xh
            rs2[r] = rs
            h = xh * g_row(1) + b_row(1)
            h32[r] = h
            hb[r] = h.astype(BF)

    @pl.when(is_dec)
    def _():
        cross_forward()

    @pl.loop(0, NT * R)
    def _(i):
        for rel in range(3):
            @pl.when(i == 2 * rel + 2)
            def _():
                ready(UP, rel)

        a = shard_at(lax.div(i, 2))
        r = lax.rem(i, 2)
        av, gv = gelu_both(dot(hb[r], wup[a]))
        act[r, a] = av.astype(BF)
        gp[r, a] = gv.astype(BF)

    send_opp(DOWN)
    for rel in range(3):
        ready(DOWN, rel)
    locals_[1].wait()

    last = jnp.where(is_enc, 1, 2)
    g_last = jnp.where(is_enc, g_row(1), g_row(2))
    b_last = jnp.where(is_enc, b_row(1), b_row(2))

    def add_norm(at, xh, dy):
        ng[pl.ds(at, 1)] += jnp.sum(dy * xh, axis=0, keepdims=True)
        ng[pl.ds(at + 3, 1)] += jnp.sum(dy, axis=0, keepdims=True)

    row_i = lax.broadcasted_iota(jnp.int32, (T, D), 0)
    is_mem_row = jnp.logical_and(row_i < MEM, jnp.logical_and(is_enc, t == 0))

    @pl.loop(0, R)
    def _(r):
        third = h32[r]
        for a in range(NT):
            third = third + dot(act[r, a], wdown[a])
        xh, rs = normed(third)
        h32[r] = xh * g_last + b_last
        dy = jnp.where(is_mem_row, 0.0, d32[r])
        d3 = norm_back(xh, rs, g_last, dy)
        ng[pl.ds(last, 1)] += jnp.sum(dy * xh, axis=0, keepdims=True)
        ng[pl.ds(last + 3, 1)] += jnp.sum(dy, axis=0, keepdims=True)
        d32[r] = d3
        dab[r] = d3.astype(BF)

    @pl.when(jnp.logical_and(is_enc, t == 0))
    def _():
        for r in range(R):
            h32[r, 0:24] = jnp.where(
                lax.broadcasted_iota(jnp.int32, (24, D), 0) < MEM, md[r * MP:r * MP + 24], h32[r, 0:24])

    y_copy = pltpu.make_async_copy(h32, y_out, lsem.at[9])
    y_copy.start()

    def at(k):
        return CHUNKS[k][0], CHUNKS[k][0] // 2, CHUNKS[k][1] // 2

    def own_half(k):
        start, lo, hf = at(k)
        return start + core * hf

    def pair(k, a):
        start, lo, hf = at(k)
        return remote(g.at[a, pl.ds(start + (1 - core) * hf, hf), :], r1.at[a, pl.ds(lo, hf), :],
                      s1.at[k, a], q1.at[k, a], dp=sib)

    def pair_sum(k, a):
        start, lo, hf = at(k)
        rows = pl.ds(own_half(k), hf)
        g[a, rows] = (g[a, rows].astype(F32) + r1[a, lo:lo + hf].astype(F32)).astype(BF)

    def over_tensor(k, a):
        start, lo, hf = at(k)
        rel = lax.rem(a - t + NT, NT) - 1
        return remote(g.at[a, pl.ds(own_half(k), hf), :], r2.at[rel, pl.ds(lo - LATE, hf), :],
                      s2.at[k, rel], q2.at[k, rel], tensor=a)

    def from_tensor(k, rel):
        start, lo, hf = at(k)
        return remote(g.at[0, pl.ds(own_half(k), hf), :], r2.at[rel, pl.ds(lo - LATE, hf), :],
                      s2.at[k, rel], q2.at[k, rel], tensor=right)

    def tensor_sum(k):
        start, lo, hf = at(k)
        tot = g[t, pl.ds(own_half(k), hf)].astype(F32)
        for rel in range(3):
            tot = tot + r2[rel, lo - LATE:lo - LATE + hf].astype(F32)
        ysum[lo - LATE:lo - LATE + hf] = tot.astype(BF)

    def over_chips(k):
        start, lo, hf = at(k)
        n = hf // chips
        out = []
        for off in range(1, chips):
            to = chip_at(off)
            out.append(remote(ysum.at[pl.ds(lo - LATE + to * n, n), :],
                              r3.at[off - 1, pl.ds((lo - LATE) // chips, n), :],
                              s3.at[k, off - 1], q3.at[k, off - 1], dp=to * 2 + core))
        return out

    def chips_sum(k):
        start, lo, hf = at(k)
        n = hf // chips
        tot = ysum[pl.ds(lo - LATE + chip * n, n)].astype(F32)
        for o in range(chips - 1):
            tot = tot + r3[o, (lo - LATE) // chips:(lo - LATE) // chips + n].astype(F32)
        full[pl.ds(own_half(k) + chip * n, n)] = tot.astype(BF)

    def chips_first(k):
        start, lo, hf = at(k)
        n = hf // chips
        out = []
        for off in range(1, chips):
            to = chip_at(off)
            out.append(remote(g.at[:, pl.ds(own_half(k) + to * n, n), :],
                              rx.at[off - 1, :, pl.ds(lo // chips, n), :],
                              s3.at[k, off - 1], q3.at[k, off - 1], dp=to * 2 + core))
        return out

    def chips_first_sum(k):
        start, lo, hf = at(k)
        n = hf // chips
        rows = pl.ds(own_half(k) + chip * n, n)
        for a in range(NT):
            tot = g[a, rows].astype(F32)
            for o in range(chips - 1):
                tot = tot + rx[o, a, lo // chips:lo // chips + n].astype(F32)
            ry[3, a, lo // chips:lo // chips + n] = tot.astype(BF)

    def tensor_second(k):
        start, lo, hf = at(k)
        n = hf // chips
        out = []
        for off in (1, 2, 3):
            to = lax.rem(t + off, NT)
            out.append(remote(ry.at[3, to, pl.ds(lo // chips, n), :], ry.at[off - 1, 0, pl.ds(lo // chips, n), :],
                              s2.at[k, off - 1], q2.at[k, off - 1], tensor=to))
        return out

    def tensor_second_sum(k):
        start, lo, hf = at(k)
        n = hf // chips
        tot = ry[3, t, lo // chips:lo // chips + n].astype(F32)
        for o in range(3):
            tot = tot + ry[o, 0, lo // chips:lo // chips + n].astype(F32)
        full[pl.ds(own_half(k) + chip * n, n)] = tot.astype(BF)

    def spread(k):
        start, lo, hf = at(k)
        n = hf // chips
        mine = full.at[pl.ds(own_half(k) + chip * n, n), :]
        return [remote(mine, mine, s4.at[k, off - 1], q4.at[k, off - 1], dp=chip_at(off) * 2 + core)
                for off in range(1, chips)]

    def hand(k):
        start, lo, hf = at(k)
        mine = full.at[pl.ds(own_half(k), hf), :]
        return [remote(mine, mine, s5.at[k], q5.at[k], dp=sib)]

    def go(cs):
        for c in cs:
            c.start()

    def come(cs):
        for c in cs:
            c.wait_recv()

    def gone(cs):
        for c in cs:
            c.wait_send()

    def all_pairs(k):
        for a in range(NT):
            pair(k, a).start()

    def all_pairs_sum(k):
        for a in range(NT):
            pair(k, a).wait_recv()
            pair_sum(k, a)

    def spread_chunk(k):
        come(spread(k))
        go(hand(k))

    @pl.loop(0, NT)
    def _(a):
        for r in range(R):
            gp[r, a] = (dot_nt(dab[r], wdown[a]) * gp[r, a].astype(F32)).astype(BF)
        wd = dot_tn(act[0, a], dab[0]) + dot_tn(act[1, a], dab[1])
        wu = dot_tn(hb[0], gp[0, a]) + dot_tn(hb[1], gp[1, a])
        for j in range(4):
            g[a, G_DOWN + D * j:G_DOWN + D * (j + 1)] = wd[:, 128 * j:128 * j + 128].astype(BF)
            g[a, G_UP + D * j:G_UP + D * (j + 1)] = wu[:, 128 * j:128 * j + 128].astype(BF)

        @pl.when(jnp.logical_or(is_dec, a != t))
        def _():
            pair(C_DOWN, a).start()
            pair(C_UP, a).start()

    @pl.loop(0, R)
    def _(r):
        d = d32[r]
        for a in range(NT):
            d = d + dot_nt(gp[r, a], wup[a])
        d32[r] = d

    dkv_copies = [
        remote(dkvm_s.at[b], dkvm_r.at[t], dsend.at[b], drecv.at[t], section=other, tensor=b) for b in range(NT)
    ]

    def cross_backward():
        wc0 = full_cross(0)
        wc1 = full_cross(1)

        @pl.loop(0, R)
        def _(r):
            dy = d32[r]
            add_norm(1, xh2[r], dy)
            d2 = norm_back(xh2[r], rs2[r], g_row(1), dy)
            d32[r] = d2
            dcb = d2.astype(BF)
            dab[r] = dcb
            dc = dot(dcb, wc1).astype(BF)
            p = cpt[r].astype(F32).reshape(8, MP, T)
            dp_ = dot_nt(vblk[r], dc).reshape(8, MP, T)
            ds = p * (dp_ - jnp.sum(p * dp_, axis=1, keepdims=True))
            ds = ds.reshape(256, T).astype(BF)
            dk = dot(ds, cq[r])
            dv = dot(cpt[r], dc)
            rows = pl.ds(pl.multiple_of(r * MP, MP), MP)
            for a in range(NT):
                for j, val in ((0, dk), (1, dv)):
                    dkvm_s[a, j, rows] = jnp.where(
                        low_m, val[64 * a:64 * a + MP, 128 * a:128 * a + 128],
                        val[64 * a + MP:64 * a + 2 * MP, 128 * a:128 * a + 128])
            dq = (dot_tn(ds, kblk[r]) * SCALE).astype(BF)
            cq[r] = dq

        for c in dkv_copies:
            c.start()

        gq = dot_tn(h1b[0], cq[0]) + dot_tn(h1b[1], cq[1])
        go_ = dot_tn(dab[0], cctx[0]) + dot_tn(dab[1], cctx[1])
        for a in range(NT):
            g[a, G_CROSS:G_CROSS + D] = gq[:, 128 * a:128 * a + 128].astype(BF)
            g[a, G_CROSS + D:G_CROSS + 2 * D] = go_[:, 128 * a:128 * a + 128].astype(BF)
        all_pairs(C_CROSS)

        @pl.loop(0, R)
        def _(r):
            d32[r] += dot_nt(cq[r], wc0)

        for k in (C_DOWN, C_UP):
            all_pairs_sum(k)
            go(chips_first(k))

    @pl.when(is_dec)
    def _():
        cross_backward()

    @pl.loop(0, R)
    def _(r):
        dy = d32[r]
        add_norm(0, xh1[r], dy)
        d1 = norm_back(xh1[r], rs1[r], g_row(0), dy)
        d32[r] = d1
        db = d1.astype(BF)
        dab[r] = db
        drr = dot_nt(db, w_out_full()).astype(BF)
        for a in range(NT):
            dr[r, a] = drr[:, 128 * a:128 * a + 128]

    wo_all = dot_tn(wide(ctx, 0), dab[0]) + dot_tn(wide(ctx, 1), dab[1])
    for a in range(NT):
        for j in range(4):
            g[a, G_OUT + 128 * j:G_OUT + 128 * j + 128] = (
                wo_all[128 * a:128 * a + 128, 128 * j:128 * j + 128].astype(BF))

    def out_pairs(a):
        @pl.when(jnp.logical_or(is_dec, a != t))
        def _():
            pair(C_OUT, a).start()

    for a in range(NT):
        out_pairs(a)

    def attend_back(a, r, width, encoder):
        dk = jnp.zeros((width, 128), F32)
        dv = jnp.zeros((width, 128), F32)
        dqs = []
        kt = kk[a, r, 0:width].astype(F32).T.astype(BF)
        for h in range(2):
            q_h = qs[a, r] * hmask[h]
            dr_h = dr[r, a] * hmask[h]
            pb = pt[a, r, h, 0:width]
            p = pb.astype(F32)
            dp_ = dot_nt(vv[a, r, 0:width], dr_h)
            ds = (p * (dp_ - jnp.sum(p * dp_, axis=0, keepdims=True))).astype(BF)
            dqs.append(dot(kt[h * 64:h * 64 + 64], ds))
            dk = dk + dot(ds, q_h)
            dv = dv + dot(pb, dr_h)
        act[r, a, :, 0:128] = (jnp.concatenate(dqs, axis=0).T * SCALE).astype(BF)
        for j, val in ((0, dk), (1, dv)):
            dkv[a, r, j] = val[0:T]
            halo_s[0, a, r, j] = val[T:T + HALO].astype(BF)
            if encoder:
                halo_s[1, a, r, j] = val[T + HALO:T + 2 * HALO].astype(BF)
                memd_s[a, r, j] = val[MEM_AT:MEM_AT + MP].astype(BF)

    def halo_copies(a):
        return (remote(halo_s.at[0, a], halo_r.at[0, a], hsend.at[0, a], hrecv.at[0, a], tensor=left),
                remote(halo_s.at[1, a], halo_r.at[1, a], hsend.at[1, a], hrecv.at[1, a], tensor=right))

    first = jnp.where(t == 0, 1.0, 0.0)
    dq_copy = remote(ex_dq.at[t], ex_dq.at[t], qsend.at[0], qrecv.at[t], tensor=0)

    def add_g(start, val):
        n = val.shape[0]
        g[t, start:start + n] = (g[t, start:start + n].astype(F32) + val).astype(BF)

    def add_norm_m(at_, xh, dy):
        ng[at_:at_ + 1] += first * jnp.sum(dy * xh, axis=0, keepdims=True)
        ng[at_ + 3:at_ + 4] += first * jnp.sum(dy, axis=0, keepdims=True)

    def mem_back_first():
        for b in range(NT):
            remote(dkvm_s.at[b], dkvm_r.at[b], dsend.at[b], drecv.at[b], section=other, tensor=b).wait_recv()
        grads = []
        for j in range(2):
            tot = dkvm_r[0, j] + dkvm_r[1, j] + dkvm_r[2, j] + dkvm_r[3, j]
            grads.append(tot.astype(BF))
        ex_m[t] = (dot_nt(grads[0], wcross[t, 0]) + dot_nt(grads[1], wcross[t, 1])).astype(BF)
        ex_start(3)
        for j in range(2):
            g[t, G_CROSS + D * j:G_CROSS + D * j + D] = dot_tn(mm[...], grads[j]).astype(BF)
        pair(C_CROSS, t).start()

    def mem_back_second():
        ex_wait(3)
        dm = ex_m[0].astype(F32)
        for s in range(1, NT):
            dm = dm + ex_m[s].astype(F32)
        add_norm_m(2, mx3[...], dm)
        rows_m = lax.broadcasted_iota(jnp.int32, (R * MP, D), 0)

        @pl.when(t == 0)
        def _():
            mem_local[1].wait()

        @pl.when(t > 0)
        def _():
            mem_c[0].wait_recv()

        cm = jnp.concatenate([cotm[0], cotm[1]], axis=0)
        cm = jnp.where(lax.rem(rows_m, MP) < MEM, cm, 0.0)
        dy = cm + norm_back(mx3[...], mr3[...], g_row(2), dm)
        add_norm_m(1, mx2[...], dy)
        d3 = norm_back(mx2[...], mr2[...], g_row(1), dy)
        md[...] = d3
        d3b = d3.astype(BF)
        dum = (dot_nt(d3b, wdown[t]) * mgp[...]).astype(BF)
        ex_h[t] = dot_nt(dum, wup[t]).astype(BF)
        ex_start(4)
        wd = dot_tn(mact[...], d3b)
        wu = dot_tn(mh[...].astype(BF), dum)
        for j in range(4):
            add_g(G_DOWN + D * j, wd[:, 128 * j:128 * j + 128])
            add_g(G_UP + D * j, wu[:, 128 * j:128 * j + 128])
        pair(C_DOWN, t).start()
        pair(C_UP, t).start()

    def mem_back_third():
        ex_wait(4)
        d2 = md[...]
        for s in range(NT):
            d2 = d2 + ex_h[s].astype(F32)
        add_norm_m(0, mx1[...], d2)
        d1 = norm_back(mx1[...], mr1[...], g_row(0), d2)
        md[...] = d1
        d1b = d1.astype(BF)
        drm = dot_nt(d1b, w_out_full()).astype(BF).astype(F32)
        mh[...] = drm
        prod = drm * mc[...]
        for r in range(R):
            acc = jnp.zeros((MP, 128), F32)
            for hh in range(8):
                cols = prod[r * MP:r * MP + MP, (hh // 2) * 128:(hh // 2) * 128 + 128]
                cols = jnp.where(low_m if hh % 2 == 0 else jnp.logical_not(low_m), cols, 0.0)
                acc = jnp.where(lane_m == hh, jnp.sum(cols, axis=1, keepdims=True), acc)
            mst[1, r * MP:r * MP + MP] = acc
        for a in range(NT):
            @pl.when(t == a)
            def _():
                wo = dot_tn(mc[:, 128 * a:128 * a + 128].astype(BF), d1b)
                for j in range(4):
                    add_g(G_OUT + 128 * j, wo[:, 128 * j:128 * j + 128])
        pair(C_OUT, t).start()

    def mem_attend_back():
        for a in range(NT):
            for r in range(R):
                rows = slice(r * MP, r * MP + MP)
                lse = mst[0, rows]
                dlt = mst[1, rows]
                lse = jnp.concatenate([lse[:, 2 * a:2 * a + 1], lse[:, 2 * a + 1:2 * a + 2]], axis=0)
                dlt = jnp.concatenate([dlt[:, 2 * a:2 * a + 1], dlt[:, 2 * a + 1:2 * a + 2]], axis=0)
                lhs = qm[a, r]
                ko, vo = kk[a, r, 0:T], vv[a, r, 0:T]
                p = jnp.exp(dot_nt(lhs, ko) - lse)
                dra = mh[rows, 128 * a:128 * a + 128]
                dra = jnp.concatenate([jnp.where(low_m, dra, 0.0), jnp.where(low_m, 0.0, dra)], axis=0).astype(BF)
                ds = (p * (dot_nt(dra, vo) - dlt)).astype(BF)
                dq = dot(ds, ko)
                ex_dq[t, a, rows] = (jnp.where(low_m, dq[0:MP], dq[MP:2 * MP]) * SCALE).astype(BF)
                dkv[a, r, 0] += dot_tn(ds, lhs)
                dkv[a, r, 1] += dot_tn(p.astype(BF), dra)

        @pl.when(t > 0)
        def _():
            dq_copy.start()

    @pl.loop(0, NT * R)
    def _(i):
        a = lax.div(i, 2)
        r = lax.rem(i, 2)

        @pl.when(is_enc)
        def _():
            attend_back(a, r, W_ENC, True)

        @pl.when(is_dec)
        def _():
            attend_back(a, r, W_DEC, False)

        @pl.when(r == 1)
        def _():
            to_left, to_right = halo_copies(a)
            to_left.start()

            @pl.when(is_enc)
            def _():
                to_right.start()

        @pl.when(is_dec)
        def _():
            @pl.when(i == 1)
            def _():
                all_pairs_sum(C_CROSS)
                for off in (1, 2, 3):
                    over_tensor(C_CROSS, lax.rem(t + off, NT)).start()
                all_pairs_sum(C_OUT)
                for off in (1, 2, 3):
                    over_tensor(C_OUT, lax.rem(t + off, NT)).start()

        @pl.when(is_enc)
        def _():
            @pl.when(i == 2)
            def _():
                mem_back_first()

            @pl.when(i == 4)
            def _():
                mem_back_second()

            @pl.when(i == 6)
            def _():
                for k in (C_DOWN, C_UP):
                    all_pairs_sum(k)
                    go(chips_first(k))
                mem_back_third()

    to_first = remote(memd_s, memd_r.at[t], gsend.at[0], grecv.at[t], tensor=0)

    n1 = [remote(ny.at[t], ny.at[t], ns.at[o - 1], nq.at[o - 1], tensor=lax.rem(t + o, NT)) for o in (1, 2, 3)]
    n2 = [remote(nc.at[0], nc.at[1], ns.at[3], nq.at[3], dp=sib)]
    n3 = [remote(nx.at[chip], nx.at[chip], ns.at[3 + o], nq.at[3 + o], dp=chip_at(o) * 2 + core)
          for o in range(1, chips)]

    def mem_last():
        @pl.when(t > 0)
        def _():
            to_first.start()

        mem_attend_back()
        all_pairs_sum(C_OUT)
        for off in (1, 2, 3):
            over_tensor(C_OUT, lax.rem(t + off, NT)).start()
        pair(C_CROSS, t).wait_recv()
        pair_sum(C_CROSS, t)
        start, lo, hf = at(C_CROSS)
        ysum[lo - LATE:lo - LATE + hf] = g[t, pl.ds(own_half(C_CROSS), hf)]
        go(over_chips(C_CROSS))

        @pl.when(t == 0)
        def _():
            for r in range(R):
                d32[r, 0:MP] += md[r * MP:r * MP + MP]
            for s in range(1, NT):
                remote(memd_s, memd_r.at[s], gsend.at[0], grecv.at[s], tensor=0).wait_recv()
                remote(ex_dq.at[s], ex_dq.at[s], qsend.at[0], qrecv.at[s], tensor=0).wait_recv()
            for a in range(NT):
                for r in range(R):
                    rows = slice(r * MP, r * MP + MP)
                    for j in range(2):
                        tot = memd_s[a, r, j].astype(F32)
                        for s in range(1, NT):
                            tot = tot + memd_r[s, a, r, j].astype(F32)
                        dkv[a, r, j, 0:MP] += tot
                    tot = ex_dq[0, a, rows].astype(F32)
                    for s in range(1, NT):
                        tot = tot + ex_dq[s, a, rows].astype(F32)
                    act[r, a, 0:MP, 0:128] = (act[r, a, 0:MP, 0:128].astype(F32) + tot).astype(BF)

    ny[t] = ng[...]

    @pl.when(is_dec)
    def _():
        go(n1)

    @pl.when(is_enc)
    def _():
        go(n1)
        mem_last()

    @pl.loop(0, NT)
    def _(i):
        a = lax.rem(t + jnp.where(i == 0, 2, jnp.where(i == 1, 3, jnp.where(i == 2, 1, 0))), NT)
        to_left, to_right = halo_copies(a)
        to_left.wait_recv()

        @pl.when(is_enc)
        def _():
            to_right.wait_recv()

        for r in range(R):
            for j in range(2):
                dkv[a, r, j, T - HALO:T] += halo_r[0, a, r, j].astype(F32)

                @pl.when(is_enc)
                def _():
                    dkv[a, r, j, 0:HALO] += halo_r[1, a, r, j].astype(F32)

                act[r, a, :, 128 * (j + 1):128 * (j + 2)] = dkv[a, r, j].astype(BF)
        gw = dot_tn(x_ext[0, 0:T], act[0, a, :, 0:384]) + dot_tn(x_ext[1, 0:T], act[1, a, :, 0:384])
        for j in range(3):
            g[a, G_QKV + D * j:G_QKV + D * j + D] = gw[:, 128 * j:128 * j + 128].astype(BF)
        pair(C_QKV, a).start()
        wfull = jnp.concatenate([wqkv[a, j] for j in range(3)], axis=1)
        for r in range(R):
            d32[r] += dot_nt(act[r, a, :, 0:384], wfull)
        pair(C_QKV, a).wait_recv()
        pair_sum(C_QKV, a)

        @pl.when(a != t)
        def _():
            over_tensor(C_QKV, a).start()

    dx_copy = pltpu.make_async_copy(d32, dx_out, lsem.at[10])
    dx_copy.start()

    come(n1)
    nc[0] = ny[0] + ny[1] + ny[2] + ny[3]
    go(n2)
    for k in (C_DOWN, C_UP):
        come(chips_first(k))
        chips_first_sum(k)
        go(tensor_second(k))
    come(n2)
    nx[chip] = nc[0] + nc[1]
    go(n3)

    @pl.when(is_dec)
    def _():
        for rel in range(3):
            from_tensor(C_CROSS, rel).wait_recv()
        tensor_sum(C_CROSS)
        go(over_chips(C_CROSS))

    for rel in range(3):
        from_tensor(C_OUT, rel).wait_recv()
    tensor_sum(C_OUT)
    go(over_chips(C_OUT))
    for k in (C_DOWN, C_UP):
        come(tensor_second(k))
        tensor_second_sum(k)
        go(spread(k))
    for rel in range(3):
        from_tensor(C_QKV, rel).wait_recv()
    tensor_sum(C_QKV)
    go(over_chips(C_QKV))
    for k in (C_CROSS, C_OUT):
        come(over_chips(k))
        chips_sum(k)
        go(spread(k))
    come(n3)
    tot_n = nx[0]
    for o in range(1, chips):
        tot_n = tot_n + nx[o]
    ng_tot[...] = tot_n
    for k in (C_DOWN, C_UP):
        spread_chunk(k)
    come(over_chips(C_QKV))
    chips_sum(C_QKV)
    go(spread(C_QKV))
    for k in (C_CROSS, C_OUT, C_QKV):
        spread_chunk(k)
    for k in range(5):
        come(hand(k))

    y_copy.wait()
    dx_copy.wait()
    for i in (QKV, OUT, UP, DOWN):
        gone(copies[i])
    x_right.wait_send()
    for a in range(NT):
        halo_copies(a)[0].wait_send()
    gone(n1)
    gone(n2)
    gone(n3)
    for k in range(5):
        if k in (C_DOWN, C_UP):
            gone(chips_first(k))
            gone(tensor_second(k))
        else:
            gone(over_chips(k))
        if k != C_CROSS:
            for a in range(NT):
                pair(k, a).wait_send()
        gone(spread(k))
        gone(hand(k))
    for k in (C_OUT, C_QKV):
        for rel in range(3):
            from_tensor(k, rel).wait_send()

    @pl.when(is_dec)
    def _():
        gone(copies[CROSS])
        gone(dkv_copies)
        for a in range(NT):
            pair(C_CROSS, a).wait_send()
        for rel in range(3):
            from_tensor(C_CROSS, rel).wait_send()

    @pl.when(is_enc)
    def _():
        x_left.wait_send()
        pair(C_CROSS, t).wait_send()
        for a in range(NT):
            halo_copies(a)[1].wait_send()
        for e in range(5):
            gone(exchanges[e])
        gone(kv_copies)

        @pl.when(t == 0)
        def _():
            gone(mem_x)
            gone(mem_c)

        @pl.when(t > 0)
        def _():
            to_first.wait_send()
            dq_copy.wait_send()


def layer_call(chips, lens, x, cot, wqkv, wout, wcross, wup, wdown, gain, bias):
    any_ = pl.BlockSpec(memory_space=pl.ANY)
    vmem = pl.BlockSpec(memory_space=pltpu.VMEM)
    M = R * MP
    W = W_ENC
    S = pltpu.SemaphoreType.DMA
    C = len(CHUNKS)
    o = max(chips - 1, 1)
    late = HALF - LATE

    def V(shape, kind):
        return pltpu.VMEM(shape, kind)

    scratch = dict(
        x_ext=V((R, W, D), BF), cotm=V((R, MP, D), F32), d32=V((R, T, D), F32),
        wqkv=V((NT, 3, D, 128), BF), wout=V((NT, 128, D), BF), wcross=V((NT, 2, D, 128), BF),
        wup=V((NT, D, D), BF), wdown=V((NT, D, D), BF),
        kk=V((NT, R, W, 128), BF), vv=V((NT, R, W, 128), BF), vt=V((NT, R, 128, W), BF),
        qs=V((NT, R, T, 128), BF), pt=V((NT, R, 2, W, T), BF), ctx=V((R, NT, T, 128), BF),
        mask=V((R, W, T), F32), hmask=V((2, T, 128), BF),
        xh1=V((R, T, D), F32), xh2=V((R, T, D), F32), rs1=V((R, T, 1), F32), rs2=V((R, T, 1), F32),
        h32=V((R, T, D), F32), hb=V((R, T, D), BF), h1b=V((R, T, D), BF),
        act=V((R, NT, T, D), BF), gp=V((R, NT, T, D), BF), dab=V((R, T, D), BF), dr=V((R, NT, T, 128), BF),
        dkv=V((NT, R, 2, T, 128), F32), halo_s=V((2, NT, R, 2, HALO, 128), BF),
        halo_r=V((2, NT, R, 2, HALO, 128), BF), memd_s=V((NT, R, 2, MP, 128), BF),
        memd_r=V((NT, NT, R, 2, MP, 128), BF),
        ex_o=V((NT, NT, M, 128), BF), ex_st=V((NT, M, 128), F32), ex_f=V((NT, M, D), BF), ex_m=V((NT, M, D), BF),
        ex_h=V((NT, M, D), BF), ex_dq=V((NT, NT, M, 128), BF), qm=V((NT, R, 2 * MP, 128), BF),
        kvm=V((NT, 2, M, 128), BF), dkvm_s=V((NT, 2, M, 128), F32), dkvm_r=V((NT, 2, M, 128), F32),
        kblk=V((R, 256, D), BF), vblk=V((R, 256, D), BF), cpt=V((R, 256, T), BF), cq=V((R, T, D), BF),
        cctx=V((R, T, D), BF),
        mx1=V((M, D), F32), mx2=V((M, D), F32), mx3=V((M, D), F32), mr1=V((M, 1), F32), mr2=V((M, 1), F32),
        mr3=V((M, 1), F32), mh=V((M, D), F32), mact=V((M, D), BF), mgp=V((M, D), F32), mc=V((M, D), F32),
        mm=V((M, D), BF), mst=V((2, M, 128), F32), md=V((M, D), F32),
        g=V((NT, G_ROWS, 128), BF), r1=V((NT, HALF, 128), BF), r2=V((3, late, 128), BF),
        r3=V((o, late // chips, 128), BF), rx=V((o, NT, LATE // chips, 128), BF), ry=V((4, NT, LATE // chips, 128), BF),
        ysum=V((late, 128), BF), ng=V((8, D), F32), ny=V((NT, 8, D), F32), nc=V((2, 8, D), F32),
        nx=V((chips, 8, D), F32),
        lsem=S((11,)), wsend=S((5, 7)), wrecv=S((5, 7)), xsend=S((2,)), xrecv=S((2,)), msend=S((2, 3)), mrecv=S((2,)),
        esend=S((5, 3)), erecv=S((5, 3)), ksend=S((NT,)), krecv=S((NT,)), dsend=S((NT,)), drecv=S((NT,)),
        hsend=S((2, NT)), hrecv=S((2, NT)), gsend=S((1,)), grecv=S((NT,)), qsend=S((1,)), qrecv=S((NT,)),
        s1=S((C, NT)), q1=S((C, NT)), s2=S((C, 3)), q2=S((C, 3)), s3=S((C, o)), q3=S((C, o)),
        s4=S((C, o)), q4=S((C, o)), s5=S((C,)), q5=S((C,)), ns=S((4 + o,)), nq=S((4 + o,)),
    )
    names = tuple(scratch)

    def kernel(*refs):
        layer_kernel(chips, names, *refs)

    return pl.pallas_call(
        kernel,
        out_shape=(
            jax.ShapeDtypeStruct((R, T, D), F32),
            jax.ShapeDtypeStruct((R, T, D), F32),
            jax.ShapeDtypeStruct((G_ROWS, 128), BF),
            jax.ShapeDtypeStruct((8, D), F32),
        ),
        in_specs=[pl.BlockSpec(memory_space=pltpu.SMEM)] + [any_] * 7 + [vmem] * 2,
        out_specs=(any_, any_, vmem, vmem),
        scratch_shapes=list(scratch.values()),
        compiler_params=pltpu.CompilerParams(
            collective_id=0, has_side_effects=True, vmem_limit_bytes=VMEM_BYTES
        ),
        name="layers",
    )(lens, x, cot, wqkv, wout, wcross, wup, wdown, gain, bias)


def finish_kernel(y_in, dx_in, full, ng, y, dx, o_qkv, o_out, o_cross, o_up, o_down, o_gain, o_bias, sems):
    copies = [pltpu.make_async_copy(y_in, y.at[0], sems.at[0]), pltpu.make_async_copy(dx_in, dx.at[0], sems.at[1])]
    for c in copies:
        c.start()
    for j in range(3):
        o_qkv[0, j] = full[G_QKV + D * j:G_QKV + D * j + D].astype(F32)
    for j in range(2):
        o_cross[0, j] = full[G_CROSS + D * j:G_CROSS + D * j + D].astype(F32)
    for j in range(4):
        cols = slice(128 * j, 128 * j + 128)
        o_out[0, :, cols] = full[G_OUT + 128 * j:G_OUT + 128 * j + 128].astype(F32)
        o_up[0, :, cols] = full[G_UP + D * j:G_UP + D * j + D].astype(F32)
        o_down[0, :, cols] = full[G_DOWN + D * j:G_DOWN + D * j + D].astype(F32)
    o_gain[0] = ng[0:3]
    o_bias[0] = ng[3:6]
    for c in copies:
        c.wait()


def finish_call(y, dx, full, ng):
    any_ = pl.BlockSpec(memory_space=pl.ANY)
    vmem = pl.BlockSpec(memory_space=pltpu.VMEM)
    shapes = ((1, R, T, D), (1, R, T, D), (1, 3, D, 128), (1, 128, D), (1, 2, D, 128), (1, D, D), (1, D, D),
              (1, 3, D), (1, 3, D))
    return pl.pallas_call(
        finish_kernel,
        out_shape=tuple(jax.ShapeDtypeStruct(s, F32) for s in shapes),
        in_specs=[any_, any_, vmem, vmem],
        out_specs=(any_, any_) + (vmem,) * 7,
        scratch_shapes=[pltpu.SemaphoreType.DMA((2,))],
        compiler_params=pltpu.CompilerParams(vmem_limit_bytes=32 * 1024 * 1024),
        name="finish",
    )(y, dx, full, ng)


def solution(mesh):
    chips = mesh.shape["dp"] // 2

    def shards(inputs, lengths, w_qkv, w_out, w_cross, w_up, w_down, norm_gain, norm_bias, cotangent):
        y, dx, full, ng = layer_call(
            chips, lengths, inputs[0], cotangent[0], w_qkv[0], w_out[0], w_cross[0], w_up[0], w_down[0],
            norm_gain, norm_bias)
        return finish_call(y, dx, full, ng)

    return jax.shard_map(
        shards,
        mesh=mesh,
        in_specs=(
            P("section", "dp", "tensor", None),
            P("dp", None),
            P("section", None, None, "tensor"),
            P("section", "tensor", None),
            P("section", None, None, "tensor"),
            P("section", None, "tensor"),
            P("section", "tensor", None),
            P("section", None, None),
            P("section", None, None),
            P("section", "dp", "tensor", None),
        ),
        out_specs=(
            P("section", "dp", "tensor", None),
            P("section", "dp", "tensor", None),
            P("section", None, None, "tensor"),
            P("section", "tensor", None),
            P("section", None, None, "tensor"),
            P("section", None, "tensor"),
            P("section", "tensor", None),
            P("section", None, None),
            P("section", None, None),
        ),
        check_vma=False,
    )
```

time: 214 us -> 173 us (0.81); the launches traced: 213 us -> 170 us
  Pallas kernels: 199 us -> 161 us
  local copies, waits for them, and re-layouts: 13.5 us -> 8.44 us
    pallas_call x2, Pallas kernels: 199 us -> 161 us  [the longest x1 158 us: layer_call(): pl.pallas_call(kernel, out_shape=(jax.ShapeDtypeStruct((R, T, D), F32), j...]
    unnamed x18 -> x10, local copies, waits for them, and re-layouts: 13.5 us -> 7.24 us
where the time goes in v2:
time: 173 us; the launch traced here: 170 us
  Pallas kernels  161 us (93%)
  local copies, waits for them, and re-layouts  8.44 us (5%)
    pallas_call x1, Pallas kernels, layer_call(): pl.pallas_call(kernel, out_shape=(jax.ShapeDtypeStruct((R, T, D), F32), j...  158 us
    unnamed x10, local copies, waits for them, and re-layouts  7.24 us

profile of v2, /device:TPU:1, one launch (start us, length us, event | category | flops | bytes accessed | tf_op | source)
XLA Modules:
  0.0 170.2 jit_solution(18156277887777606666)
XLA Ops:
  0.6 1.3 copy.19.refs_8_
  1.9 1.3 copy.20.refs_9_
  3.2 157.9 %layers.1 = (f32[2,256,512]{2,1,0:T(8,128)}, f32[2,256,512]{2,1,0:T(8,128)}, bf16[7168,128]{1,0:T(8,128)(2,1)}, f32[8,512]{1,0:T(8,128)}) custom-call(s32[2,16]{1,0:T(2,128)} %refs_0_.1, bf16[2,256,512]{2,1,0:T(8,128)(2,1)} %bitcast.8, f32[2,256,512]{2,1,0:T(8,128)} %bitcast.7, bf16[3,512,128]{2,1,0:T(8,128)(2,1)} %bitcast.11, bf16[128,512]{1,0:T(8,128)(2,1)} %bitcast.13, ...), custom_call_target="tpu_custom_call" | custom-call | tf_op jit(solution)/shard_map/layers/pallas_call | solution.py:1265
  161.1 0.0 copy-start
  161.2 1.5 copy-done
  162.6 0.0 copy-start.1
  162.6 1.2 copy-done.1
  163.9 0.0 copy-start.2
  163.9 1.2 copy-done.2
  165.1 0.0 copy-start.3
  165.1 0.7 copy-done.3
  165.8 3.2 %finish.1 = (f32[1,2,256,512]{3,2,1,0:T(8,128)}, f32[1,2,256,512]{3,2,1,0:T(8,128)}, f32[1,3,512,128]{3,2,1,0:T(8,128)}, f32[1,128,512]{2,1,0:T(8,128)}, f32[1,2...) custom-call(f32[2,256,512]{2,1,0:T(8,128)S(1)} %copy-done.1, ...), custom_call_target="tpu_custom_call" | custom-call | tf_op jit(solution)/shard_map/finish/pallas_call | solution.py:1307
  169.0 0.6 copy.21
  169.6 0.6 copy.22
Async XLA Ops:
  161.1 1.5 copy-start
  162.6 1.2 copy-start.1
  163.9 1.2 copy-start.2
  165.1 0.7 copy-start.3

commit v3 on v2

v3 whole, which is shorter than its diff:
```python
import jax
import jax.numpy as jnp
from jax import lax
from jax.experimental import pallas as pl
from jax.experimental.pallas import tpu as pltpu
from jax.sharding import PartitionSpec as P

F32 = jnp.float32
BF = jnp.bfloat16
MESH = pl.DeviceIdType.MESH
VMEM_BYTES = 62 * 1024 * 1024

MEM = 20
MP = 32
R = 2
T = 256
HALO = 160
D = 512
NT = 4
LEFT, OWN, RIGHT, MEM_2, W_ENC = 32, 192, 448, 608, 640
W_DEC = RIGHT
WIN_ENC = ((0, 480), (128, 512))
WIN_DEC = ((0, 320), (128, 320))
EPS = 1e-05
FILL = -1e30
SCALE = 0.125

G_DOWN, G_UP, G_CROSS, G_OUT, G_QKV, G_ROWS = 0, 2048, 4096, 5120, 5632, 7168
CHUNKS = ((G_DOWN, 2048), (G_UP, 2048), (G_CROSS, 1024), (G_OUT, 512), (G_QKV, 1536))
C_DOWN, C_UP, C_CROSS, C_OUT, C_QKV = range(5)
LATE = G_CROSS // 2
HALF = G_ROWS // 2
QKV, OUT, CROSS, UP, DOWN = range(5)
W_ROWS = (512, 128, 512, 512, 512)


def dot(a, b):
    return lax.dot_general(a, b, (((1,), (0,)), ((), ())), preferred_element_type=F32)


def dot_nt(a, b):
    return lax.dot_general(a, b, (((1,), (1,)), ((), ())), preferred_element_type=F32)


def dot_tn(a, b):
    return lax.dot_general(a, b, (((0,), (0,)), ((), ())), preferred_element_type=F32)


def remote(src, dst, send, recv, **device):
    return pltpu.make_async_remote_copy(
        src_ref=src, dst_ref=dst, send_sem=send, recv_sem=recv, device_id=device, device_id_type=MESH
    )


def normed(v):
    c = v - jnp.mean(v, axis=1, keepdims=True)
    rs = lax.rsqrt(jnp.mean(c * c, axis=1, keepdims=True) + EPS)
    return c * rs, rs


def norm_back(xhat, rs, gain, dy):
    dxh = dy * gain
    m1 = jnp.mean(dxh, axis=1, keepdims=True)
    m2 = jnp.mean(dxh * xhat, axis=1, keepdims=True)
    return rs * (dxh - m1 - xhat * m2)


def gelu_both(u):
    k = 0.7978845608028654
    u2 = u * u
    th = jnp.tanh(k * u * (1.0 + 0.044715 * u2))
    half = 0.5 * (1.0 + th)
    grad = half + 0.5 * u * (1.0 - th * th) * (k * (1.0 + 3.0 * 0.044715 * u2))
    return u * half, grad


def layer_kernel(chips, names, *refs):
    (lens, x_in, cot_in, wqkv_in, wout_in, wcross_in, wup_in, wdown_in, gain, bias,
     y_out, dx_out, full, ng_tot) = refs[:14]
    m = dict(zip(names, refs[14:]))
    x_ext, cotm, d32, wqkv, wout, wcross, wup, wdown = (
        m[n] for n in ("x_ext", "cotm", "d32", "wqkv", "wout", "wcross", "wup", "wdown"))
    kk, vv, qs, pt, ctx, mask, hmask = (m[n] for n in ("kk", "vv", "qs", "pt", "ctx", "mask", "hmask"))
    xh1, xh2, rs1, rs2, h32, hb, h1b, act, gp, dab, dr = (
        m[n] for n in ("xh1", "xh2", "rs1", "rs2", "h32", "hb", "h1b", "act", "gp", "dab", "dr"))
    dkv, halo_s, halo_r, mg_s, mg_r, dxm_s, dxm_r, mdu = (
        m[n] for n in ("dkv", "halo_s", "halo_r", "mg_s", "mg_r", "dxm_s", "dxm_r", "mdu"))
    ex_o, ex_st, ex_f, ex_m, qm, rq, rqs, rqr = (
        m[n] for n in ("ex_o", "ex_st", "ex_f", "ex_m", "qm", "rq", "rqs", "rqr"))
    kvm, dkvm_s, dkvm_r, kblk, vblk, cpt, cq, cctx = (
        m[n] for n in ("kvm", "dkvm_s", "dkvm_r", "kblk", "vblk", "cpt", "cq", "cctx"))
    mx1, mx2, mx3, mr1, mr2, mr3, mh, mact, mgp, mc, mm, mst, md = (
        m[n] for n in ("mx1", "mx2", "mx3", "mr1", "mr2", "mr3", "mh", "mact", "mgp", "mc", "mm", "mst", "md"))
    g, r1, r2, r3, rx, ry_s, ry_r, zz, ysum, ng, ny, nc, nx, cdb = (
        m[n] for n in ("g", "r1", "r2", "r3", "rx", "ry_s", "ry_r", "zz", "ysum", "ng", "ny", "nc", "nx", "cdb"))
    (lsem, wsend, wrecv, xsend, xrecv, msend, mrecv, esend, erecv, ksend, krecv, dsend, drecv,
     hsend, hrecv, gsend, grecv, qsend, qrecv) = (
        m[n] for n in ("lsem", "wsend", "wrecv", "xsend", "xrecv", "msend", "mrecv", "esend", "erecv", "ksend",
                       "krecv", "dsend", "drecv", "hsend", "hrecv", "gsend", "grecv", "qsend", "qrecv"))
    s1, q1, s2, q2, s3, q3, s4, q4, s5, q5, ns, nq = (
        m[n] for n in ("s1", "q1", "s2", "q2", "s3", "q3", "s4", "q4", "s5", "q5", "ns", "nq"))
    w2send, w2recv, sx, qx, sz, qz, sq, qq = (
        m[n] for n in ("w2send", "w2recv", "sx", "qx", "sz", "qz", "sq", "qq"))

    def g_row(i):
        return gain[i]

    def b_row(i):
        return bias[i]

    sec = lax.axis_index("section")
    dp = lax.axis_index("dp")
    t = lax.axis_index("tensor")
    core = lax.rem(dp, 2)
    chip = lax.div(dp, 2)
    sib = dp + 1 - 2 * core
    is_enc = sec == 0
    is_dec = sec == 1
    left = lax.rem(t + 3, NT)
    right = lax.rem(t + 1, NT)
    opp = lax.rem(t + 2, NT)
    other = 1 - sec
    xi = lax.div(dp, 4)

    def x_dev(off):
        return lax.rem(xi + off, 4) * 4 + lax.rem(dp, 4)

    z_dev = xi * 4 + lax.rem(dp + 2, 4)

    def source(off):
        return lax.rem(t + NT - off, NT)

    def chip_at(off):
        return lax.rem(chip + off, chips)

    ins = (wqkv_in, wout_in, wcross_in, wup_in, wdown_in)
    ws = (wqkv, wout, wcross, wup, wdown)

    def part(i, ref, start, n):
        if i in (QKV, CROSS):
            return ref.at[:, pl.ds(start, n), :]
        return ref.at[pl.ds(start, n), :]

    def slot(i, a, start, n):
        if i in (QKV, CROSS):
            return ws[i].at[a, :, pl.ds(start, n), :]
        return ws[i].at[a, pl.ds(start, n), :]

    barrier = pltpu.get_barrier_semaphore()
    for off in (1, 2, 3):
        pl.semaphore_signal(barrier, inc=1, device_id={"tensor": lax.rem(t + off, NT)}, device_id_type=MESH)
    pl.semaphore_signal(barrier, inc=1, device_id={"dp": sib}, device_id_type=MESH)
    for b in range(NT):
        pl.semaphore_signal(barrier, inc=1, device_id={"section": other, "tensor": b}, device_id_type=MESH)
    for off in range(1, chips):
        pl.semaphore_signal(barrier, inc=1, device_id={"dp": chip_at(off) * 2 + core}, device_id_type=MESH)

    locals_ = [
        pltpu.make_async_copy(x_in, x_ext.at[:, pl.ds(OWN, T), :], lsem.at[0]),
        pltpu.make_async_copy(cot_in, d32, lsem.at[1]),
    ]
    for i in range(5):
        locals_.append(pltpu.make_async_copy(ins[i], ws[i].at[t], lsem.at[2 + i]))
    for c in locals_:
        c.start()

    pl.semaphore_wait(barrier, 8 + chips - 1)

    x_right = remote(x_in.at[:, pl.ds(T - HALO, HALO), :], x_ext.at[:, pl.ds(LEFT, HALO), :],
                     xsend.at[0], xrecv.at[0], tensor=right)
    x_left = remote(x_in.at[:, pl.ds(0, HALO), :], x_ext.at[:, pl.ds(RIGHT, HALO), :],
                    xsend.at[1], xrecv.at[1], tensor=left)
    mem_x, mem_c = [], []
    for off in (1, 2, 3):
        to = lax.rem(t + off, NT)
        mem_x.append(remote(x_in.at[:, pl.ds(0, MP), :], x_ext.at[:, pl.ds(0, MP), :],
                            msend.at[0, off - 1], mrecv.at[0], tensor=to))
        mem_c.append(remote(cot_in.at[:, pl.ds(0, MP), :], cotm, msend.at[1, off - 1], mrecv.at[1], tensor=to))
    mem_local = [
        pltpu.make_async_copy(x_in.at[:, pl.ds(0, MP), :], x_ext.at[:, pl.ds(0, MP), :], lsem.at[7]),
        pltpu.make_async_copy(cot_in.at[:, pl.ds(0, MP), :], cotm, lsem.at[8]),
    ]

    def w_direct(i):
        hf = W_ROWS[i] // 2
        mine = core * hf
        return [remote(part(i, ins[i], mine, hf), slot(i, t, mine, hf), wsend.at[i, off - 1], wrecv.at[i, off - 1],
                       tensor=lax.rem(t + off, NT)) for off in (1, 2, 3)]

    eighth = D // 8
    at_8 = core * (D // 2) + xi * eighth

    def w_eighth(i):
        return [remote(part(i, ins[i], at_8, eighth), slot(i, t, at_8, eighth),
                       wsend.at[i, off - 1], wrecv.at[i, off - 1], tensor=lax.rem(t + off, NT)) for off in (1, 2, 3)]

    def w_along(i):
        out = []
        for off in (1, 2, 3):
            rows = slot(i, source(off), at_8, eighth)
            for xo in (1, 2, 3):
                out.append(remote(rows, rows, w2send.at[i - UP, off - 1, xo - 1], w2recv.at[i - UP, off - 1, xo - 1],
                                  dp=x_dev(xo)))
        return out

    def w_pair(i):
        hf = W_ROWS[i] // 2
        out = []
        for off in (1, 2, 3):
            rows = slot(i, source(off), core * hf, hf)
            out.append(remote(rows, rows, wsend.at[i, 2 + off], wrecv.at[i, 2 + off], dp=sib))
        return out

    def go(cs):
        for c in cs:
            c.start()

    def come(cs):
        for c in cs:
            c.wait_recv()

    def gone(cs):
        for c in cs:
            c.wait_send()

    def arrive(i):
        for c, p in zip(w_direct(i), w_pair(i)):
            c.wait_recv()
            p.start()

    def go_along(i):
        along = w_along(i)
        for off, c in enumerate(w_eighth(i)):
            c.wait_recv()
            go(along[3 * off:3 * off + 3])

    def come_along(i):
        along = w_along(i)
        for off, p in enumerate(w_pair(i)):
            come(along[3 * off:3 * off + 3])
            p.start()

    def ready(i):
        come(w_pair(i))

    @pl.when(is_enc)
    def _():
        @pl.when(t == 0)
        def _():
            go(mem_x + mem_local)

        go(w_direct(QKV))
        x_right.start()
        x_left.start()

    @pl.when(is_dec)
    def _():
        x_right.start()
        go(w_direct(QKV))
        go(w_direct(OUT))
        go(w_eighth(UP))
        go(w_eighth(DOWN))
        go(w_direct(CROSS))

    lane = lax.broadcasted_iota(jnp.int32, (T, 128), 1)
    hmask[0] = jnp.where(lane < 64, 1.0, 0.0).astype(BF)
    hmask[1] = jnp.where(lane < 64, 0.0, 1.0).astype(BF)

    def segments(pos, r):
        off = pos - MEM
        seg = jnp.where(off >= 0, 1, 0)
        end = jnp.int32(0)
        for k in range(16):
            end = end + lens[r, k]
            seg = seg + jnp.where(off >= end, 1, 0)
        return seg

    def make_masks(windows, encoder):
        for r in range(R):
            for b, (w0, wn) in enumerate(windows):
                e = lax.broadcasted_iota(jnp.int32, (wn, 128), 0) + w0
                pos = e - OWN + t * T
                ks = segments(pos, r)
                qpos = lax.broadcasted_iota(jnp.int32, (8, 128), 1) + (t * T + b * 128)
                same = ks == segments(qpos, r)[0:1]
                if encoder:
                    mem_i = jnp.where(e < LEFT, e, jnp.where(e >= MEM_2, e - MEM_2, MEM))
                    ok = jnp.logical_or(mem_i < MEM, jnp.logical_and(
                        jnp.logical_and(e >= LEFT, e < MEM_2), jnp.logical_and(same, ks > 0)))
                else:
                    ok = jnp.logical_and(jnp.logical_and(same, e >= LEFT),
                                         jnp.logical_and(pos <= qpos[0:1], pos >= 0))
                mask[r, b, 0:wn] = jnp.where(ok, 0.0, FILL)

    @pl.when(is_enc)
    def _():
        make_masks(WIN_ENC, True)

    @pl.when(is_dec)
    def _():
        make_masks(WIN_DEC, False)
        x_ext[:, 0:MP] = jnp.zeros((R, MP, D), BF)

    ex_st[t] = jnp.zeros((R * MP, 128), F32)
    ng[...] = jnp.zeros(ng.shape, F32)

    for c in locals_:
        c.wait()

    def shard_at(step):
        return lax.rem(t + jnp.where(step == 0, 0, jnp.where(step == 1, 3, step - 1)), NT)

    lane_m = lax.broadcasted_iota(jnp.int32, (MP, 128), 1)
    low_m = lane_m < 64

    def keys(a, r, lo, hi, wkv):
        kv = dot(x_ext[r, lo:hi], wkv)
        k32, v32 = kv[:, 0:128], kv[:, 128:256]
        kk[a, r, lo:hi] = k32.astype(BF)
        vv[a, r, lo:hi] = v32.astype(BF)

    def keys_weight(a):
        return jnp.concatenate([wqkv[a, 1], wqkv[a, 2]], axis=1)

    def queries(a, r):
        q = dot(x_ext[r, OWN:OWN + T], wqkv[a, 0]).astype(BF)
        q = (q.astype(F32) * SCALE).astype(BF)
        for b in range(2):
            for h in range(2):
                qs[a, r, b, h * 128:h * 128 + 128] = q[b * 128:b * 128 + 128] * hmask[h, 0:128]

    def turned(ref, a, r, hi):
        return ref[a, r, 0:hi].astype(F32).T.astype(BF)

    def project_own(a):
        wkv = keys_weight(a)
        for r in range(R):
            keys(a, r, OWN, OWN + T, wkv)
            queries(a, r)
            m32 = dot(x_ext[r, 0:MP], wqkv[a, 0]).astype(BF).astype(F32) * SCALE
            lhs = jnp.concatenate([jnp.where(low_m, m32, 0.0), jnp.where(low_m, 0.0, m32)], axis=0).astype(BF)
            qm[a, r] = lhs
            s = dot_nt(lhs, kk[a, r, OWN:OWN + T])
            top = jnp.max(s, axis=1, keepdims=True)
            p = jnp.exp(s - top)
            total = jnp.sum(p, axis=1, keepdims=True)
            o = dot(p.astype(BF), vv[a, r, OWN:OWN + T]) / total
            ex_o[t, a, r * MP:r * MP + MP] = jnp.where(low_m, o[0:MP], o[MP:2 * MP]).astype(BF)
            st = ex_st[t, r * MP:r * MP + MP]
            st = jnp.where(lane_m == 2 * a, top[0:MP], st)
            st = jnp.where(lane_m == 2 * a + 1, top[MP:2 * MP], st)
            st = jnp.where(lane_m == 2 * a + 8, total[0:MP], st)
            st = jnp.where(lane_m == 2 * a + 9, total[MP:2 * MP], st)
            ex_st[t, r * MP:r * MP + MP] = st

    def project_rest(a):
        wkv = keys_weight(a)
        for r in range(R):
            keys(a, r, 0, OWN, wkv)
            keys(a, r, RIGHT, W_ENC, wkv)

    def project_all(a):
        wkv = keys_weight(a)
        for r in range(R):
            keys(a, r, 0, W_DEC, wkv)
            queries(a, r)

    def ex_copies(e, buf):
        out = []
        for off in (1, 2, 3):
            out.append(remote(buf.at[t], buf.at[t], esend.at[e, off - 1], erecv.at[e, off - 1],
                              tensor=lax.rem(t + off, NT)))
        return out

    exchanges = [ex_copies(e, buf) for e, buf in enumerate((ex_o, ex_st, ex_f, ex_m))]

    def ex_start(e):
        for c in exchanges[e]:
            c.start()

    def ex_wait(e):
        for c in exchanges[e]:
            c.wait_recv()

    def wide(ref, r):
        return jnp.concatenate([ref[r, a] for a in range(NT)], axis=1)

    def w_out_full():
        return wout[...].reshape(D, D)

    def mem_combine():
        for r in range(R):
            rows = slice(r * MP, r * MP + MP)
            sts = [ex_st[s, rows] for s in range(NT)]
            top = jnp.maximum(jnp.maximum(sts[0], sts[1]), jnp.maximum(sts[2], sts[3]))
            wts = [pltpu.roll(sts[s], 120, 1) * jnp.exp(sts[s] - top) for s in range(NT)]
            total = wts[0] + wts[1] + wts[2] + wts[3]
            total = jnp.where(lane_m < 8, total, 1.0)
            inv = 1.0 / total
            mst[0, rows] = jnp.where(lane_m < 8, top + jnp.log(total), 0.0)
            for a in range(NT):
                acc = jnp.zeros((MP, 128), F32)
                for s in range(NT):
                    w = wts[s] * inv
                    wide_w = jnp.where(low_m, w[:, 2 * a:2 * a + 1], w[:, 2 * a + 1:2 * a + 2])
                    acc = acc + wide_w * ex_o[s, a, rows].astype(F32)
                mc[rows, a * 128:a * 128 + 128] = acc

    def x_mem():
        return jnp.concatenate([x_ext[r, 0:MP] for r in range(R)], axis=0)

    def mem_first():
        mem_combine()
        xm = x_mem().astype(F32)
        xh, rs = normed(xm + dot(mc[...].astype(BF), w_out_full()))
        mx1[...] = xh
        mr1[...] = rs
        h = xh * g_row(0) + b_row(0)
        mh[...] = h
        av, _ = gelu_both(dot(h.astype(BF), wup[t]))
        mact[...] = av.astype(BF)
        ex_f[t] = dot(av.astype(BF), wdown[t]).astype(BF)
        ex_start(2)

    kv_copies = [remote(kvm.at[t], kvm.at[t], ksend.at[b], krecv.at[t], section=other, tensor=b) for b in range(NT)]

    def mem_second():
        third = mh[...]
        for s in range(NT):
            third = third + ex_f[s].astype(F32)
        xh, rs = normed(third)
        mx2[...] = xh
        mr2[...] = rs
        y = xh * g_row(1) + b_row(1)
        md[...] = y
        xh, rs = normed(y)
        mx3[...] = xh
        mr3[...] = rs
        mv = (xh * g_row(2) + b_row(2)).astype(BF)
        mm[...] = mv
        kvm[t, 0] = dot(mv, wcross[t, 0]).astype(BF)
        kvm[t, 1] = dot(mv, wcross[t, 1]).astype(BF)
        for c in kv_copies:
            c.start()

    def attend(a, r, windows):
        v_t = turned(vv, a, r, windows[1][0] + windows[1][1])
        for b, (w0, wn) in enumerate(windows):
            mk = mask[r, b, 0:wn]
            s = dot_nt(kk[a, r, w0:w0 + wn], qs[a, r, b]) + jnp.concatenate([mk, mk], axis=1)
            p = jnp.exp(s - jnp.max(s, axis=0, keepdims=True))
            p = (p * (1.0 / jnp.sum(p, axis=0, keepdims=True))).astype(BF)
            pt[a, r, b, 0:wn] = p
            o = dot(v_t[:, w0:w0 + wn], p)
            o = jnp.concatenate([o[0:64, 0:128], o[64:128, 128:256]], axis=0)
            ctx[r, a, b * 128:b * 128 + 128] = o.T.astype(BF)

    def encoder_attention():
        @pl.when(t == 0)
        def _():
            mem_local[0].wait()

        @pl.when(t > 0)
        def _():
            mem_x[0].wait_recv()

        x_ext[:, MEM_2:MEM_2 + MP] = x_ext[:, 0:MP]

        @pl.loop(0, NT)
        def _(step):
            @pl.when(step == 1)
            def _():
                arrive(QKV)
                ready(QKV)

            project_own(shard_at(step))

        ex_start(0)
        ex_start(1)
        go(w_direct(OUT))
        go(w_eighth(UP))
        x_right.wait_recv()
        x_left.wait_recv()

        @pl.loop(0, NT)
        def _(step):
            project_rest(shard_at(step))

        @pl.loop(0, NT * R)
        def _(i):
            @pl.when(i == 2)
            def _():
                arrive(OUT)
                ex_wait(0)
                ex_wait(1)
                ready(OUT)
                mem_first()
                go(w_eighth(DOWN))
                go_along(UP)

            @pl.when(i == 6)
            def _():
                ex_wait(2)
                mem_second()
                go_along(DOWN)

                @pl.when(t == 0)
                def _():
                    go(mem_c)

            attend(shard_at(lax.div(i, 2)), lax.rem(i, 2), WIN_ENC)

    def decoder_attention():
        x_right.wait_recv()

        @pl.loop(0, NT * R)
        def _(i):
            @pl.when(i == 1)
            def _():
                arrive(QKV)

            @pl.when(i == 2)
            def _():
                ready(QKV)

            step_from = jnp.where(i == 0, 0, jnp.where(i == 2, 1, 4))
            step_to = jnp.where(i == 0, 1, 4)

            @pl.loop(step_from, step_to)
            def _(step):
                project_all(shard_at(step))

            @pl.when(i == 2)
            def _():
                arrive(OUT)
                go_along(UP)

            @pl.when(i == 5)
            def _():
                go_along(DOWN)
                ready(OUT)

            attend(shard_at(lax.div(i, 2)), lax.rem(i, 2), WIN_DEC)

        arrive(CROSS)

    @pl.when(is_enc)
    def _():
        encoder_attention()

    @pl.when(is_dec)
    def _():
        decoder_attention()

    @pl.loop(0, R)
    def _(r):
        a0 = x_ext[r, OWN:OWN + T].astype(F32) + dot(wide(ctx, r), w_out_full())
        xh, rs = normed(a0)
        xh1[r] = xh
        rs1[r] = rs
        h = xh * g_row(0) + b_row(0)
        h32[r] = h
        hb[r] = h.astype(BF)

    come_along(UP)

    pad_mask = jnp.where(
        lax.rem(lax.broadcasted_iota(jnp.int32, (256, T), 0), MP) < MEM, 0.0, FILL)

    def full_cross(j):
        return jnp.concatenate([wcross[a, j] for a in range(NT)], axis=1)

    def cross_forward():
        ready(CROSS)
        wc0 = full_cross(0)
        wc1 = full_cross(1)
        kblk[...] = jnp.zeros(kblk.shape, BF)
        vblk[...] = jnp.zeros(vblk.shape, BF)

        @pl.loop(0, R)
        def _(r):
            h1b[r] = hb[r]
            q = dot(hb[r], wc0).astype(BF)
            cq[r] = (q.astype(F32) * SCALE).astype(BF)

        for b in range(NT):
            remote(kvm.at[b], kvm.at[b], ksend.at[b], krecv.at[b], section=other, tensor=b).wait_recv()
        for r in range(R):
            for a in range(NT):
                for h in range(2):
                    at = slice(a * 64 + h * MP, a * 64 + h * MP + MP)
                    kblk[r, at, a * 128:a * 128 + 128] = kvm[a, 0, r * MP:r * MP + MP] * hmask[h, 0:MP]
                    vblk[r, at, a * 128:a * 128 + 128] = kvm[a, 1, r * MP:r * MP + MP] * hmask[h, 0:MP]

        @pl.loop(0, R)
        def _(r):
            s = dot_nt(kblk[r], cq[r]) + pad_mask
            s = s.reshape(8, MP, T)
            p = jnp.exp(s - jnp.max(s, axis=1, keepdims=True))
            p = p * (1.0 / jnp.sum(p, axis=1, keepdims=True))
            p = p.reshape(256, T).astype(BF)
            cpt[r] = p
            c = dot_tn(p, vblk[r]).astype(BF)
            cctx[r] = c
            xh, rs = normed(h32[r] + dot_nt(c, wc1))
            xh2[r] = xh
            rs2[r] = rs
            h = xh * g_row(1) + b_row(1)
            h32[r] = h
            hb[r] = h.astype(BF)

    @pl.when(is_dec)
    def _():
        cross_forward()

    @pl.loop(0, NT * R)
    def _(i):
        @pl.when(i == 2)
        def _():
            ready(UP)

        a = shard_at(lax.div(i, 2))
        r = lax.rem(i, 2)
        av, gv = gelu_both(dot(hb[r], wup[a]))
        act[r, a] = av.astype(BF)
        gp[r, a] = gv.astype(BF)

    @pl.when(is_enc)
    def _():
        for a in range(NT):
            _, gv = gelu_both(dot(mh[...].astype(BF), wup[a]))
            mgp[a] = gv

    come_along(DOWN)
    ready(DOWN)

    last = jnp.where(is_enc, 1, 2)
    g_last = jnp.where(is_enc, g_row(1), g_row(2))
    b_last = jnp.where(is_enc, b_row(1), b_row(2))

    def add_norm(at, xh, dy):
        ng[pl.ds(at, 1)] += jnp.sum(dy * xh, axis=0, keepdims=True)
        ng[pl.ds(at + 3, 1)] += jnp.sum(dy, axis=0, keepdims=True)

    row_i = lax.broadcasted_iota(jnp.int32, (T, D), 0)
    is_mem_row = jnp.logical_and(row_i < MEM, jnp.logical_and(is_enc, t == 0))

    @pl.loop(0, R)
    def _(r):
        third = h32[r]
        for a in range(NT):
            third = third + dot(act[r, a], wdown[a])
        xh, rs = normed(third)
        h32[r] = xh * g_last + b_last
        dy = jnp.where(is_mem_row, 0.0, d32[r])
        d3 = norm_back(xh, rs, g_last, dy)
        ng[pl.ds(last, 1)] += jnp.sum(dy * xh, axis=0, keepdims=True)
        ng[pl.ds(last + 3, 1)] += jnp.sum(dy, axis=0, keepdims=True)
        d32[r] = d3
        dab[r] = d3.astype(BF)

    @pl.when(jnp.logical_and(is_enc, t == 0))
    def _():
        for r in range(R):
            h32[r, 0:24] = jnp.where(
                lax.broadcasted_iota(jnp.int32, (24, D), 0) < MEM, md[r * MP:r * MP + 24], h32[r, 0:24])

    y_copy = pltpu.make_async_copy(h32, y_out, lsem.at[9])
    y_copy.start()

    def at(k):
        return CHUNKS[k][0], CHUNKS[k][0] // 2, CHUNKS[k][1] // 2

    def own_half(k):
        start, lo, hf = at(k)
        return start + core * hf

    def shard_of(q):
        return lax.rem(t + 1 + q, NT)

    def rel_of(a):
        return lax.rem(a - t + 3, NT)

    def pair(k, q):
        start, lo, hf = at(k)
        return remote(g.at[q, pl.ds(start + (1 - core) * hf, hf), :], r1.at[q, pl.ds(lo, hf), :],
                      s1.at[k, q], q1.at[k, q], dp=sib)

    def pair_sum(k, q):
        start, lo, hf = at(k)
        rows = pl.ds(own_half(k), hf)
        g[q, rows] = (g[q, rows].astype(F32) + r1[q, lo:lo + hf].astype(F32)).astype(BF)

    def over_tensor(k, q):
        start, lo, hf = at(k)
        return remote(g.at[q, pl.ds(own_half(k), hf), :], r2.at[q, pl.ds(lo - LATE, hf), :],
                      s2.at[k, q], q2.at[k, q], tensor=shard_of(q))

    def tensor_sum(k):
        start, lo, hf = at(k)
        tot = g[3, pl.ds(own_half(k), hf)].astype(F32)
        for rel in range(3):
            tot = tot + r2[rel, lo - LATE:lo - LATE + hf].astype(F32)
        ysum[lo - LATE:lo - LATE + hf] = tot.astype(BF)

    def over_chips(k):
        start, lo, hf = at(k)
        n = hf // chips
        out = []
        for off in range(1, chips):
            to = chip_at(off)
            out.append(remote(ysum.at[pl.ds(lo - LATE + to * n, n), :],
                              r3.at[off - 1, pl.ds((lo - LATE) // chips, n), :],
                              s3.at[k, off - 1], q3.at[k, off - 1], dp=to * 2 + core))
        return out

    def chips_sum(k):
        start, lo, hf = at(k)
        n = hf // chips
        tot = ysum[pl.ds(lo - LATE + chip * n, n)].astype(F32)
        for o in range(chips - 1):
            tot = tot + r3[o, (lo - LATE) // chips:(lo - LATE) // chips + n].astype(F32)
        full[pl.ds(own_half(k) + chip * n, n)] = tot.astype(BF)

    def chips_first(k, q):
        start, lo, hf = at(k)
        n = hf // chips
        out = []
        for off in range(1, chips):
            to = chip_at(off)
            out.append(remote(g.at[q, pl.ds(own_half(k) + to * n, n), :], rq.at[off - 1, q],
                              sq.at[q, off - 1], qq.at[q, off - 1], dp=to * 2 + core))
        return out

    def chips_first_sum(k, q):
        start, lo, hf = at(k)
        n = hf // chips
        tot = g[q, pl.ds(own_half(k) + chip * n, n)].astype(F32)
        for o in range(chips - 1):
            tot = tot + rq[o, q].astype(F32)
        rqs[q] = tot.astype(BF)

    def tensor_third(k):
        return [remote(rqs.at[q], rqr.at[q], s2.at[k, q], q2.at[k, q], tensor=shard_of(q)) for q in range(3)]

    def tensor_third_sum(k):
        start, lo, hf = at(k)
        n = hf // chips
        tot = rqs[3].astype(F32)
        for q in range(3):
            tot = tot + rqr[q].astype(F32)
        full[pl.ds(own_half(k) + chip * n, n)] = tot.astype(BF)

    quarter = LATE // 8

    def along_x(k, own):
        some = pl.ds(3, 1) if own else pl.ds(0, 3)
        out = []
        for off in (1, 2, 3):
            to = lax.rem(xi + off, 4)
            out.append(remote(g.at[some, pl.ds(own_half(k) + to * quarter, quarter), :],
                              rx.at[off - 1, some, pl.ds(k * quarter, quarter), :],
                              sx.at[k, int(own), off - 1], qx.at[k, int(own), off - 1], dp=x_dev(off)))
        return out

    def along_x_sum(k, q):
        rows = slice(k * quarter, (k + 1) * quarter)
        tot = g[q, pl.ds(own_half(k) + xi * quarter, quarter)].astype(F32)
        for o in range(3):
            tot = tot + rx[o, q, rows].astype(F32)
        ry_s[q, rows] = tot.astype(BF)

    def tensor_second(k):
        rows = pl.ds(k * quarter, quarter)
        return [remote(ry_s.at[q, rows, :], ry_r.at[q, rows, :], s2.at[k, q], q2.at[k, q], tensor=shard_of(q))
                for q in range(3)]

    def tensor_second_sum(k):
        rows = slice(k * quarter, (k + 1) * quarter)
        tot = ry_s[3, rows].astype(F32)
        for q in range(3):
            tot = tot + ry_r[q, rows].astype(F32)
        zz[0, rows] = tot.astype(BF)

    def over_z(k):
        rows = pl.ds(k * quarter, quarter)
        return [remote(zz.at[0, rows, :], zz.at[1, rows, :], sz.at[k], qz.at[k], dp=z_dev)]

    def over_z_sum(k):
        rows = slice(k * quarter, (k + 1) * quarter)
        full[pl.ds(own_half(k) + xi * quarter, quarter)] = (zz[0, rows].astype(F32) + zz[1, rows].astype(F32)).astype(BF)

    def spread_x(k):
        mine = full.at[pl.ds(own_half(k) + xi * quarter, quarter), :]
        return [remote(mine, mine, s4.at[k, off - 1], q4.at[k, off - 1], dp=x_dev(off)) for off in (1, 2, 3)]

    def spread(k):
        start, lo, hf = at(k)
        n = hf // chips
        mine = full.at[pl.ds(own_half(k) + chip * n, n), :]
        return [remote(mine, mine, s4.at[k, off - 1], q4.at[k, off - 1], dp=chip_at(off) * 2 + core)
                for off in range(1, chips)]

    def hand(k):
        start, lo, hf = at(k)
        mine = full.at[pl.ds(own_half(k), hf), :]
        return [remote(mine, mine, s5.at[k], q5.at[k], dp=sib)]

    def all_pairs(k):
        for q in range(NT):
            pair(k, q).start()

    def all_pairs_sum(k, some=range(NT)):
        for q in some:
            pair(k, q).wait_recv()
            pair_sum(k, q)

    def put_feed(k, q, w):
        for j in range(4):
            g[q, CHUNKS[k][0] + D * j:CHUNKS[k][0] + D * (j + 1)] = w[:, 128 * j:128 * j + 128].astype(BF)

        @pl.when(jnp.logical_or(is_dec, q < 3))
        def _():
            pair(k, q).start()

    @pl.loop(0, NT)
    def _(q):
        a = shard_of(q)
        put_feed(C_DOWN, q, dot_tn(act[0, a], dab[0]) + dot_tn(act[1, a], dab[1]))

    @pl.loop(0, R)
    def _(r):
        d = d32[r]
        for a in range(NT):
            du = (dot_nt(dab[r], wdown[a]) * gp[r, a].astype(F32)).astype(BF)
            gp[r, a] = du
            d = d + dot_nt(du, wup[a])
        d32[r] = d

    def feed_on(k):
        all_pairs_sum(k, range(3))
        go(along_x(k, False))

        @pl.when(is_dec)
        def _():
            all_pairs_sum(k, (3,))
            go(along_x(k, True))

    feed_on(C_DOWN)

    dkv_copies = [
        remote(dkvm_s.at[b], dkvm_r.at[t], dsend.at[b], drecv.at[t], section=other, tensor=b) for b in range(NT)
    ]

    def cross_backward():
        wc0 = full_cross(0)
        wc1 = full_cross(1)

        @pl.loop(0, R)
        def _(r):
            dy = d32[r]
            add_norm(1, xh2[r], dy)
            d2 = norm_back(xh2[r], rs2[r], g_row(1), dy)
            d32[r] = d2
            dcb = d2.astype(BF)
            cdb[r] = dcb
            dc = dot(dcb, wc1).astype(BF)
            p = cpt[r].astype(F32).reshape(8, MP, T)
            dp_ = dot_nt(vblk[r], dc).reshape(8, MP, T)
            ds = p * (dp_ - jnp.sum(p * dp_, axis=1, keepdims=True))
            ds = ds.reshape(256, T).astype(BF)
            dk = dot(ds, cq[r])
            dv = dot(cpt[r], dc)
            rows = pl.ds(pl.multiple_of(r * MP, MP), MP)
            for a in range(NT):
                for j, val in ((0, dk), (1, dv)):
                    dkvm_s[a, j, rows] = jnp.where(
                        low_m, val[64 * a:64 * a + MP, 128 * a:128 * a + 128],
                        val[64 * a + MP:64 * a + 2 * MP, 128 * a:128 * a + 128])
            dq = (dot_tn(ds, kblk[r]) * SCALE).astype(BF)
            cq[r] = dq

        for c in dkv_copies:
            c.start()

        gq = dot_tn(h1b[0], cq[0]) + dot_tn(h1b[1], cq[1])
        go_ = dot_tn(cdb[0], cctx[0]) + dot_tn(cdb[1], cctx[1])
        for a in range(NT):
            q = rel_of(a)
            g[q, G_CROSS:G_CROSS + D] = gq[:, 128 * a:128 * a + 128].astype(BF)
            g[q, G_CROSS + D:G_CROSS + 2 * D] = go_[:, 128 * a:128 * a + 128].astype(BF)
        all_pairs(C_CROSS)

        @pl.loop(0, R)
        def _(r):
            d32[r] += dot_nt(cq[r], wc0)

    @pl.when(is_dec)
    def _():
        cross_backward()

    @pl.loop(0, NT)
    def _(q):
        a = shard_of(q)
        put_feed(C_UP, q, dot_tn(hb[0], gp[0, a]) + dot_tn(hb[1], gp[1, a]))

    @pl.loop(0, R)
    def _(r):
        dy = d32[r]
        add_norm(0, xh1[r], dy)
        d1 = norm_back(xh1[r], rs1[r], g_row(0), dy)
        d32[r] = d1
        db = d1.astype(BF)
        dab[r] = db
        drr = dot_nt(db, w_out_full()).astype(BF)
        for a in range(NT):
            dr[r, a] = drr[:, 128 * a:128 * a + 128]

    wo_all = dot_tn(wide(ctx, 0), dab[0]) + dot_tn(wide(ctx, 1), dab[1])
    for a in range(NT):
        for j in range(4):
            g[rel_of(a), G_OUT + 128 * j:G_OUT + 128 * j + 128] = (
                wo_all[128 * a:128 * a + 128, 128 * j:128 * j + 128].astype(BF))
    for q in range(3):
        pair(C_OUT, q).start()

    @pl.when(is_dec)
    def _():
        pair(C_OUT, 3).start()

    feed_on(C_UP)

    def attend_back(a, r, windows, encoder):
        k_t = turned(kk, a, r, windows[1][0] + windows[1][1])
        dks, dvs = [], []
        for b, (w0, wn) in enumerate(windows):
            rows = slice(b * 128, b * 128 + 128)
            d_r = dr[r, a, rows]
            d_r = jnp.concatenate([d_r * hmask[0, 0:128], d_r * hmask[1, 0:128]], axis=0)
            pb = pt[a, r, b, 0:wn]
            p = pb.astype(F32)
            dp_ = dot_nt(vv[a, r, w0:w0 + wn], d_r)
            ds = (p * (dp_ - jnp.sum(p * dp_, axis=0, keepdims=True))).astype(BF)
            dq = dot(k_t[:, w0:w0 + wn], ds)
            dq = jnp.concatenate([dq[0:64, 0:128], dq[64:128, 128:256]], axis=0)
            act[r, a, rows, 0:128] = (dq.T * SCALE).astype(BF)
            dks.append(dot(ds, qs[a, r, b]))
            dvs.append(dot(pb, d_r))
        (_, n0), (w1, n1_) = windows
        for j, (lo, hi) in enumerate((dks, dvs)):
            both = lo[w1:n0] + hi[0:n0 - w1]
            val = jnp.concatenate([lo[0:w1], both, hi[n0 - w1:n1_]], axis=0)
            dkv[a, r, j] = val[OWN:OWN + T]
            halo_s[0, a, r, j] = val[LEFT:LEFT + HALO].astype(BF)
            if encoder:
                halo_s[1, a, r, j] = val[RIGHT:RIGHT + HALO].astype(BF)
                mg_s[a, r, j + 1] = (val[0:MP] + val[MEM_2:MEM_2 + MP]).astype(BF)

    def halo_copies(a):
        return (remote(halo_s.at[0, a], halo_r.at[0, a], hsend.at[0, a], hrecv.at[0, a], tensor=left),
                remote(halo_s.at[1, a], halo_r.at[1, a], hsend.at[1, a], hrecv.at[1, a], tensor=right))

    first = jnp.where(t == 0, 1.0, 0.0)
    mg_copies = [remote(mg_s.at[lax.rem(t + off, NT)], mg_r.at[off - 1], qsend.at[off - 1], qrecv.at[off - 1],
                        tensor=lax.rem(t + off, NT)) for off in (1, 2, 3)]

    def add_g(start, val):
        n = val.shape[0]
        g[3, start:start + n] = (g[3, start:start + n].astype(F32) + val).astype(BF)

    def add_norm_m(at_, xh, dy):
        ng[at_:at_ + 1] += first * jnp.sum(dy * xh, axis=0, keepdims=True)
        ng[at_ + 3:at_ + 4] += first * jnp.sum(dy, axis=0, keepdims=True)

    def mem_back_first():
        for b in range(NT):
            remote(dkvm_s.at[b], dkvm_r.at[b], dsend.at[b], drecv.at[b], section=other, tensor=b).wait_recv()
        grads = []
        for j in range(2):
            tot = dkvm_r[0, j] + dkvm_r[1, j] + dkvm_r[2, j] + dkvm_r[3, j]
            grads.append(tot.astype(BF))
        ex_m[t] = (dot_nt(grads[0], wcross[t, 0]) + dot_nt(grads[1], wcross[t, 1])).astype(BF)
        ex_start(3)
        for j in range(2):
            g[3, G_CROSS + D * j:G_CROSS + D * j + D] = dot_tn(mm[...], grads[j]).astype(BF)
        pair(C_CROSS, 3).start()

    def mem_back_second():
        ex_wait(3)
        dm = ex_m[0].astype(F32)
        for s in range(1, NT):
            dm = dm + ex_m[s].astype(F32)
        add_norm_m(2, mx3[...], dm)
        rows_m = lax.broadcasted_iota(jnp.int32, (R * MP, D), 0)

        @pl.when(t == 0)
        def _():
            mem_local[1].wait()

        @pl.when(t > 0)
        def _():
            mem_c[0].wait_recv()

        cm = jnp.concatenate([cotm[0], cotm[1]], axis=0)
        cm = jnp.where(lax.rem(rows_m, MP) < MEM, cm, 0.0)
        dy = cm + norm_back(mx3[...], mr3[...], g_row(2), dm)
        add_norm_m(1, mx2[...], dy)
        d3 = norm_back(mx2[...], mr2[...], g_row(1), dy)
        d3b = d3.astype(BF)
        d2 = d3
        for a in range(NT):
            dum = (dot_nt(d3b, wdown[a]) * mgp[a]).astype(BF)
            d2 = d2 + dot_nt(dum, wup[a])
            mdu[a] = dum
        wd = dot_tn(mact[...], d3b)
        wu = dot_tn(mh[...].astype(BF), mdu[t])
        md[...] = d2
        for j in range(4):
            add_g(G_DOWN + D * j, wd[:, 128 * j:128 * j + 128])
            add_g(G_UP + D * j, wu[:, 128 * j:128 * j + 128])
        pair(C_DOWN, 3).start()
        pair(C_UP, 3).start()

    def mem_back_third():
        d2 = md[...]
        add_norm_m(0, mx1[...], d2)
        d1 = norm_back(mx1[...], mr1[...], g_row(0), d2)
        md[...] = d1
        d1b = d1.astype(BF)
        drm = dot_nt(d1b, w_out_full()).astype(BF).astype(F32)
        mh[...] = drm
        prod = drm * mc[...]
        for r in range(R):
            acc = jnp.zeros((MP, 128), F32)
            for hh in range(8):
                cols = prod[r * MP:r * MP + MP, (hh // 2) * 128:(hh // 2) * 128 + 128]
                cols = jnp.where(low_m if hh % 2 == 0 else jnp.logical_not(low_m), cols, 0.0)
                acc = jnp.where(lane_m == hh, jnp.sum(cols, axis=1, keepdims=True), acc)
            mst[1, r * MP:r * MP + MP] = acc
        for a in range(NT):
            @pl.when(t == a)
            def _():
                wo = dot_tn(mc[:, 128 * a:128 * a + 128].astype(BF), d1b)
                for j in range(4):
                    add_g(G_OUT + 128 * j, wo[:, 128 * j:128 * j + 128])
        pair(C_OUT, 3).start()

    def mem_attend_back():
        for a in range(NT):
            for r in range(R):
                rows = slice(r * MP, r * MP + MP)
                lse = mst[0, rows]
                dlt = mst[1, rows]
                lse = jnp.concatenate([lse[:, 2 * a:2 * a + 1], lse[:, 2 * a + 1:2 * a + 2]], axis=0)
                dlt = jnp.concatenate([dlt[:, 2 * a:2 * a + 1], dlt[:, 2 * a + 1:2 * a + 2]], axis=0)
                lhs = qm[a, r]
                ko, vo = kk[a, r, OWN:OWN + T], vv[a, r, OWN:OWN + T]
                p = jnp.exp(dot_nt(lhs, ko) - lse)
                dra = mh[rows, 128 * a:128 * a + 128]
                dra = jnp.concatenate([jnp.where(low_m, dra, 0.0), jnp.where(low_m, 0.0, dra)], axis=0).astype(BF)
                ds = (p * (dot_nt(dra, vo) - dlt)).astype(BF)
                dq = dot(ds, ko)
                mg_s[a, r, 0] = (jnp.where(low_m, dq[0:MP], dq[MP:2 * MP]) * SCALE).astype(BF)
                dkv[a, r, 0] += dot_tn(ds, lhs)
                dkv[a, r, 1] += dot_tn(p.astype(BF), dra)

        go(mg_copies)

    def order(i):
        return jnp.where(i == 0, 1, jnp.where(i == 1, 0, i))

    @pl.loop(0, NT * R)
    def _(i):
        a = shard_of(order(lax.div(i, 2)))
        r = lax.rem(i, 2)

        @pl.when(is_enc)
        def _():
            attend_back(a, r, WIN_ENC, True)

        @pl.when(is_dec)
        def _():
            attend_back(a, r, WIN_DEC, False)

        @pl.when(r == 1)
        def _():
            to_left, to_right = halo_copies(a)
            to_left.start()

            @pl.when(is_enc)
            def _():
                to_right.start()

        @pl.when(is_dec)
        def _():
            @pl.when(i == 1)
            def _():
                for k in (C_CROSS, C_OUT):
                    all_pairs_sum(k)
                    go([over_tensor(k, q) for q in range(3)])

        @pl.when(is_enc)
        def _():
            @pl.when(i == 1)
            def _():
                mem_back_first()

            @pl.when(i == 5)
            def _():
                mem_back_second()

            @pl.when(i == 6)
            def _():
                mem_back_third()

    n1 = [remote(ny.at[t], ny.at[t], ns.at[o - 1], nq.at[o - 1], tensor=lax.rem(t + o, NT)) for o in (1, 2, 3)]
    n2 = [remote(nc.at[0], nc.at[1], ns.at[3], nq.at[3], dp=sib)]
    n3 = [remote(nx.at[chip], nx.at[chip], ns.at[3 + o], nq.at[3 + o], dp=chip_at(o) * 2 + core)
          for o in range(1, chips)]

    def mem_last():
        for k in (C_DOWN, C_UP):
            all_pairs_sum(k, (3,))
            go(along_x(k, True))
        mem_attend_back()
        all_pairs_sum(C_OUT)
        go([over_tensor(C_OUT, q) for q in range(3)])
        all_pairs_sum(C_CROSS, (3,))
        start, lo, hf = at(C_CROSS)
        ysum[lo - LATE:lo - LATE + hf] = g[3, pl.ds(own_half(C_CROSS), hf)]
        go(over_chips(C_CROSS))

    ny[t] = ng[...]

    @pl.when(is_dec)
    def _():
        go(n1)

    @pl.when(is_enc)
    def _():
        go(n1)
        mem_last()

    dxm_copy = remote(dxm_s, dxm_r.at[t], gsend.at[0], grecv.at[t], tensor=0)

    def qkv_on(q):
        all_pairs_sum(C_QKV, (q,))
        go(chips_first(C_QKV, q))

    def mem_own():
        come(mg_copies)
        cols = []
        for j in range(3):
            both = []
            for r in range(R):
                tot = mg_s[t, r, j].astype(F32)
                for o in range(3):
                    tot = tot + mg_r[o, r, j].astype(F32)
                both.append(tot)
            cols.append(jnp.concatenate(both, axis=0))
        dm = jnp.concatenate(cols, axis=1).astype(BF)
        gw = dot_tn(x_mem(), dm)
        for j in range(3):
            add_g(G_QKV + D * j, gw[:, 128 * j:128 * j + 128])
        return dm

    @pl.loop(0, NT)
    def _(i):
        q = order(i)
        a = shard_of(q)
        to_left, to_right = halo_copies(a)
        to_left.wait_recv()

        @pl.when(is_enc)
        def _():
            to_right.wait_recv()

        for r in range(R):
            for j in range(2):
                dkv[a, r, j, T - HALO:T] += halo_r[0, a, r, j].astype(F32)

                @pl.when(is_enc)
                def _():
                    dkv[a, r, j, 0:HALO] += halo_r[1, a, r, j].astype(F32)

                act[r, a, :, 128 * (j + 1):128 * (j + 2)] = dkv[a, r, j].astype(BF)
        gw = dot_tn(x_ext[0, OWN:OWN + T], act[0, a, :, 0:384]) + dot_tn(x_ext[1, OWN:OWN + T], act[1, a, :, 0:384])
        for j in range(3):
            g[q, G_QKV + D * j:G_QKV + D * j + D] = gw[:, 128 * j:128 * j + 128].astype(BF)

        @pl.when(q < 3)
        def _():
            pair(C_QKV, q).start()

        wfull = jnp.concatenate([wqkv[a, j] for j in range(3)], axis=1)

        @pl.when(q == 3)
        def _():
            @pl.when(is_enc)
            def _():
                dm = mem_own()
                pair(C_QKV, 3).start()
                dxm_s[...] = dot_nt(dm, wfull).astype(BF)

                @pl.when(t > 0)
                def _():
                    dxm_copy.start()

            @pl.when(is_dec)
            def _():
                pair(C_QKV, 3).start()

        for r in range(R):
            d32[r] += dot_nt(act[r, a, :, 0:384], wfull)

        @pl.when(i > 0)
        def _():
            qkv_on(order(i - 1))

    qkv_on(3)

    come(n1)
    nc[0] = ny[0] + ny[1] + ny[2] + ny[3]
    go(n2)
    for k in (C_DOWN, C_UP):
        come(along_x(k, False))
        for q in range(3):
            along_x_sum(k, q)
        go(tensor_second(k))
    come(n2)
    nx[chip] = nc[0] + nc[1]
    go(n3)

    @pl.when(is_dec)
    def _():
        come([over_tensor(C_CROSS, q) for q in range(3)])
        tensor_sum(C_CROSS)
        go(over_chips(C_CROSS))

    come([over_tensor(C_OUT, q) for q in range(3)])
    tensor_sum(C_OUT)
    go(over_chips(C_OUT))
    for q in range(NT):
        come(chips_first(C_QKV, q))
        chips_first_sum(C_QKV, q)
    go(tensor_third(C_QKV))
    for k in (C_DOWN, C_UP):
        come(along_x(k, True))
        along_x_sum(k, 3)
        come(tensor_second(k))
        tensor_second_sum(k)
        go(over_z(k))
    come(tensor_third(C_QKV))
    tensor_third_sum(C_QKV)
    go(spread(C_QKV))
    for k in (C_CROSS, C_OUT):
        come(over_chips(k))
        chips_sum(k)
        go(spread(k))
    for k in (C_DOWN, C_UP):
        come(over_z(k))
        over_z_sum(k)
        go(spread_x(k))

    @pl.when(jnp.logical_and(is_enc, t == 0))
    def _():
        tot = md[...] + dxm_s[...].astype(F32)
        for s in range(1, NT):
            remote(dxm_s, dxm_r.at[s], gsend.at[0], grecv.at[s], tensor=0).wait_recv()
            tot = tot + dxm_r[s].astype(F32)
        for r in range(R):
            d32[r, 0:MP] += tot[r * MP:r * MP + MP]

    dx_copy = pltpu.make_async_copy(d32, dx_out, lsem.at[10])
    dx_copy.start()
    come(n3)
    tot_n = nx[0]
    for o in range(1, chips):
        tot_n = tot_n + nx[o]
    ng_tot[...] = tot_n
    for k in (C_CROSS, C_OUT):
        come(spread(k))
        go(hand(k))
    for k in (C_DOWN, C_UP):
        come(spread_x(k))
        go(hand(k))
    come(spread(C_QKV))
    go(hand(C_QKV))
    for k in range(5):
        come(hand(k))

    y_copy.wait()
    dx_copy.wait()
    for i in (QKV, OUT):
        gone(w_direct(i))
        gone(w_pair(i))
    for i in (UP, DOWN):
        gone(w_eighth(i))
        gone(w_along(i))
        gone(w_pair(i))
    x_right.wait_send()
    for a in range(NT):
        halo_copies(a)[0].wait_send()
    gone(n1)
    gone(n2)
    gone(n3)
    for k in range(5):
        if k in (C_DOWN, C_UP):
            gone(along_x(k, False))
            gone(along_x(k, True))
            gone(tensor_second(k))
            gone(over_z(k))
            gone(spread_x(k))
        elif k == C_QKV:
            for q in range(NT):
                gone(chips_first(k, q))
            gone(tensor_third(k))
            gone(spread(k))
        else:
            gone(over_chips(k))
            gone(spread(k))
        if k != C_CROSS:
            gone([pair(k, q) for q in range(NT)])
        gone(hand(k))
    gone([over_tensor(C_OUT, q) for q in range(3)])

    @pl.when(is_dec)
    def _():
        gone(w_direct(CROSS))
        gone(w_pair(CROSS))
        gone(dkv_copies)
        gone([pair(C_CROSS, q) for q in range(NT)])
        gone([over_tensor(C_CROSS, q) for q in range(3)])

    @pl.when(is_enc)
    def _():
        x_left.wait_send()
        pair(C_CROSS, 3).wait_send()
        for a in range(NT):
            halo_copies(a)[1].wait_send()
        for e in range(4):
            gone(exchanges[e])
        gone(mg_copies)
        gone(kv_copies)

        @pl.when(t == 0)
        def _():
            gone(mem_x)
            gone(mem_c)

        @pl.when(t > 0)
        def _():
            dxm_copy.wait_send()


def layer_call(chips, lens, x, cot, wqkv, wout, wcross, wup, wdown, gain, bias):
    any_ = pl.BlockSpec(memory_space=pl.ANY)
    vmem = pl.BlockSpec(memory_space=pltpu.VMEM)
    M = R * MP
    W = W_ENC
    S = pltpu.SemaphoreType.DMA
    C = len(CHUNKS)
    o = max(chips - 1, 1)
    late = HALF - LATE

    def V(shape, kind):
        return pltpu.VMEM(shape, kind)

    scratch = dict(
        x_ext=V((R, W, D), BF), cotm=V((R, MP, D), F32), d32=V((R, T, D), F32),
        wqkv=V((NT, 3, D, 128), BF), wout=V((NT, 128, D), BF), wcross=V((NT, 2, D, 128), BF),
        wup=V((NT, D, D), BF), wdown=V((NT, D, D), BF),
        kk=V((NT, R, W, 128), BF), vv=V((NT, R, W, 128), BF),
        qs=V((NT, R, 2, T, 128), BF), pt=V((NT, R, 2, 512, T), BF), ctx=V((R, NT, T, 128), BF),
        mask=V((R, 2, 512, 128), F32), hmask=V((2, T, 128), BF),
        xh1=V((R, T, D), F32), xh2=V((R, T, D), F32), rs1=V((R, T, 1), F32), rs2=V((R, T, 1), F32),
        h32=V((R, T, D), F32), hb=V((R, T, D), BF), h1b=V((R, T, D), BF),
        act=V((R, NT, T, D), BF), gp=V((R, NT, T, D), BF), dab=V((R, T, D), BF), dr=V((R, NT, T, 128), BF),
        dkv=V((NT, R, 2, T, 128), F32), halo_s=V((2, NT, R, 2, HALO, 128), BF),
        halo_r=V((2, NT, R, 2, HALO, 128), BF), mg_s=V((NT, R, 3, MP, 128), BF), mg_r=V((3, R, 3, MP, 128), BF),
        dxm_s=V((M, D), BF), dxm_r=V((NT, M, D), BF), mdu=V((NT, M, D), BF),
        ex_o=V((NT, NT, M, 128), BF), ex_st=V((NT, M, 128), F32), ex_f=V((NT, M, D), BF), ex_m=V((NT, M, D), BF),
        qm=V((NT, R, 2 * MP, 128), BF),
        kvm=V((NT, 2, M, 128), BF), dkvm_s=V((NT, 2, M, 128), F32), dkvm_r=V((NT, 2, M, 128), F32),
        kblk=V((R, 256, D), BF), vblk=V((R, 256, D), BF), cpt=V((R, 256, T), BF), cq=V((R, T, D), BF),
        cctx=V((R, T, D), BF), cdb=V((R, T, D), BF),
        mx1=V((M, D), F32), mx2=V((M, D), F32), mx3=V((M, D), F32), mr1=V((M, 1), F32), mr2=V((M, 1), F32),
        mr3=V((M, 1), F32), mh=V((M, D), F32), mact=V((M, D), BF), mgp=V((NT, M, D), F32), mc=V((M, D), F32),
        mm=V((M, D), BF), mst=V((2, M, 128), F32), md=V((M, D), F32),
        g=V((NT, G_ROWS, 128), BF), r1=V((NT, HALF, 128), BF), r2=V((3, late, 128), BF),
        r3=V((o, late // chips, 128), BF), rx=V((3, NT, LATE // 4, 128), BF), ry_s=V((NT, LATE // 4, 128), BF),
        ry_r=V((3, LATE // 4, 128), BF), zz=V((2, LATE // 4, 128), BF),
        rq=V((o, NT, 768 // chips, 128), BF), rqs=V((NT, 768 // chips, 128), BF), rqr=V((3, 768 // chips, 128), BF),
        ysum=V((late, 128), BF), ng=V((8, D), F32), ny=V((NT, 8, D), F32), nc=V((2, 8, D), F32),
        nx=V((chips, 8, D), F32),
        lsem=S((11,)), wsend=S((5, 6)), wrecv=S((5, 6)), w2send=S((2, 3, 3)), w2recv=S((2, 3, 3)), xsend=S((2,)), xrecv=S((2,)), msend=S((2, 3)), mrecv=S((2,)),
        esend=S((5, 3)), erecv=S((5, 3)), ksend=S((NT,)), krecv=S((NT,)), dsend=S((NT,)), drecv=S((NT,)),
        hsend=S((2, NT)), hrecv=S((2, NT)), gsend=S((1,)), grecv=S((NT,)), qsend=S((3,)), qrecv=S((3,)), sq=S((NT, o)), qq=S((NT, o)),
        s1=S((C, NT)), q1=S((C, NT)), s2=S((C, 3)), q2=S((C, 3)), s3=S((C, o)), q3=S((C, o)),
        s4=S((C, o)), q4=S((C, o)), s5=S((C,)), q5=S((C,)), ns=S((4 + o,)), nq=S((4 + o,)),
        sx=S((2, 2, 3)), qx=S((2, 2, 3)), sz=S((2,)), qz=S((2,)),
    )
    names = tuple(scratch)

    def kernel(*refs):
        layer_kernel(chips, names, *refs)

    return pl.pallas_call(
        kernel,
        out_shape=(
            jax.ShapeDtypeStruct((R, T, D), F32),
            jax.ShapeDtypeStruct((R, T, D), F32),
            jax.ShapeDtypeStruct((G_ROWS, 128), BF),
            jax.ShapeDtypeStruct((8, D), F32),
        ),
        in_specs=[pl.BlockSpec(memory_space=pltpu.SMEM)] + [any_] * 7 + [vmem] * 2,
        out_specs=(any_, any_, vmem, vmem),
        scratch_shapes=list(scratch.values()),
        compiler_params=pltpu.CompilerParams(
            collective_id=0, has_side_effects=True, vmem_limit_bytes=VMEM_BYTES
        ),
        name="layers",
    )(lens, x, cot, wqkv, wout, wcross, wup, wdown, gain, bias)


def finish_kernel(y_in, dx_in, full, ng, y, dx, o_qkv, o_out, o_cross, o_up, o_down, o_gain, o_bias, sems):
    copies = [pltpu.make_async_copy(y_in, y.at[0], sems.at[0]), pltpu.make_async_copy(dx_in, dx.at[0], sems.at[1])]
    for c in copies:
        c.start()
    for j in range(3):
        o_qkv[0, j] = full[G_QKV + D * j:G_QKV + D * j + D].astype(F32)
    for j in range(2):
        o_cross[0, j] = full[G_CROSS + D * j:G_CROSS + D * j + D].astype(F32)
    for j in range(4):
        cols = slice(128 * j, 128 * j + 128)
        o_out[0, :, cols] = full[G_OUT + 128 * j:G_OUT + 128 * j + 128].astype(F32)
        o_up[0, :, cols] = full[G_UP + D * j:G_UP + D * j + D].astype(F32)
        o_down[0, :, cols] = full[G_DOWN + D * j:G_DOWN + D * j + D].astype(F32)
    for i in range(3):
        o_gain[i] = ng[i:i + 1]
        o_bias[i] = ng[i + 3:i + 4]
    for c in copies:
        c.wait()


def finish_call(y, dx, full, ng):
    any_ = pl.BlockSpec(memory_space=pl.ANY)
    vmem = pl.BlockSpec(memory_space=pltpu.VMEM)
    shapes = ((1, R, T, D), (1, R, T, D), (1, 3, D, 128), (1, 128, D), (1, 2, D, 128), (1, D, D), (1, D, D),
              (3, 1, D), (3, 1, D))
    return pl.pallas_call(
        finish_kernel,
        out_shape=tuple(jax.ShapeDtypeStruct(s, F32) for s in shapes),
        in_specs=[vmem] * 4,
        out_specs=(any_, any_) + (vmem,) * 7,
        scratch_shapes=[pltpu.SemaphoreType.DMA((2,))],
        compiler_params=pltpu.CompilerParams(vmem_limit_bytes=VMEM_BYTES),
        name="finish",
    )(y, dx, full, ng)


def solution(mesh):
    chips = mesh.shape["dp"] // 2

    def shards(inputs, lengths, w_qkv, w_out, w_cross, w_up, w_down, norm_gain, norm_bias, cotangent):
        y, dx, full, ng = layer_call(
            chips, lengths, inputs[0], cotangent[0], w_qkv[0], w_out[0], w_cross[0], w_up[0], w_down[0],
            jnp.transpose(norm_gain, (1, 0, 2)), jnp.transpose(norm_bias, (1, 0, 2)))
        outs = finish_call(y, dx, full, ng)
        return outs[:7] + tuple(jnp.transpose(v, (1, 0, 2)) for v in outs[7:])

    return jax.shard_map(
        shards,
        mesh=mesh,
        in_specs=(
            P("section", "dp", "tensor", None),
            P("dp", None),
            P("section", None, None, "tensor"),
            P("section", "tensor", None),
            P("section", None, None, "tensor"),
            P("section", None, "tensor"),
            P("section", "tensor", None),
            P("section", None, None),
            P("section", None, None),
            P("section", "dp", "tensor", None),
        ),
        out_specs=(
            P("section", "dp", "tensor", None),
            P("section", "dp", "tensor", None),
            P("section", None, None, "tensor"),
            P("section", "tensor", None),
            P("section", None, None, "tensor"),
            P("section", None, "tensor"),
            P("section", "tensor", None),
            P("section", None, None),
            P("section", None, None),
        ),
        check_vma=False,
    )
```

time: 173 us -> 143 us (0.83)
  the two profiles are of different devices: /device:TPU:1 before, /device:TPU:33 now
where the time goes in v3:
time: 143 us
  Pallas kernels  142 us (99%)
    pallas_call x1, Pallas kernels, layer_call(): pl.pallas_call(kernel, out_shape=(jax.ShapeDtypeStruct((R, T, D), F32), j...  137 us
    pallas_call x1, Pallas kernels, finish_call(): pl.pallas_call(finish_kernel, out_shape=tuple((jax.ShapeDtypeStruct(s, F3...  5.32 us

profile of v3, /device:TPU:33, one launch (start us, length us, event | category | flops | bytes accessed | tf_op | source)
XLA Modules:
  0.0 142.8 jit_solution(5451659827237117866)
XLA Ops:
  0.6 136.7 %layers.1 = (f32[2,256,512]{2,1,0:T(8,128)}, f32[2,256,512]{2,1,0:T(8,128)}, bf16[7168,128]{1,0:T(8,128)(2,1)}, f32[8,512]{1,0:T(8,128)}) custom-call(s32[2,16]{1,0:T(2,128)} %refs_0_.1, bf16[2,256,512]{2,1,0:T(8,128)(2,1)} %bitcast.12, f32[2,256,512]{2,1,0:T(8,128)} %bitcast.11, bf16[3,512,128]{2,1,0:T(8,128)(2,1)} %bitcast.15, bf16[128,512]{1,0:T(8,128)(2,1)} %bitcast.17, ...), custom_call_target="tpu_custom_call" | custom-call | tf_op jit(solution)/shard_map/layers/pallas_call | solution.py:1408
  137.3 5.3 %finish.1 = (f32[1,2,256,512]{3,2,1,0:T(8,128)}, f32[1,2,256,512]{3,2,1,0:T(8,128)}, f32[1,3,512,128]{3,2,1,0:T(8,128)}, f32[1,128,512]{2,1,0:T(8,128)}, f32[1,2...) custom-call(f32[2,256,512]{2,1,0:T(8,128)} %get-tuple-element.22.y_i, ...), custom_call_target="tpu_custom_call" | custom-call | tf_op jit(solution)/shard_map/finish/pallas_call | solution.py:1451

commit v4 on v3

--- a/solution.py
+++ b/solution.py
@@ -13,6 +13,7 @@
 MEM = 20
 MP = 32
 R = 2
+M = R * MP
 T = 256
 HALO = 160
 D = 512
@@ -26,11 +27,14 @@
 SCALE = 0.125
 
 G_DOWN, G_UP, G_CROSS, G_OUT, G_QKV, G_ROWS = 0, 2048, 4096, 5120, 5632, 7168
-CHUNKS = ((G_DOWN, 2048), (G_UP, 2048), (G_CROSS, 1024), (G_OUT, 512), (G_QKV, 1536))
-C_DOWN, C_UP, C_CROSS, C_OUT, C_QKV = range(5)
+G_KV = G_QKV + 512
+CHUNKS = ((G_DOWN, 2048), (G_UP, 2048), (G_CROSS, 1024), (G_OUT, 512), (G_QKV, 512), (G_KV, 1024))
+CN = len(CHUNKS)
+C_DOWN, C_UP, C_CROSS, C_OUT, C_Q, C_KV = range(CN)
 LATE = G_CROSS // 2
 HALF = G_ROWS // 2
 QKV, OUT, CROSS, UP, DOWN = range(5)
+ALONG = {QKV: 0, UP: 1, DOWN: 2}
 W_ROWS = (512, 128, 512, 512, 512)
 
 
@@ -89,16 +93,16 @@
         m[n] for n in ("ex_o", "ex_st", "ex_f", "ex_m", "qm", "rq", "rqs", "rqr"))
     kvm, dkvm_s, dkvm_r, kblk, vblk, cpt, cq, cctx = (
         m[n] for n in ("kvm", "dkvm_s", "dkvm_r", "kblk", "vblk", "cpt", "cq", "cctx"))
-    mx1, mx2, mx3, mr1, mr2, mr3, mh, mact, mgp, mc, mm, mst, md = (
-        m[n] for n in ("mx1", "mx2", "mx3", "mr1", "mr2", "mr3", "mh", "mact", "mgp", "mc", "mm", "mst", "md"))
-    g, r1, r2, r3, rx, ry_s, ry_r, zz, ysum, ng, ny, nc, nx, cdb = (
-        m[n] for n in ("g", "r1", "r2", "r3", "rx", "ry_s", "ry_r", "zz", "ysum", "ng", "ny", "nc", "nx", "cdb"))
+    mx1, mx2, mx3, mr1, mr2, mr3, mh, mact, mc, mm, mst, md = (
+        m[n] for n in ("mx1", "mx2", "mx3", "mr1", "mr2", "mr3", "mh", "mact", "mc", "mm", "mst", "md"))
+    g, r1, rx, ry_s, ry_r, zz, ng, ny, nc, nx, cdb, dmb = (
+        m[n] for n in ("g", "r1", "rx", "ry_s", "ry_r", "zz", "ng", "ny", "nc", "nx", "cdb", "dmb"))
     (lsem, wsend, wrecv, xsend, xrecv, msend, mrecv, esend, erecv, ksend, krecv, dsend, drecv,
      hsend, hrecv, gsend, grecv, qsend, qrecv) = (
         m[n] for n in ("lsem", "wsend", "wrecv", "xsend", "xrecv", "msend", "mrecv", "esend", "erecv", "ksend",
                        "krecv", "dsend", "drecv", "hsend", "hrecv", "gsend", "grecv", "qsend", "qrecv"))
-    s1, q1, s2, q2, s3, q3, s4, q4, s5, q5, ns, nq = (
-        m[n] for n in ("s1", "q1", "s2", "q2", "s3", "q3", "s4", "q4", "s5", "q5", "ns", "nq"))
+    s1, q1, s2, q2, s4, q4, s5, q5, ns, nq = (
+        m[n] for n in ("s1", "q1", "s2", "q2", "s4", "q4", "s5", "q5", "ns", "nq"))
     w2send, w2recv, sx, qx, sz, qz, sq, qq = (
         m[n] for n in ("w2send", "w2recv", "sx", "qx", "sz", "qz", "sq", "qq"))
 
@@ -199,7 +203,7 @@
         for off in (1, 2, 3):
             rows = slot(i, source(off), at_8, eighth)
             for xo in (1, 2, 3):
-                out.append(remote(rows, rows, w2send.at[i - UP, off - 1, xo - 1], w2recv.at[i - UP, off - 1, xo - 1],
+                out.append(remote(rows, rows, w2send.at[ALONG[i], off - 1, xo - 1], w2recv.at[ALONG[i], off - 1, xo - 1],
                                   dp=x_dev(xo)))
         return out
 
@@ -243,22 +247,24 @@
     def ready(i):
         come(w_pair(i))
 
+    go(w_eighth(QKV))
+
     @pl.when(is_enc)
     def _():
         @pl.when(t == 0)
         def _():
             go(mem_x + mem_local)
 
-        go(w_direct(QKV))
         x_right.start()
         x_left.start()
+        go(w_eighth(UP))
+        go(w_direct(OUT))
 
     @pl.when(is_dec)
     def _():
         x_right.start()
-        go(w_direct(QKV))
+        go(w_eighth(UP))
         go(w_direct(OUT))
-        go(w_eighth(UP))
         go(w_eighth(DOWN))
         go(w_direct(CROSS))
 
@@ -266,30 +272,30 @@
     hmask[0] = jnp.where(lane < 64, 1.0, 0.0).astype(BF)
     hmask[1] = jnp.where(lane < 64, 0.0, 1.0).astype(BF)
 
-    def segments(pos, r):
-        off = pos - MEM
-        seg = jnp.where(off >= 0, 1, 0)
-        end = jnp.int32(0)
+    def bounds(pos, r):
+        end = jnp.int32(MEM)
+        first = jnp.where(pos >= MEM, MEM, 0)
+        after = jnp.full(pos.shape, MEM, jnp.int32)
         for k in range(16):
+            after = jnp.where(pos >= end, end + lens[r, k], after)
+            first = jnp.where(pos >= end, end, first)
             end = end + lens[r, k]
-            seg = seg + jnp.where(off >= end, 1, 0)
-        return seg
+        return first, after
 
     def make_masks(windows, encoder):
         for r in range(R):
             for b, (w0, wn) in enumerate(windows):
                 e = lax.broadcasted_iota(jnp.int32, (wn, 128), 0) + w0
                 pos = e - OWN + t * T
-                ks = segments(pos, r)
                 qpos = lax.broadcasted_iota(jnp.int32, (8, 128), 1) + (t * T + b * 128)
-                same = ks == segments(qpos, r)[0:1]
+                first, after = bounds(qpos, r)
+                ok = jnp.logical_and(pos >= first[0:1], pos < after[0:1])
                 if encoder:
                     mem_i = jnp.where(e < LEFT, e, jnp.where(e >= MEM_2, e - MEM_2, MEM))
                     ok = jnp.logical_or(mem_i < MEM, jnp.logical_and(
-                        jnp.logical_and(e >= LEFT, e < MEM_2), jnp.logical_and(same, ks > 0)))
+                        jnp.logical_and(e >= LEFT, e < MEM_2), jnp.logical_and(ok, pos >= MEM)))
                 else:
-                    ok = jnp.logical_and(jnp.logical_and(same, e >= LEFT),
-                                         jnp.logical_and(pos <= qpos[0:1], pos >= 0))
+                    ok = jnp.logical_and(jnp.logical_and(ok, e >= LEFT), pos <= qpos[0:1])
                 mask[r, b, 0:wn] = jnp.where(ok, 0.0, FILL)
 
     @pl.when(is_enc)
@@ -304,6 +310,7 @@
     ex_st[t] = jnp.zeros((R * MP, 128), F32)
     ng[...] = jnp.zeros(ng.shape, F32)
 
+    go_along(QKV)
     for c in locals_:
         c.wait()
 
@@ -332,25 +339,33 @@
     def turned(ref, a, r, hi):
         return ref[a, r, 0:hi].astype(F32).T.astype(BF)
 
-    def project_own(a):
-        wkv = keys_weight(a)
+    def project_own(shards_):
+        jobs = [(a, r) for a in shards_ for r in range(R)]
+        for a in shards_:
+            wkv = keys_weight(a)
+            for r in range(R):
+                keys(a, r, OWN, OWN + T, wkv)
+                queries(a, r)
+        lhs = []
+        for a, r in jobs:
+            m32 = dot(x_ext[r, 0:MP], wqkv[a, 0]).astype(BF).astype(F32) * SCALE
+            lhs.append(jnp.concatenate([jnp.where(low_m, m32, 0.0), jnp.where(low_m, 0.0, m32)], axis=0).astype(BF))
+        ss = [dot_nt(v, kk[a, r, OWN:OWN + T]) for v, (a, r) in zip(lhs, jobs)]
+        tops = [jnp.max(s, axis=1, keepdims=True) for s in ss]
+        ps = [jnp.exp(s - top) for s, top in zip(ss, tops)]
+        totals = [jnp.sum(p, axis=1, keepdims=True) for p in ps]
+        os_ = [dot(p.astype(BF), vv[a, r, OWN:OWN + T]) / total for p, total, (a, r) in zip(ps, totals, jobs)]
+        for (a, r), v, o in zip(jobs, lhs, os_):
+            qm[a, r] = v
+            ex_o[t, a, r * MP:r * MP + MP] = jnp.where(low_m, o[0:MP], o[MP:2 * MP]).astype(BF)
         for r in range(R):
-            keys(a, r, OWN, OWN + T, wkv)
-            queries(a, r)
-            m32 = dot(x_ext[r, 0:MP], wqkv[a, 0]).astype(BF).astype(F32) * SCALE
-            lhs = jnp.concatenate([jnp.where(low_m, m32, 0.0), jnp.where(low_m, 0.0, m32)], axis=0).astype(BF)
-            qm[a, r] = lhs
-            s = dot_nt(lhs, kk[a, r, OWN:OWN + T])
-            top = jnp.max(s, axis=1, keepdims=True)
-            p = jnp.exp(s - top)
-            total = jnp.sum(p, axis=1, keepdims=True)
-            o = dot(p.astype(BF), vv[a, r, OWN:OWN + T]) / total
-            ex_o[t, a, r * MP:r * MP + MP] = jnp.where(low_m, o[0:MP], o[MP:2 * MP]).astype(BF)
             st = ex_st[t, r * MP:r * MP + MP]
-            st = jnp.where(lane_m == 2 * a, top[0:MP], st)
-            st = jnp.where(lane_m == 2 * a + 1, top[MP:2 * MP], st)
-            st = jnp.where(lane_m == 2 * a + 8, total[0:MP], st)
-            st = jnp.where(lane_m == 2 * a + 9, total[MP:2 * MP], st)
+            for (a, r_), top, total in zip(jobs, tops, totals):
+                if r_ == r:
+                    st = jnp.where(lane_m == 2 * a, top[0:MP], st)
+                    st = jnp.where(lane_m == 2 * a + 1, top[MP:2 * MP], st)
+                    st = jnp.where(lane_m == 2 * a + 8, total[0:MP], st)
+                    st = jnp.where(lane_m == 2 * a + 9, total[MP:2 * MP], st)
             ex_st[t, r * MP:r * MP + MP] = st
 
     def project_rest(a):
@@ -443,15 +458,20 @@
         for c in kv_copies:
             c.start()
 
-    def attend(a, r, windows):
-        v_t = turned(vv, a, r, windows[1][0] + windows[1][1])
-        for b, (w0, wn) in enumerate(windows):
+    def attend(a, windows):
+        jobs = [(r, b, w0, wn) for r in range(R) for b, (w0, wn) in enumerate(windows)]
+        v_t = [turned(vv, a, r, windows[1][0] + windows[1][1]) for r in range(R)]
+        scores = []
+        for r, b, w0, wn in jobs:
             mk = mask[r, b, 0:wn]
-            s = dot_nt(kk[a, r, w0:w0 + wn], qs[a, r, b]) + jnp.concatenate([mk, mk], axis=1)
+            scores.append(dot_nt(kk[a, r, w0:w0 + wn], qs[a, r, b]) + jnp.concatenate([mk, mk], axis=1))
+        ps = []
+        for s in scores:
             p = jnp.exp(s - jnp.max(s, axis=0, keepdims=True))
-            p = (p * (1.0 / jnp.sum(p, axis=0, keepdims=True))).astype(BF)
+            ps.append((p * (1.0 / jnp.sum(p, axis=0, keepdims=True))).astype(BF))
+        for (r, b, w0, wn), p in zip(jobs, ps):
             pt[a, r, b, 0:wn] = p
-            o = dot(v_t[:, w0:w0 + wn], p)
+            o = dot(v_t[r][:, w0:w0 + wn], p)
             o = jnp.concatenate([o[0:64, 0:128], o[64:128, 128:256]], axis=0)
             ctx[r, a, b * 128:b * 128 + 128] = o.T.astype(BF)
 
@@ -466,83 +486,70 @@
 
         x_ext[:, MEM_2:MEM_2 + MP] = x_ext[:, 0:MP]
 
-        @pl.loop(0, NT)
-        def _(step):
-            @pl.when(step == 1)
-            def _():
-                arrive(QKV)
-                ready(QKV)
-
-            project_own(shard_at(step))
-
+        project_own([t])
+        come_along(QKV)
+        ready(QKV)
+        project_own([left, right, opp])
         ex_start(0)
         ex_start(1)
-        go(w_direct(OUT))
-        go(w_eighth(UP))
+        go(w_eighth(DOWN))
         x_right.wait_recv()
         x_left.wait_recv()
+        go_along(UP)
+        arrive(OUT)
 
         @pl.loop(0, NT)
         def _(step):
             project_rest(shard_at(step))
 
-        @pl.loop(0, NT * R)
+        @pl.loop(0, NT)
         def _(i):
             @pl.when(i == 2)
             def _():
-                arrive(OUT)
                 ex_wait(0)
                 ex_wait(1)
                 ready(OUT)
                 mem_first()
-                go(w_eighth(DOWN))
-                go_along(UP)
-
-            @pl.when(i == 6)
+                go_along(DOWN)
+
+            @pl.when(i == 3)
             def _():
                 ex_wait(2)
                 mem_second()
-                go_along(DOWN)
 
                 @pl.when(t == 0)
                 def _():
                     go(mem_c)
 
-            attend(shard_at(lax.div(i, 2)), lax.rem(i, 2), WIN_ENC)
+            attend(shard_at(i), WIN_ENC)
 
     def decoder_attention():
         x_right.wait_recv()
 
-        @pl.loop(0, NT * R)
+        project_all(t)
+
+        @pl.loop(0, NT)
         def _(i):
             @pl.when(i == 1)
             def _():
-                arrive(QKV)
-
-            @pl.when(i == 2)
-            def _():
+                come_along(QKV)
+                go_along(UP)
                 ready(QKV)
 
-            step_from = jnp.where(i == 0, 0, jnp.where(i == 2, 1, 4))
-            step_to = jnp.where(i == 0, 1, 4)
-
-            @pl.loop(step_from, step_to)
-            def _(step):
-                project_all(shard_at(step))
+                @pl.loop(1, NT)
+                def _(step):
+                    project_all(shard_at(step))
 
             @pl.when(i == 2)
             def _():
                 arrive(OUT)
-                go_along(UP)
-
-            @pl.when(i == 5)
+
+            @pl.when(i == 3)
             def _():
                 go_along(DOWN)
                 ready(OUT)
 
-            attend(shard_at(lax.div(i, 2)), lax.rem(i, 2), WIN_DEC)
-
-        arrive(CROSS)
+            attend(shard_at(i), WIN_DEC)
 
     @pl.when(is_enc)
     def _():
@@ -552,18 +559,15 @@
     def _():
         decoder_attention()
 
-    @pl.loop(0, R)
-    def _(r):
-        a0 = x_ext[r, OWN:OWN + T].astype(F32) + dot(wide(ctx, r), w_out_full())
-        xh, rs = normed(a0)
+    both = range(R)
+    a0s = [x_ext[r, OWN:OWN + T].astype(F32) + dot(wide(ctx, r), w_out_full()) for r in both]
+    for r, (xh, rs) in enumerate([normed(v) for v in a0s]):
         xh1[r] = xh
         rs1[r] = rs
         h = xh * g_row(0) + b_row(0)
         h32[r] = h
         hb[r] = h.astype(BF)
 
-    come_along(UP)
-
     pad_mask = jnp.where(
         lax.rem(lax.broadcasted_iota(jnp.int32, (256, T), 0), MP) < MEM, 0.0, FILL)
 
@@ -571,6 +575,8 @@
         return jnp.concatenate([wcross[a, j] for a in range(NT)], axis=1)
 
     def cross_forward():
+        arrive(CROSS)
+        come_along(UP)
         ready(CROSS)
         wc0 = full_cross(0)
         wc1 = full_cross(1)
@@ -592,17 +598,16 @@
                     kblk[r, at, a * 128:a * 128 + 128] = kvm[a, 0, r * MP:r * MP + MP] * hmask[h, 0:MP]
                     vblk[r, at, a * 128:a * 128 + 128] = kvm[a, 1, r * MP:r * MP + MP] * hmask[h, 0:MP]
 
-        @pl.loop(0, R)
-        def _(r):
-            s = dot_nt(kblk[r], cq[r]) + pad_mask
-            s = s.reshape(8, MP, T)
+        ss = [(dot_nt(kblk[r], cq[r]) + pad_mask).reshape(8, MP, T) for r in both]
+        ps = []
+        for s in ss:
             p = jnp.exp(s - jnp.max(s, axis=1, keepdims=True))
-            p = p * (1.0 / jnp.sum(p, axis=1, keepdims=True))
-            p = p.reshape(256, T).astype(BF)
-            cpt[r] = p
-            c = dot_tn(p, vblk[r]).astype(BF)
-            cctx[r] = c
-            xh, rs = normed(h32[r] + dot_nt(c, wc1))
+            ps.append((p * (1.0 / jnp.sum(p, axis=1, keepdims=True))).reshape(256, T).astype(BF))
+        cs = [dot_tn(p, vblk[r]).astype(BF) for r, p in enumerate(ps)]
+        sums = [h32[r] + dot_nt(c, wc1) for r, c in enumerate(cs)]
+        for r, (xh, rs) in enumerate([normed(v) for v in sums]):
+            cpt[r] = ps[r]
+            cctx[r] = cs[r]
             xh2[r] = xh
             rs2[r] = rs
             h = xh * g_row(1) + b_row(1)
@@ -613,23 +618,27 @@
     def _():
         cross_forward()
 
-    @pl.loop(0, NT * R)
+    @pl.when(is_enc)
+    def _():
+        come_along(UP)
+
+    @pl.loop(0, NT)
     def _(i):
-        @pl.when(i == 2)
+        @pl.when(i == 1)
         def _():
             ready(UP)
 
-        a = shard_at(lax.div(i, 2))
-        r = lax.rem(i, 2)
-        av, gv = gelu_both(dot(hb[r], wup[a]))
-        act[r, a] = av.astype(BF)
-        gp[r, a] = gv.astype(BF)
+        a = shard_at(i)
+        us = [dot(hb[r], wup[a]) for r in both]
+        for r, (av, gv) in enumerate([gelu_both(u) for u in us]):
+            act[r, a] = av.astype(BF)
+            gp[r, a] = gv.astype(BF)
 
     @pl.when(is_enc)
     def _():
         for a in range(NT):
             _, gv = gelu_both(dot(mh[...].astype(BF), wup[a]))
-            mgp[a] = gv
+            xh2[a // 2, (a % 2) * M:(a % 2) * M + M] = gv
 
     come_along(DOWN)
     ready(DOWN)
@@ -645,19 +654,17 @@
     row_i = lax.broadcasted_iota(jnp.int32, (T, D), 0)
     is_mem_row = jnp.logical_and(row_i < MEM, jnp.logical_and(is_enc, t == 0))
 
-    @pl.loop(0, R)
-    def _(r):
-        third = h32[r]
-        for a in range(NT):
-            third = third + dot(act[r, a], wdown[a])
-        xh, rs = normed(third)
+    thirds = [h32[r] + dot(wide(act, r), wdown[...].reshape(NT * D, D)) for r in both]
+    nrms = [normed(v) for v in thirds]
+    dys = [jnp.where(is_mem_row, 0.0, d32[r]) for r in both]
+    d3s = [norm_back(xh, rs, g_last, dy) for (xh, rs), dy in zip(nrms, dys)]
+    for r in both:
+        xh, dy = nrms[r][0], dys[r]
         h32[r] = xh * g_last + b_last
-        dy = jnp.where(is_mem_row, 0.0, d32[r])
-        d3 = norm_back(xh, rs, g_last, dy)
         ng[pl.ds(last, 1)] += jnp.sum(dy * xh, axis=0, keepdims=True)
         ng[pl.ds(last + 3, 1)] += jnp.sum(dy, axis=0, keepdims=True)
-        d32[r] = d3
-        dab[r] = d3.astype(BF)
+        d32[r] = d3s[r]
+        dab[r] = d3s[r].astype(BF)
 
     @pl.when(jnp.logical_and(is_enc, t == 0))
     def _():
@@ -690,37 +697,6 @@
         start, lo, hf = at(k)
         rows = pl.ds(own_half(k), hf)
         g[q, rows] = (g[q, rows].astype(F32) + r1[q, lo:lo + hf].astype(F32)).astype(BF)
-
-    def over_tensor(k, q):
-        start, lo, hf = at(k)
-        return remote(g.at[q, pl.ds(own_half(k), hf), :], r2.at[q, pl.ds(lo - LATE, hf), :],
-                      s2.at[k, q], q2.at[k, q], tensor=shard_of(q))
-
-    def tensor_sum(k):
-        start, lo, hf = at(k)
-        tot = g[3, pl.ds(own_half(k), hf)].astype(F32)
-        for rel in range(3):
-            tot = tot + r2[rel, lo - LATE:lo - LATE + hf].astype(F32)
-        ysum[lo - LATE:lo - LATE + hf] = tot.astype(BF)
-
-    def over_chips(k):
-        start, lo, hf = at(k)
-        n = hf // chips
-        out = []
-        for off in range(1, chips):
-            to = chip_at(off)
-            out.append(remote(ysum.at[pl.ds(lo - LATE + to * n, n), :],
-                              r3.at[off - 1, pl.ds((lo - LATE) // chips, n), :],
-                              s3.at[k, off - 1], q3.at[k, off - 1], dp=to * 2 + core))
-        return out
-
-    def chips_sum(k):
-        start, lo, hf = at(k)
-        n = hf // chips
-        tot = ysum[pl.ds(lo - LATE + chip * n, n)].astype(F32)
-        for o in range(chips - 1):
-            tot = tot + r3[o, (lo - LATE) // chips:(lo - LATE) // chips + n].astype(F32)
-        full[pl.ds(own_half(k) + chip * n, n)] = tot.astype(BF)
 
     def chips_first(k, q):
         start, lo, hf = at(k)
@@ -728,27 +704,41 @@
         out = []
         for off in range(1, chips):
             to = chip_at(off)
-            out.append(remote(g.at[q, pl.ds(own_half(k) + to * n, n), :], rq.at[off - 1, q],
-                              sq.at[q, off - 1], qq.at[q, off - 1], dp=to * 2 + core))
+            out.append(remote(g.at[q, pl.ds(own_half(k) + to * n, n), :],
+                              rq.at[off - 1, q, pl.ds((lo - LATE) // chips, n), :],
+                              sq.at[k, q, off - 1], qq.at[k, q, off - 1], dp=to * 2 + core))
         return out
 
-    def chips_first_sum(k, q):
+    def chips_on(k, some):
+        all_pairs_sum(k, some)
+        for q in some:
+            go(chips_first(k, q))
+
+    def chips_done(k, some):
         start, lo, hf = at(k)
         n = hf // chips
-        tot = g[q, pl.ds(own_half(k) + chip * n, n)].astype(F32)
-        for o in range(chips - 1):
-            tot = tot + rq[o, q].astype(F32)
-        rqs[q] = tot.astype(BF)
+        base = (lo - LATE) // chips
+        for q in some:
+            come(chips_first(k, q))
+            tot = g[q, pl.ds(own_half(k) + chip * n, n)].astype(F32)
+            for o in range(chips - 1):
+                tot = tot + rq[o, q, base:base + n].astype(F32)
+            rqs[q, base:base + n] = tot.astype(BF)
 
     def tensor_third(k):
-        return [remote(rqs.at[q], rqr.at[q], s2.at[k, q], q2.at[k, q], tensor=shard_of(q)) for q in range(3)]
-
-    def tensor_third_sum(k):
+        start, lo, hf = at(k)
+        rows = pl.ds((lo - LATE) // chips, hf // chips)
+        return [remote(rqs.at[q, rows, :], rqr.at[q, rows, :], s2.at[k, q], q2.at[k, q], tensor=shard_of(q))
+                for q in range(3)]
+
+    def tensor_third_sum(k, only_own=False):
         start, lo, hf = at(k)
         n = hf // chips
-        tot = rqs[3].astype(F32)
-        for q in range(3):
-            tot = tot + rqr[q].astype(F32)
+        base = (lo - LATE) // chips
+        tot = rqs[3, base:base + n].astype(F32)
+        if not only_own:
+            for q in range(3):
+                tot = tot + rqr[q, base:base + n].astype(F32)
         full[pl.ds(own_half(k) + chip * n, n)] = tot.astype(BF)
 
     quarter = LATE // 8
@@ -828,14 +818,15 @@
         a = shard_of(q)
         put_feed(C_DOWN, q, dot_tn(act[0, a], dab[0]) + dot_tn(act[1, a], dab[1]))
 
-    @pl.loop(0, R)
-    def _(r):
-        d = d32[r]
-        for a in range(NT):
-            du = (dot_nt(dab[r], wdown[a]) * gp[r, a].astype(F32)).astype(BF)
-            gp[r, a] = du
-            d = d + dot_nt(du, wup[a])
-        d32[r] = d
+    @pl.loop(0, NT)
+    def _(a):
+        dacts = [dot_nt(dab[r], wdown[a]) for r in both]
+        for r in both:
+            gp[r, a] = (dacts[r] * gp[r, a].astype(F32)).astype(BF)
+
+    w_up_all = jnp.concatenate([wup[a] for a in range(NT)], axis=1)
+    for r in both:
+        d32[r] += dot_nt(wide(gp, r), w_up_all)
 
     def feed_on(k):
         all_pairs_sum(k, range(3))
@@ -856,33 +847,38 @@
         wc0 = full_cross(0)
         wc1 = full_cross(1)
 
-        @pl.loop(0, R)
-        def _(r):
-            dy = d32[r]
-            add_norm(1, xh2[r], dy)
-            d2 = norm_back(xh2[r], rs2[r], g_row(1), dy)
-            d32[r] = d2
-            dcb = d2.astype(BF)
-            cdb[r] = dcb
-            dc = dot(dcb, wc1).astype(BF)
+        dys = [d32[r] for r in both]
+        d2s = [norm_back(xh2[r], rs2[r], g_row(1), dys[r]) for r in both]
+        dcs = []
+        for r in both:
+            d32[r] = d2s[r]
+            cdb[r] = d2s[r].astype(BF)
+        for r in both:
+            dcs.append(dot(cdb[r], wc1).astype(BF))
+        dps = [dot_nt(vblk[r], dcs[r]).reshape(8, MP, T) for r in both]
+        dss = []
+        for r in both:
             p = cpt[r].astype(F32).reshape(8, MP, T)
-            dp_ = dot_nt(vblk[r], dc).reshape(8, MP, T)
-            ds = p * (dp_ - jnp.sum(p * dp_, axis=1, keepdims=True))
-            ds = ds.reshape(256, T).astype(BF)
-            dk = dot(ds, cq[r])
-            dv = dot(cpt[r], dc)
-            rows = pl.ds(pl.multiple_of(r * MP, MP), MP)
+            ds = p * (dps[r] - jnp.sum(p * dps[r], axis=1, keepdims=True))
+            dss.append(ds.reshape(256, T).astype(BF))
+        dks = [dot(dss[r], cq[r]) for r in both]
+        dvs = [dot(cpt[r], dcs[r]) for r in both]
+        for r in both:
+            rows = slice(r * MP, r * MP + MP)
             for a in range(NT):
-                for j, val in ((0, dk), (1, dv)):
+                for j, val in ((0, dks[r]), (1, dvs[r])):
                     dkvm_s[a, j, rows] = jnp.where(
                         low_m, val[64 * a:64 * a + MP, 128 * a:128 * a + 128],
                         val[64 * a + MP:64 * a + 2 * MP, 128 * a:128 * a + 128])
-            dq = (dot_tn(ds, kblk[r]) * SCALE).astype(BF)
-            cq[r] = dq
-
-        for c in dkv_copies:
-            c.start()
-
+        go(dkv_copies)
+        dqs = [(dot_tn(dss[r], kblk[r]) * SCALE).astype(BF) for r in both]
+        for r in both:
+            add_norm(1, xh2[r], dys[r])
+            cq[r] = dqs[r]
+        for r in both:
+            d32[r] += dot_nt(dqs[r], wc0)
+
+    def cross_grads():
         gq = dot_tn(h1b[0], cq[0]) + dot_tn(h1b[1], cq[1])
         go_ = dot_tn(cdb[0], cctx[0]) + dot_tn(cdb[1], cctx[1])
         for a in range(NT):
@@ -891,10 +887,6 @@
             g[q, G_CROSS + D:G_CROSS + 2 * D] = go_[:, 128 * a:128 * a + 128].astype(BF)
         all_pairs(C_CROSS)
 
-        @pl.loop(0, R)
-        def _(r):
-            d32[r] += dot_nt(cq[r], wc0)
-
     @pl.when(is_dec)
     def _():
         cross_backward()
@@ -904,57 +896,63 @@
         a = shard_of(q)
         put_feed(C_UP, q, dot_tn(hb[0], gp[0, a]) + dot_tn(hb[1], gp[1, a]))
 
-    @pl.loop(0, R)
-    def _(r):
-        dy = d32[r]
-        add_norm(0, xh1[r], dy)
-        d1 = norm_back(xh1[r], rs1[r], g_row(0), dy)
-        d32[r] = d1
-        db = d1.astype(BF)
-        dab[r] = db
-        drr = dot_nt(db, w_out_full()).astype(BF)
+    dys1 = [d32[r] for r in both]
+    d1s = [norm_back(xh1[r], rs1[r], g_row(0), dys1[r]) for r in both]
+    for r in both:
+        d32[r] = d1s[r]
+        dab[r] = d1s[r].astype(BF)
+    for r in both:
+        drr = dot_nt(dab[r], w_out_full()).astype(BF)
         for a in range(NT):
             dr[r, a] = drr[:, 128 * a:128 * a + 128]
-
-    wo_all = dot_tn(wide(ctx, 0), dab[0]) + dot_tn(wide(ctx, 1), dab[1])
-    for a in range(NT):
-        for j in range(4):
-            g[rel_of(a), G_OUT + 128 * j:G_OUT + 128 * j + 128] = (
-                wo_all[128 * a:128 * a + 128, 128 * j:128 * j + 128].astype(BF))
-    for q in range(3):
-        pair(C_OUT, q).start()
-
-    @pl.when(is_dec)
-    def _():
-        pair(C_OUT, 3).start()
+    for r in both:
+        add_norm(0, xh1[r], dys1[r])
+
+    def out_grads():
+        wo_all = dot_tn(wide(ctx, 0), dab[0]) + dot_tn(wide(ctx, 1), dab[1])
+        for a in range(NT):
+            for j in range(4):
+                g[rel_of(a), G_OUT + 128 * j:G_OUT + 128 * j + 128] = (
+                    wo_all[128 * a:128 * a + 128, 128 * j:128 * j + 128].astype(BF))
+        for q in range(3):
+            pair(C_OUT, q).start()
+
+        @pl.when(is_dec)
+        def _():
+            pair(C_OUT, 3).start()
 
     feed_on(C_UP)
 
-    def attend_back(a, r, windows, encoder):
-        k_t = turned(kk, a, r, windows[1][0] + windows[1][1])
+    def attend_back(a, windows, encoder):
+        jobs = [(r, b, w0, wn) for r in range(R) for b, (w0, wn) in enumerate(windows)]
+        k_t = [turned(kk, a, r, windows[1][0] + windows[1][1]) for r in range(R)]
+        drs, dps, dss = [], [], []
+        for r, b, w0, wn in jobs:
+            d_r = dr[r, a, b * 128:b * 128 + 128]
+            d_r = jnp.concatenate([d_r * hmask[0, 0:128], d_r * hmask[1, 0:128]], axis=0)
+            drs.append(d_r)
+            dps.append(dot_nt(vv[a, r, w0:w0 + wn], d_r))
+        for (r, b, w0, wn), dp_ in zip(jobs, dps):
+            p = pt[a, r, b, 0:wn].astype(F32)
+            dss.append((p * (dp_ - jnp.sum(p * dp_, axis=0, keepdims=True))).astype(BF))
         dks, dvs = [], []
-        for b, (w0, wn) in enumerate(windows):
-            rows = slice(b * 128, b * 128 + 128)
-            d_r = dr[r, a, rows]
-            d_r = jnp.concatenate([d_r * hmask[0, 0:128], d_r * hmask[1, 0:128]], axis=0)
-            pb = pt[a, r, b, 0:wn]
-            p = pb.astype(F32)
-            dp_ = dot_nt(vv[a, r, w0:w0 + wn], d_r)
-            ds = (p * (dp_ - jnp.sum(p * dp_, axis=0, keepdims=True))).astype(BF)
-            dq = dot(k_t[:, w0:w0 + wn], ds)
+        for (r, b, w0, wn), ds, d_r in zip(jobs, dss, drs):
+            dq = dot(k_t[r][:, w0:w0 + wn], ds)
             dq = jnp.concatenate([dq[0:64, 0:128], dq[64:128, 128:256]], axis=0)
-            act[r, a, rows, 0:128] = (dq.T * SCALE).astype(BF)
+            act[r, a, b * 128:b * 128 + 128, 0:128] = (dq.T * SCALE).astype(BF)
             dks.append(dot(ds, qs[a, r, b]))
-            dvs.append(dot(pb, d_r))
+            dvs.append(dot(pt[a, r, b, 0:wn], d_r))
         (_, n0), (w1, n1_) = windows
-        for j, (lo, hi) in enumerate((dks, dvs)):
-            both = lo[w1:n0] + hi[0:n0 - w1]
-            val = jnp.concatenate([lo[0:w1], both, hi[n0 - w1:n1_]], axis=0)
-            dkv[a, r, j] = val[OWN:OWN + T]
-            halo_s[0, a, r, j] = val[LEFT:LEFT + HALO].astype(BF)
-            if encoder:
-                halo_s[1, a, r, j] = val[RIGHT:RIGHT + HALO].astype(BF)
-                mg_s[a, r, j + 1] = (val[0:MP] + val[MEM_2:MEM_2 + MP]).astype(BF)
+        for r in range(R):
+            for j, parts in enumerate((dks, dvs)):
+                lo, hi = parts[2 * r], parts[2 * r + 1]
+                both = lo[w1:n0] + hi[0:n0 - w1]
+                val = jnp.concatenate([lo[0:w1], both, hi[n0 - w1:n1_]], axis=0)
+                dkv[a, r, j] = val[OWN:OWN + T]
+                halo_s[0, a, r, j] = val[LEFT:LEFT + HALO].astype(BF)
+                if encoder:
+                    halo_s[1, a, r, j] = val[RIGHT:RIGHT + HALO].astype(BF)
+                    mg_s[a, r, j + 1] = (val[0:MP] + val[MEM_2:MEM_2 + MP]).astype(BF)
 
     def halo_copies(a):
         return (remote(halo_s.at[0, a], halo_r.at[0, a], hsend.at[0, a], hrecv.at[0, a], tensor=left),
@@ -1009,7 +1007,7 @@
         d3b = d3.astype(BF)
         d2 = d3
         for a in range(NT):
-            dum = (dot_nt(d3b, wdown[a]) * mgp[a]).astype(BF)
+            dum = (dot_nt(d3b, wdown[a]) * xh2[a // 2, (a % 2) * M:(a % 2) * M + M]).astype(BF)
             d2 = d2 + dot_nt(dum, wup[a])
             mdu[a] = dum
         wd = dot_tn(mact[...], d3b)
@@ -1027,6 +1025,7 @@
         d1 = norm_back(mx1[...], mr1[...], g_row(0), d2)
         md[...] = d1
         d1b = d1.astype(BF)
+        dmb[...] = d1b
         drm = dot_nt(d1b, w_out_full()).astype(BF).astype(F32)
         mh[...] = drm
         prod = drm * mc[...]
@@ -1037,79 +1036,89 @@
                 cols = jnp.where(low_m if hh % 2 == 0 else jnp.logical_not(low_m), cols, 0.0)
                 acc = jnp.where(lane_m == hh, jnp.sum(cols, axis=1, keepdims=True), acc)
             mst[1, r * MP:r * MP + MP] = acc
+    def mem_out():
         for a in range(NT):
             @pl.when(t == a)
             def _():
-                wo = dot_tn(mc[:, 128 * a:128 * a + 128].astype(BF), d1b)
+                wo = dot_tn(mc[:, 128 * a:128 * a + 128].astype(BF), dmb[...])
                 for j in range(4):
                     add_g(G_OUT + 128 * j, wo[:, 128 * j:128 * j + 128])
         pair(C_OUT, 3).start()
 
     def mem_attend_back():
-        for a in range(NT):
-            for r in range(R):
-                rows = slice(r * MP, r * MP + MP)
-                lse = mst[0, rows]
-                dlt = mst[1, rows]
-                lse = jnp.concatenate([lse[:, 2 * a:2 * a + 1], lse[:, 2 * a + 1:2 * a + 2]], axis=0)
-                dlt = jnp.concatenate([dlt[:, 2 * a:2 * a + 1], dlt[:, 2 * a + 1:2 * a + 2]], axis=0)
-                lhs = qm[a, r]
-                ko, vo = kk[a, r, OWN:OWN + T], vv[a, r, OWN:OWN + T]
-                p = jnp.exp(dot_nt(lhs, ko) - lse)
-                dra = mh[rows, 128 * a:128 * a + 128]
-                dra = jnp.concatenate([jnp.where(low_m, dra, 0.0), jnp.where(low_m, 0.0, dra)], axis=0).astype(BF)
-                ds = (p * (dot_nt(dra, vo) - dlt)).astype(BF)
-                dq = dot(ds, ko)
-                mg_s[a, r, 0] = (jnp.where(low_m, dq[0:MP], dq[MP:2 * MP]) * SCALE).astype(BF)
-                dkv[a, r, 0] += dot_tn(ds, lhs)
-                dkv[a, r, 1] += dot_tn(p.astype(BF), dra)
-
+        jobs = [(a, r) for a in range(NT) for r in range(R)]
+        ss = [dot_nt(qm[a, r], kk[a, r, OWN:OWN + T]) for a, r in jobs]
+        dras, dlts, ps = [], [], []
+        for (a, r), s in zip(jobs, ss):
+            rows = slice(r * MP, r * MP + MP)
+            lse = mst[0, rows]
+            dlt = mst[1, rows]
+            lse = jnp.concatenate([lse[:, 2 * a:2 * a + 1], lse[:, 2 * a + 1:2 * a + 2]], axis=0)
+            dlts.append(jnp.concatenate([dlt[:, 2 * a:2 * a + 1], dlt[:, 2 * a + 1:2 * a + 2]], axis=0))
+            ps.append(jnp.exp(s - lse))
+            dra = mh[rows, 128 * a:128 * a + 128]
+            dras.append(
+                jnp.concatenate([jnp.where(low_m, dra, 0.0), jnp.where(low_m, 0.0, dra)], axis=0).astype(BF))
+        dps = [dot_nt(d, vv[a, r, OWN:OWN + T]) for d, (a, r) in zip(dras, jobs)]
+        dss = [(p * (dp_ - dlt)).astype(BF) for p, dp_, dlt in zip(ps, dps, dlts)]
+        dqs = [dot(ds, kk[a, r, OWN:OWN + T]) for ds, (a, r) in zip(dss, jobs)]
+        for (a, r), dq in zip(jobs, dqs):
+            mg_s[a, r, 0] = (jnp.where(low_m, dq[0:MP], dq[MP:2 * MP]) * SCALE).astype(BF)
         go(mg_copies)
+        for (a, r), ds, p, dra in zip(jobs, dss, ps, dras):
+            dkv[a, r, 0] += dot_tn(ds, qm[a, r])
+            dkv[a, r, 1] += dot_tn(p.astype(BF), dra)
+
+    def x_done(k, own):
+        come(along_x(k, own))
+        if own:
+            along_x_sum(k, 3)
+            return
+        for q in range(3):
+            along_x_sum(k, q)
+        go(tensor_second(k))
 
     def order(i):
         return jnp.where(i == 0, 1, jnp.where(i == 1, 0, i))
 
-    @pl.loop(0, NT * R)
+    @pl.loop(0, NT)
     def _(i):
-        a = shard_of(order(lax.div(i, 2)))
-        r = lax.rem(i, 2)
+        a = shard_of(order(i))
 
         @pl.when(is_enc)
         def _():
-            attend_back(a, r, WIN_ENC, True)
+            attend_back(a, WIN_ENC, True)
 
         @pl.when(is_dec)
         def _():
-            attend_back(a, r, WIN_DEC, False)
-
-        @pl.when(r == 1)
-        def _():
-            to_left, to_right = halo_copies(a)
-            to_left.start()
-
-            @pl.when(is_enc)
+            attend_back(a, WIN_DEC, False)
+
+        to_left, to_right = halo_copies(a)
+        to_left.start()
+
+        @pl.when(is_enc)
+        def _():
+            to_right.start()
+
+        @pl.when(is_dec)
+        def _():
+            @pl.when(i == 3)
             def _():
-                to_right.start()
-
-        @pl.when(is_dec)
-        def _():
-            @pl.when(i == 1)
-            def _():
-                for k in (C_CROSS, C_OUT):
-                    all_pairs_sum(k)
-                    go([over_tensor(k, q) for q in range(3)])
+                cross_grads()
+                x_done(C_DOWN, False)
+                x_done(C_DOWN, True)
 
         @pl.when(is_enc)
         def _():
-            @pl.when(i == 1)
+            @pl.when(i == 0)
             def _():
                 mem_back_first()
 
-            @pl.when(i == 5)
+            @pl.when(i == 2)
             def _():
                 mem_back_second()
 
-            @pl.when(i == 6)
+            @pl.when(i == 3)
             def _():
                 mem_back_third()
 
@@ -1118,34 +1127,47 @@
     n3 = [remote(nx.at[chip], nx.at[chip], ns.at[3 + o], nq.at[3 + o], dp=chip_at(o) * 2 + core)
           for o in range(1, chips)]
 
+    def query_grads(q):
+        a = shard_of(q)
+        gw = dot_tn(x_ext[0, OWN:OWN + T], act[0, a, :, 0:128]) + dot_tn(x_ext[1, OWN:OWN + T], act[1, a, :, 0:128])
+        g[q, G_QKV:G_QKV + D] = gw.astype(BF)
+
     def mem_last():
+        mem_attend_back()
         for k in (C_DOWN, C_UP):
             all_pairs_sum(k, (3,))
             go(along_x(k, True))
-        mem_attend_back()
-        all_pairs_sum(C_OUT)
-        go([over_tensor(C_OUT, q) for q in range(3)])
-        all_pairs_sum(C_CROSS, (3,))
-        start, lo, hf = at(C_CROSS)
-        ysum[lo - LATE:lo - LATE + hf] = g[3, pl.ds(own_half(C_CROSS), hf)]
-        go(over_chips(C_CROSS))
+        out_grads()
+        mem_out()
+        chips_on(C_CROSS, (3,))
+        for q in range(NT):
+            query_grads(q)
+        for q in range(3):
+            pair(C_Q, q).start()
+        chips_on(C_OUT, range(NT))
+        chips_on(C_Q, range(3))
+
+    def decoder_last():
+        out_grads()
+        for q in range(NT):
+            query_grads(q)
+            pair(C_Q, q).start()
+        chips_on(C_CROSS, range(NT))
+        chips_on(C_OUT, range(NT))
+        chips_on(C_Q, range(NT))
 
     ny[t] = ng[...]
+    go(n1)
 
     @pl.when(is_dec)
     def _():
-        go(n1)
+        decoder_last()
 
     @pl.when(is_enc)
     def _():
-        go(n1)
         mem_last()
 
     dxm_copy = remote(dxm_s, dxm_r.at[t], gsend.at[0], grecv.at[t], tensor=0)
-
-    def qkv_on(q):
-        all_pairs_sum(C_QKV, (q,))
-        go(chips_first(C_QKV, q))
 
     def mem_own():
         come(mg_copies)
@@ -1162,7 +1184,18 @@
         gw = dot_tn(x_mem(), dm)
         for j in range(3):
             add_g(G_QKV + D * j, gw[:, 128 * j:128 * j + 128])
+        pair(C_Q, 3).start()
+        pair(C_KV, 3).start()
         return dm
+
+    def qkv_full(a):
+        return jnp.concatenate([wqkv[a, j] for j in range(3)], axis=1)
+
+    @pl.when(is_dec)
+    def _():
+        come(tensor_second(C_DOWN))
+        tensor_second_sum(C_DOWN)
+        go(over_z(C_DOWN))
 
     @pl.loop(0, NT)
     def _(i):
@@ -1184,83 +1217,109 @@
                     dkv[a, r, j, 0:HALO] += halo_r[1, a, r, j].astype(F32)
 
                 act[r, a, :, 128 * (j + 1):128 * (j + 2)] = dkv[a, r, j].astype(BF)
-        gw = dot_tn(x_ext[0, OWN:OWN + T], act[0, a, :, 0:384]) + dot_tn(x_ext[1, OWN:OWN + T], act[1, a, :, 0:384])
-        for j in range(3):
-            g[q, G_QKV + D * j:G_QKV + D * j + D] = gw[:, 128 * j:128 * j + 128].astype(BF)
-
-        @pl.when(q < 3)
-        def _():
-            pair(C_QKV, q).start()
-
-        wfull = jnp.concatenate([wqkv[a, j] for j in range(3)], axis=1)
-
-        @pl.when(q == 3)
-        def _():
-            @pl.when(is_enc)
+        gw = (dot_tn(x_ext[0, OWN:OWN + T], act[0, a, :, 128:384])
+              + dot_tn(x_ext[1, OWN:OWN + T], act[1, a, :, 128:384]))
+        for j in range(2):
+            g[q, G_KV + D * j:G_KV + D * j + D] = gw[:, 128 * j:128 * j + 128].astype(BF)
+
+        @pl.when(jnp.logical_or(is_dec, q < 3))
+        def _():
+            pair(C_KV, q).start()
+
+        @pl.when(jnp.logical_and(is_enc, q == 3))
+        def _():
+            dm = mem_own()
+            dxm_s[...] = dot_nt(dm, qkv_full(t)).astype(BF)
+
+            @pl.when(t > 0)
             def _():
-                dm = mem_own()
-                pair(C_QKV, 3).start()
-                dxm_s[...] = dot_nt(dm, wfull).astype(BF)
-
-                @pl.when(t > 0)
-                def _():
-                    dxm_copy.start()
-
-            @pl.when(is_dec)
-            def _():
-                pair(C_QKV, 3).start()
-
-        for r in range(R):
-            d32[r] += dot_nt(act[r, a, :, 0:384], wfull)
+                dxm_copy.start()
 
         @pl.when(i > 0)
         def _():
-            qkv_on(order(i - 1))
-
-    qkv_on(3)
+            q_before = order(i - 1)
+            pair(C_KV, q_before).wait_recv()
+            pair_sum(C_KV, q_before)
+            go(chips_first(C_KV, q_before))
+
+    chips_on(C_KV, (3,))
+
+    @pl.when(is_enc)
+    def _():
+        chips_on(C_Q, (3,))
 
     come(n1)
     nc[0] = ny[0] + ny[1] + ny[2] + ny[3]
     go(n2)
-    for k in (C_DOWN, C_UP):
-        come(along_x(k, False))
-        for q in range(3):
-            along_x_sum(k, q)
-        go(tensor_second(k))
+
+    @pl.when(is_enc)
+    def _():
+        x_done(C_DOWN, False)
+        x_done(C_UP, False)
+
+    @pl.when(is_dec)
+    def _():
+        x_done(C_UP, False)
+        x_done(C_UP, True)
+        chips_done(C_CROSS, range(NT))
+        go(tensor_third(C_CROSS))
+
+    w_qkv_all = jnp.concatenate([qkv_full(a) for a in range(NT)], axis=1)
+    for r in both:
+        d_all = jnp.concatenate([act[r, a, :, 0:384] for a in range(NT)], axis=1)
+        d32[r] += dot_nt(d_all, w_qkv_all)
+
     come(n2)
     nx[chip] = nc[0] + nc[1]
     go(n3)
 
     @pl.when(is_dec)
     def _():
-        come([over_tensor(C_CROSS, q) for q in range(3)])
-        tensor_sum(C_CROSS)
-        go(over_chips(C_CROSS))
-
-    come([over_tensor(C_OUT, q) for q in range(3)])
-    tensor_sum(C_OUT)
-    go(over_chips(C_OUT))
-    for q in range(NT):
-        come(chips_first(C_QKV, q))
-        chips_first_sum(C_QKV, q)
-    go(tensor_third(C_QKV))
-    for k in (C_DOWN, C_UP):
-        come(along_x(k, True))
-        along_x_sum(k, 3)
-        come(tensor_second(k))
-        tensor_second_sum(k)
-        go(over_z(k))
-    come(tensor_third(C_QKV))
-    tensor_third_sum(C_QKV)
-    go(spread(C_QKV))
-    for k in (C_CROSS, C_OUT):
-        come(over_chips(k))
-        chips_sum(k)
+        come(over_z(C_DOWN))
+        over_z_sum(C_DOWN)
+        go(spread_x(C_DOWN))
+
+    @pl.when(is_enc)
+    def _():
+        x_done(C_DOWN, True)
+        x_done(C_UP, True)
+        chips_done(C_CROSS, (3,))
+        tensor_third_sum(C_CROSS, True)
+        go(spread(C_CROSS))
+
+    for k in (C_OUT, C_Q, C_KV):
+        chips_done(k, range(NT))
+        go(tensor_third(k))
+
+    @pl.when(is_enc)
+    def _():
+        come(tensor_second(C_DOWN))
+        tensor_second_sum(C_DOWN)
+        go(over_z(C_DOWN))
+
+    @pl.when(is_dec)
+    def _():
+        come(tensor_third(C_CROSS))
+        tensor_third_sum(C_CROSS)
+        go(spread(C_CROSS))
+
+    come(tensor_second(C_UP))
+    tensor_second_sum(C_UP)
+    go(over_z(C_UP))
+    for k in (C_OUT, C_Q, C_KV):
+        come(tensor_third(k))
+        tensor_third_sum(k)
         go(spread(k))
-    for k in (C_DOWN, C_UP):
-        come(over_z(k))
-        over_z_sum(k)
-        go(spread_x(k))
+
+    @pl.when(is_enc)
+    def _():
+        come(over_z(C_DOWN))
+        over_z_sum(C_DOWN)
+        go(spread_x(C_DOWN))
+
+    come(over_z(C_UP))
+    over_z_sum(C_UP)
+    go(spread_x(C_UP))
 
     @pl.when(jnp.logical_and(is_enc, t == 0))
     def _():
@@ -1278,23 +1337,23 @@
     for o in range(1, chips):
         tot_n = tot_n + nx[o]
     ng_tot[...] = tot_n
-    for k in (C_CROSS, C_OUT):
+    come(spread(C_CROSS))
+    go(hand(C_CROSS))
+    come(spread_x(C_DOWN))
+    go(hand(C_DOWN))
+    for k in (C_OUT, C_Q, C_KV):
         come(spread(k))
         go(hand(k))
-    for k in (C_DOWN, C_UP):
-        come(spread_x(k))
-        go(hand(k))
-    come(spread(C_QKV))
-    go(hand(C_QKV))
-    for k in range(5):
+    come(spread_x(C_UP))
+    go(hand(C_UP))
+    for k in range(CN):
         come(hand(k))
 
     y_copy.wait()
     dx_copy.wait()
-    for i in (QKV, OUT):
-        gone(w_direct(i))
-        gone(w_pair(i))
-    for i in (UP, DOWN):
+    gone(w_direct(OUT))
+    gone(w_pair(OUT))
+    for i in (QKV, UP, DOWN):
         gone(w_eighth(i))
         gone(w_along(i))
         gone(w_pair(i))
@@ -1304,25 +1363,22 @@
     gone(n1)
     gone(n2)
     gone(n3)
-    for k in range(5):
+    for k in range(CN):
         if k in (C_DOWN, C_UP):
             gone(along_x(k, False))
             gone(along_x(k, True))
             gone(tensor_second(k))
             gone(over_z(k))
             gone(spread_x(k))
-        elif k == C_QKV:
+        else:
+            gone(spread(k))
+        if k in (C_OUT, C_Q, C_KV):
             for q in range(NT):
                 gone(chips_first(k, q))
             gone(tensor_third(k))
-            gone(spread(k))
-        else:
-            gone(over_chips(k))
-            gone(spread(k))
         if k != C_CROSS:
             gone([pair(k, q) for q in range(NT)])
         gone(hand(k))
-    gone([over_tensor(C_OUT, q) for q in range(3)])
 
     @pl.when(is_dec)
     def _():
@@ -1330,12 +1386,15 @@
         gone(w_pair(CROSS))
         gone(dkv_copies)
         gone([pair(C_CROSS, q) for q in range(NT)])
-        gone([over_tensor(C_CROSS, q) for q in range(3)])
+        for q in range(NT):
+            gone(chips_first(C_CROSS, q))
+        gone(tensor_third(C_CROSS))
 
     @pl.when(is_enc)
     def _():
         x_left.wait_send()
         pair(C_CROSS, 3).wait_send()
+        gone(chips_first(C_CROSS, 3))
         for a in range(NT):
             halo_copies(a)[1].wait_send()
         for e in range(4):
@@ -1356,7 +1415,6 @@
 def layer_call(chips, lens, x, cot, wqkv, wout, wcross, wup, wdown, gain, bias):
     any_ = pl.BlockSpec(memory_space=pl.ANY)
     vmem = pl.BlockSpec(memory_space=pltpu.VMEM)
-    M = R * MP
     W = W_ENC
     S = pltpu.SemaphoreType.DMA
     C = len(CHUNKS)
@@ -1385,18 +1443,18 @@
         kblk=V((R, 256, D), BF), vblk=V((R, 256, D), BF), cpt=V((R, 256, T), BF), cq=V((R, T, D), BF),
         cctx=V((R, T, D), BF), cdb=V((R, T, D), BF),
         mx1=V((M, D), F32), mx2=V((M, D), F32), mx3=V((M, D), F32), mr1=V((M, 1), F32), mr2=V((M, 1), F32),
-        mr3=V((M, 1), F32), mh=V((M, D), F32), mact=V((M, D), BF), mgp=V((NT, M, D), F32), mc=V((M, D), F32),
-        mm=V((M, D), BF), mst=V((2, M, 128), F32), md=V((M, D), F32),
-        g=V((NT, G_ROWS, 128), BF), r1=V((NT, HALF, 128), BF), r2=V((3, late, 128), BF),
-        r3=V((o, late // chips, 128), BF), rx=V((3, NT, LATE // 4, 128), BF), ry_s=V((NT, LATE // 4, 128), BF),
+        mr3=V((M, 1), F32), mh=V((M, D), F32), mact=V((M, D), BF), mc=V((M, D), F32),
+        mm=V((M, D), BF), mst=V((2, M, 128), F32), md=V((M, D), F32), dmb=V((M, D), BF),
+        g=V((NT, G_ROWS, 128), BF), r1=V((NT, HALF, 128), BF),
+        rx=V((3, NT, LATE // 4, 128), BF), ry_s=V((NT, LATE // 4, 128), BF),
         ry_r=V((3, LATE // 4, 128), BF), zz=V((2, LATE // 4, 128), BF),
-        rq=V((o, NT, 768 // chips, 128), BF), rqs=V((NT, 768 // chips, 128), BF), rqr=V((3, 768 // chips, 128), BF),
-        ysum=V((late, 128), BF), ng=V((8, D), F32), ny=V((NT, 8, D), F32), nc=V((2, 8, D), F32),
+        rq=V((o, NT, late // chips, 128), BF), rqs=V((NT, late // chips, 128), BF), rqr=V((3, late // chips, 128), BF),
+        ng=V((8, D), F32), ny=V((NT, 8, D), F32), nc=V((2, 8, D), F32),
         nx=V((chips, 8, D), F32),
-        lsem=S((11,)), wsend=S((5, 6)), wrecv=S((5, 6)), w2send=S((2, 3, 3)), w2recv=S((2, 3, 3)), xsend=S((2,)), xrecv=S((2,)), msend=S((2, 3)), mrecv=S((2,)),
+        lsem=S((11,)), wsend=S((5, 6)), wrecv=S((5, 6)), w2send=S((3, 3, 3)), w2recv=S((3, 3, 3)), xsend=S((2,)), xrecv=S((2,)), msend=S((2, 3)), mrecv=S((2,)),
         esend=S((5, 3)), erecv=S((5, 3)), ksend=S((NT,)), krecv=S((NT,)), dsend=S((NT,)), drecv=S((NT,)),
-        hsend=S((2, NT)), hrecv=S((2, NT)), gsend=S((1,)), grecv=S((NT,)), qsend=S((3,)), qrecv=S((3,)), sq=S((NT, o)), qq=S((NT, o)),
-        s1=S((C, NT)), q1=S((C, NT)), s2=S((C, 3)), q2=S((C, 3)), s3=S((C, o)), q3=S((C, o)),
+        hsend=S((2, NT)), hrecv=S((2, NT)), gsend=S((1,)), grecv=S((NT,)), qsend=S((3,)), qrecv=S((3,)), sq=S((C, NT, o)), qq=S((C, NT, o)),
+        s1=S((C, NT)), q1=S((C, NT)), s2=S((C, 3)), q2=S((C, 3)),
         s4=S((C, o)), q4=S((C, o)), s5=S((C,)), q5=S((C,)), ns=S((4 + o,)), nq=S((4 + o,)),
         sx=S((2, 2, 3)), qx=S((2, 2, 3)), sz=S((2,)), qz=S((2,)),
     )

time: 143 us -> 130 us (0.909)
  the two profiles are of different devices: /device:TPU:33 before, /device:TPU:1 now
where the time goes in v4:
time: 130 us; the launch traced here: 129 us
  Pallas kernels  129 us (99%)
    pallas_call x1, Pallas kernels, layer_call(): pl.pallas_call(kernel, out_shape=(jax.ShapeDtypeStruct((R, T, D), F32), j...  123 us
    pallas_call x1, Pallas kernels, finish_call(): pl.pallas_call(finish_kernel, out_shape=tuple((jax.ShapeDtypeStruct(s, F3...  5.32 us

profile of v4, /device:TPU:1, one launch (start us, length us, event | category | flops | bytes accessed | tf_op | source)
XLA Modules:
  0.0 129.5 jit_solution(5802474649482011739)
XLA Ops:
  0.6 123.3 %layers.1 = (f32[2,256,512]{2,1,0:T(8,128)}, f32[2,256,512]{2,1,0:T(8,128)}, bf16[7168,128]{1,0:T(8,128)(2,1)}, f32[8,512]{1,0:T(8,128)}) custom-call(s32[2,16]{1,0:T(2,128)} %refs_0_.1, bf16[2,256,512]{2,1,0:T(8,128)(2,1)} %bitcast.12, f32[2,256,512]{2,1,0:T(8,128)} %bitcast.11, bf16[3,512,128]{2,1,0:T(8,128)(2,1)} %bitcast.15, bf16[128,512]{1,0:T(8,128)(2,1)} %bitcast.17, ...), custom_call_target="tpu_custom_call" | custom-call | tf_op jit(solution)/shard_map/layers/pallas_call | solution.py:1466
  124.0 5.3 %finish.1 = (f32[1,2,256,512]{3,2,1,0:T(8,128)}, f32[1,2,256,512]{3,2,1,0:T(8,128)}, f32[1,3,512,128]{3,2,1,0:T(8,128)}, f32[1,128,512]{2,1,0:T(8,128)}, f32[1,2...) custom-call(f32[2,256,512]{2,1,0:T(8,128)} %get-tuple-element.22.y_i, ...), custom_call_target="tpu_custom_call" | custom-call | tf_op jit(solution)/shard_map/finish/pallas_call | solution.py:1509

commit v5 on v4

--- a/solution.py
+++ b/solution.py
@@ -32,6 +32,7 @@
 CN = len(CHUNKS)
 C_DOWN, C_UP, C_CROSS, C_OUT, C_Q, C_KV = range(CN)
 LATE = G_CROSS // 2
+LAST = G_OUT // 2
 HALF = G_ROWS // 2
 QKV, OUT, CROSS, UP, DOWN = range(5)
 ALONG = {QKV: 0, UP: 1, DOWN: 2}
@@ -89,8 +90,8 @@
         m[n] for n in ("xh1", "xh2", "rs1", "rs2", "h32", "hb", "h1b", "act", "gp", "dab", "dr"))
     dkv, halo_s, halo_r, mg_s, mg_r, dxm_s, dxm_r, mdu = (
         m[n] for n in ("dkv", "halo_s", "halo_r", "mg_s", "mg_r", "dxm_s", "dxm_r", "mdu"))
-    ex_o, ex_st, ex_f, ex_m, qm, rq, rqs, rqr = (
-        m[n] for n in ("ex_o", "ex_st", "ex_f", "ex_m", "qm", "rq", "rqs", "rqr"))
+    ex_o, ex_st, ex_f, ex_m, qm, rq, rqs, rqr, r2, r3, ysum = (
+        m[n] for n in ("ex_o", "ex_st", "ex_f", "ex_m", "qm", "rq", "rqs", "rqr", "r2", "r3", "ysum"))
     kvm, dkvm_s, dkvm_r, kblk, vblk, cpt, cq, cctx = (
         m[n] for n in ("kvm", "dkvm_s", "dkvm_r", "kblk", "vblk", "cpt", "cq", "cctx"))
     mx1, mx2, mx3, mr1, mr2, mr3, mh, mact, mc, mm, mst, md = (
@@ -103,8 +104,8 @@
                        "krecv", "dsend", "drecv", "hsend", "hrecv", "gsend", "grecv", "qsend", "qrecv"))
     s1, q1, s2, q2, s4, q4, s5, q5, ns, nq = (
         m[n] for n in ("s1", "q1", "s2", "q2", "s4", "q4", "s5", "q5", "ns", "nq"))
-    w2send, w2recv, sx, qx, sz, qz, sq, qq = (
-        m[n] for n in ("w2send", "w2recv", "sx", "qx", "sz", "qz", "sq", "qq"))
+    w2send, w2recv, sx, qx, sz, qz, sq, qq, s3, q3 = (
+        m[n] for n in ("w2send", "w2recv", "sx", "qx", "sz", "qz", "sq", "qq", "s3", "q3"))
 
     def g_row(i):
         return gain[i]
@@ -698,48 +699,91 @@
         rows = pl.ds(own_half(k), hf)
         g[q, rows] = (g[q, rows].astype(F32) + r1[q, lo:lo + hf].astype(F32)).astype(BF)
 
-    def chips_first(k, q):
+    def x_row(k):
+        return 0 if k == C_CROSS else 512 // chips
+
+    def chips_first(k, q, some=1):
         start, lo, hf = at(k)
         n = hf // chips
         out = []
         for off in range(1, chips):
             to = chip_at(off)
-            out.append(remote(g.at[q, pl.ds(own_half(k) + to * n, n), :],
-                              rq.at[off - 1, q, pl.ds((lo - LATE) // chips, n), :],
+            out.append(remote(g.at[pl.ds(q, some), pl.ds(own_half(k) + to * n, n), :],
+                              rq.at[off - 1, pl.ds(q, some), pl.ds(x_row(k), n), :],
                               sq.at[k, q, off - 1], qq.at[k, q, off - 1], dp=to * 2 + core))
         return out
 
-    def chips_on(k, some):
-        all_pairs_sum(k, some)
-        for q in some:
-            go(chips_first(k, q))
-
-    def chips_done(k, some):
+    def chips_on(k, q, some):
+        all_pairs_sum(k, range(q, q + some))
+        go(chips_first(k, q, some))
+
+    def chips_done(k, groups):
         start, lo, hf = at(k)
         n = hf // chips
-        base = (lo - LATE) // chips
-        for q in some:
-            come(chips_first(k, q))
-            tot = g[q, pl.ds(own_half(k) + chip * n, n)].astype(F32)
-            for o in range(chips - 1):
-                tot = tot + rq[o, q, base:base + n].astype(F32)
-            rqs[q, base:base + n] = tot.astype(BF)
+        base = x_row(k)
+        for first_q, some in groups:
+            come(chips_first(k, first_q, some))
+            for q in range(first_q, first_q + some):
+                tot = g[q, pl.ds(own_half(k) + chip * n, n)].astype(F32)
+                for o in range(chips - 1):
+                    tot = tot + rq[o, q, base:base + n].astype(F32)
+                rqs[q, base:base + n] = tot.astype(BF)
 
     def tensor_third(k):
         start, lo, hf = at(k)
-        rows = pl.ds((lo - LATE) // chips, hf // chips)
+        rows = pl.ds(x_row(k), hf // chips)
         return [remote(rqs.at[q, rows, :], rqr.at[q, rows, :], s2.at[k, q], q2.at[k, q], tensor=shard_of(q))
                 for q in range(3)]
 
     def tensor_third_sum(k, only_own=False):
         start, lo, hf = at(k)
         n = hf // chips
-        base = (lo - LATE) // chips
+        base = x_row(k)
         tot = rqs[3, base:base + n].astype(F32)
         if not only_own:
             for q in range(3):
                 tot = tot + rqr[q, base:base + n].astype(F32)
         full[pl.ds(own_half(k) + chip * n, n)] = tot.astype(BF)
+
+    def over_tensor(k, q):
+        start, lo, hf = at(k)
+        return remote(g.at[q, pl.ds(own_half(k), hf), :], r2.at[q, pl.ds(lo - LAST, hf), :],
+                      s2.at[k, q], q2.at[k, q], tensor=shard_of(q))
+
+    def tensor_on(k, some):
+        all_pairs_sum(k, some)
+        go([over_tensor(k, q) for q in some if q < 3])
+
+    def tensor_sum(k, only_own=False):
+        start, lo, hf = at(k)
+        tot = g[3, pl.ds(own_half(k), hf)].astype(F32)
+        if not only_own:
+            come([over_tensor(k, q) for q in range(3)])
+            for q in range(3):
+                tot = tot + r2[q, lo - LAST:lo - LAST + hf].astype(F32)
+        ysum[lo - LAST:lo - LAST + hf] = tot.astype(BF)
+        go(over_chips(k))
+
+    def over_chips(k):
+        start, lo, hf = at(k)
+        n = hf // chips
+        out = []
+        for off in range(1, chips):
+            to = chip_at(off)
+            out.append(remote(ysum.at[pl.ds(lo - LAST + to * n, n), :],
+                              r3.at[off - 1, pl.ds((lo - LAST) // chips, n), :],
+                              s3.at[k, off - 1], q3.at[k, off - 1], dp=to * 2 + core))
+        return out
+
+    def chips_sum(k):
+        start, lo, hf = at(k)
+        n = hf // chips
+        come(over_chips(k))
+        tot = ysum[pl.ds(lo - LAST + chip * n, n)].astype(F32)
+        for o in range(chips - 1):
+            tot = tot + r3[o, (lo - LAST) // chips:(lo - LAST) // chips + n].astype(F32)
+        full[pl.ds(own_half(k) + chip * n, n)] = tot.astype(BF)
+        go(spread(k))
 
     quarter = LATE // 8
 
@@ -1105,8 +1149,6 @@
             @pl.when(i == 3)
             def _():
                 cross_grads()
-                x_done(C_DOWN, False)
-                x_done(C_DOWN, True)
 
         @pl.when(is_enc)
         def _():
@@ -1139,22 +1181,25 @@
             go(along_x(k, True))
         out_grads()
         mem_out()
-        chips_on(C_CROSS, (3,))
+        chips_on(C_CROSS, 3, 1)
         for q in range(NT):
             query_grads(q)
         for q in range(3):
             pair(C_Q, q).start()
-        chips_on(C_OUT, range(NT))
-        chips_on(C_Q, range(3))
+        tensor_on(C_Q, range(3))
+        tensor_on(C_OUT, range(NT))
+        x_done(C_DOWN, False)
 
     def decoder_last():
         out_grads()
         for q in range(NT):
             query_grads(q)
             pair(C_Q, q).start()
-        chips_on(C_CROSS, range(NT))
-        chips_on(C_OUT, range(NT))
-        chips_on(C_Q, range(NT))
+        tensor_on(C_Q, range(NT))
+        chips_on(C_CROSS, 0, NT)
+        tensor_on(C_OUT, range(NT))
+        x_done(C_DOWN, False)
+        x_done(C_DOWN, True)
 
     ny[t] = ng[...]
     go(n1)
@@ -1191,12 +1236,6 @@
     def qkv_full(a):
         return jnp.concatenate([wqkv[a, j] for j in range(3)], axis=1)
 
-    @pl.when(is_dec)
-    def _():
-        come(tensor_second(C_DOWN))
-        tensor_second_sum(C_DOWN)
-        go(over_z(C_DOWN))
-
     @pl.loop(0, NT)
     def _(i):
         q = order(i)
@@ -1231,38 +1270,92 @@
             dm = mem_own()
             dxm_s[...] = dot_nt(dm, qkv_full(t)).astype(BF)
 
-            @pl.when(t > 0)
-            def _():
-                dxm_copy.start()
-
         @pl.when(i > 0)
         def _():
             q_before = order(i - 1)
             pair(C_KV, q_before).wait_recv()
             pair_sum(C_KV, q_before)
-            go(chips_first(C_KV, q_before))
-
-    chips_on(C_KV, (3,))
+
+            @pl.when(i == 2)
+            def _():
+                go(chips_first(C_KV, 0, 2))
+
+    all_pairs_sum(C_KV, (3,))
+    go(chips_first(C_KV, 2, 2))
 
     @pl.when(is_enc)
     def _():
-        chips_on(C_Q, (3,))
+        all_pairs_sum(C_Q, (3,))
+
+    for i in (QKV, UP, DOWN):
+        gone(w_eighth(i))
+        gone(w_along(i))
+        gone(w_pair(i))
+    gone(w_direct(OUT))
+    gone(w_pair(OUT))
+    x_right.wait_send()
+    y_copy.wait()
+
+    @pl.when(is_dec)
+    def _():
+        gone(w_direct(CROSS))
+        gone(w_pair(CROSS))
+        gone(dkv_copies)
+
+    @pl.when(is_enc)
+    def _():
+        x_left.wait_send()
+        for e in range(4):
+            gone(exchanges[e])
+        gone(kv_copies)
+        gone(mg_copies)
+
+        @pl.when(t == 0)
+        def _():
+            gone(mem_x)
+            gone(mem_c)
+
+    @pl.when(is_dec)
+    def _():
+        x_done(C_UP, False)
+        x_done(C_UP, True)
+
+    @pl.when(is_enc)
+    def _():
+        x_done(C_UP, False)
+        for k in (C_DOWN, C_UP):
+            x_done(k, True)
 
     come(n1)
     nc[0] = ny[0] + ny[1] + ny[2] + ny[3]
     go(n2)
 
+    @pl.when(is_dec)
+    def _():
+        chips_done(C_CROSS, ((0, NT),))
+        go(tensor_third(C_CROSS))
+
     @pl.when(is_enc)
     def _():
-        x_done(C_DOWN, False)
-        x_done(C_UP, False)
-
-    @pl.when(is_dec)
-    def _():
-        x_done(C_UP, False)
-        x_done(C_UP, True)
-        chips_done(C_CROSS, range(NT))
-        go(tensor_third(C_CROSS))
+        chips_done(C_CROSS, ((3, 1),))
+        tensor_third_sum(C_CROSS, True)
+        go(spread(C_CROSS))
+
+    tensor_sum(C_OUT)
+    tensor_sum(C_Q)
+    come(tensor_second(C_DOWN))
+    tensor_second_sum(C_DOWN)
+    go(over_z(C_DOWN))
+    chips_done(C_KV, ((0, 2), (2, 2)))
+    go(tensor_third(C_KV))
+
+    @pl.when(jnp.logical_and(is_enc, t > 0))
+    def _():
+        dxm_copy.start()
+
+    come(tensor_second(C_UP))
+    tensor_second_sum(C_UP)
+    go(over_z(C_UP))
 
     w_qkv_all = jnp.concatenate([qkv_full(a) for a in range(NT)], axis=1)
     for r in both:
@@ -1275,63 +1368,47 @@
 
     @pl.when(is_dec)
     def _():
-        come(over_z(C_DOWN))
-        over_z_sum(C_DOWN)
-        go(spread_x(C_DOWN))
-
-    @pl.when(is_enc)
-    def _():
-        x_done(C_DOWN, True)
-        x_done(C_UP, True)
-        chips_done(C_CROSS, (3,))
-        tensor_third_sum(C_CROSS, True)
-        go(spread(C_CROSS))
-
-    for k in (C_OUT, C_Q, C_KV):
-        chips_done(k, range(NT))
-        go(tensor_third(k))
-
-    @pl.when(is_enc)
-    def _():
-        come(tensor_second(C_DOWN))
-        tensor_second_sum(C_DOWN)
-        go(over_z(C_DOWN))
-
-    @pl.when(is_dec)
-    def _():
         come(tensor_third(C_CROSS))
         tensor_third_sum(C_CROSS)
         go(spread(C_CROSS))
 
-    come(tensor_second(C_UP))
-    tensor_second_sum(C_UP)
-    go(over_z(C_UP))
-    for k in (C_OUT, C_Q, C_KV):
-        come(tensor_third(k))
-        tensor_third_sum(k)
-        go(spread(k))
-
-    @pl.when(is_enc)
-    def _():
-        come(over_z(C_DOWN))
-        over_z_sum(C_DOWN)
-        go(spread_x(C_DOWN))
-
+    chips_sum(C_OUT)
+    chips_sum(C_Q)
+    come(over_z(C_DOWN))
+    over_z_sum(C_DOWN)
+    go(spread_x(C_DOWN))
+    come(tensor_third(C_KV))
+    tensor_third_sum(C_KV)
+    go(spread(C_KV))
     come(over_z(C_UP))
     over_z_sum(C_UP)
     go(spread_x(C_UP))
-
-    @pl.when(jnp.logical_and(is_enc, t == 0))
-    def _():
-        tot = md[...] + dxm_s[...].astype(F32)
-        for s in range(1, NT):
-            remote(dxm_s, dxm_r.at[s], gsend.at[0], grecv.at[s], tensor=0).wait_recv()
-            tot = tot + dxm_r[s].astype(F32)
-        for r in range(R):
-            d32[r, 0:MP] += tot[r * MP:r * MP + MP]
-
-    dx_copy = pltpu.make_async_copy(d32, dx_out, lsem.at[10])
-    dx_copy.start()
+    for a in range(NT):
+        halo_copies(a)[0].wait_send()
+    for k in range(CN):
+        if k in (C_DOWN, C_UP):
+            gone(along_x(k, False))
+            gone(along_x(k, True))
+            gone(tensor_second(k))
+        if k != C_CROSS:
+            gone([pair(k, q) for q in range(NT)])
+    gone(n1)
+    gone(n2)
+    gone(chips_first(C_KV, 0, 2))
+    gone(chips_first(C_KV, 2, 2))
+
+    @pl.when(is_dec)
+    def _():
+        gone([pair(C_CROSS, q) for q in range(NT)])
+        gone(chips_first(C_CROSS, 0, NT))
+
+    @pl.when(is_enc)
+    def _():
+        pair(C_CROSS, 3).wait_send()
+        for a in range(NT):
+            halo_copies(a)[1].wait_send()
+        gone(chips_first(C_CROSS, 3))
+
     come(n3)
     tot_n = nx[0]
     for o in range(1, chips):
@@ -1346,70 +1423,42 @@
         go(hand(k))
     come(spread_x(C_UP))
     go(hand(C_UP))
+    @pl.when(jnp.logical_and(is_enc, t == 0))
+    def _():
+        tot = md[...] + dxm_s[...].astype(F32)
+        for s in range(1, NT):
+            remote(dxm_s, dxm_r.at[s], gsend.at[0], grecv.at[s], tensor=0).wait_recv()
+            tot = tot + dxm_r[s].astype(F32)
+        for r in range(R):
+            d32[r, 0:MP] += tot[r * MP:r * MP + MP]
+
+    dx_copy = pltpu.make_async_copy(d32, dx_out, lsem.at[10])
+    dx_copy.start()
     for k in range(CN):
         come(hand(k))
 
-    y_copy.wait()
     dx_copy.wait()
-    gone(w_direct(OUT))
-    gone(w_pair(OUT))
-    for i in (QKV, UP, DOWN):
-        gone(w_eighth(i))
-        gone(w_along(i))
-        gone(w_pair(i))
-    x_right.wait_send()
-    for a in range(NT):
-        halo_copies(a)[0].wait_send()
-    gone(n1)
-    gone(n2)
     gone(n3)
     for k in range(CN):
         if k in (C_DOWN, C_UP):
-            gone(along_x(k, False))
-            gone(along_x(k, True))
-            gone(tensor_second(k))
             gone(over_z(k))
             gone(spread_x(k))
         else:
             gone(spread(k))
-        if k in (C_OUT, C_Q, C_KV):
-            for q in range(NT):
-                gone(chips_first(k, q))
+        if k in (C_Q, C_OUT):
+            gone([over_tensor(k, q) for q in range(3)])
+            gone(over_chips(k))
+        if k == C_KV:
             gone(tensor_third(k))
-        if k != C_CROSS:
-            gone([pair(k, q) for q in range(NT)])
         gone(hand(k))
 
     @pl.when(is_dec)
     def _():
-        gone(w_direct(CROSS))
-        gone(w_pair(CROSS))
-        gone(dkv_copies)
-        gone([pair(C_CROSS, q) for q in range(NT)])
-        for q in range(NT):
-            gone(chips_first(C_CROSS, q))
         gone(tensor_third(C_CROSS))
 
-    @pl.when(is_enc)
-    def _():
-        x_left.wait_send()
-        pair(C_CROSS, 3).wait_send()
-        gone(chips_first(C_CROSS, 3))
-        for a in range(NT):
-            halo_copies(a)[1].wait_send()
-        for e in range(4):
-            gone(exchanges[e])
-        gone(mg_copies)
-        gone(kv_copies)
-
-        @pl.when(t == 0)
-        def _():
-            gone(mem_x)
-            gone(mem_c)
-
-        @pl.when(t > 0)
-        def _():
-            dxm_copy.wait_send()
+    @pl.when(jnp.logical_and(is_enc, t > 0))
+    def _():
+        dxm_copy.wait_send()
 
 
 def layer_call(chips, lens, x, cot, wqkv, wout, wcross, wup, wdown, gain, bias):
@@ -1419,7 +1468,8 @@
     S = pltpu.SemaphoreType.DMA
     C = len(CHUNKS)
     o = max(chips - 1, 1)
-    late = HALF - LATE
+    late = G_KV // 2 - LAST
+    mid = 1024
 
     def V(shape, kind):
         return pltpu.VMEM(shape, kind)
@@ -1448,12 +1498,13 @@
         g=V((NT, G_ROWS, 128), BF), r1=V((NT, HALF, 128), BF),
         rx=V((3, NT, LATE // 4, 128), BF), ry_s=V((NT, LATE // 4, 128), BF),
         ry_r=V((3, LATE // 4, 128), BF), zz=V((2, LATE // 4, 128), BF),
-        rq=V((o, NT, late // chips, 128), BF), rqs=V((NT, late // chips, 128), BF), rqr=V((3, late // chips, 128), BF),
+        rq=V((o, NT, mid // chips, 128), BF), rqs=V((NT, mid // chips, 128), BF), rqr=V((3, mid // chips, 128), BF),
+        r2=V((3, late, 128), BF), r3=V((o, late // chips, 128), BF), ysum=V((late, 128), BF),
         ng=V((8, D), F32), ny=V((NT, 8, D), F32), nc=V((2, 8, D), F32),
         nx=V((chips, 8, D), F32),
         lsem=S((11,)), wsend=S((5, 6)), wrecv=S((5, 6)), w2send=S((3, 3, 3)), w2recv=S((3, 3, 3)), xsend=S((2,)), xrecv=S((2,)), msend=S((2, 3)), mrecv=S((2,)),
         esend=S((5, 3)), erecv=S((5, 3)), ksend=S((NT,)), krecv=S((NT,)), dsend=S((NT,)), drecv=S((NT,)),
-        hsend=S((2, NT)), hrecv=S((2, NT)), gsend=S((1,)), grecv=S((NT,)), qsend=S((3,)), qrecv=S((3,)), sq=S((C, NT, o)), qq=S((C, NT, o)),
+        hsend=S((2, NT)), hrecv=S((2, NT)), gsend=S((1,)), grecv=S((NT,)), qsend=S((3,)), qrecv=S((3,)), sq=S((C, NT, o)), qq=S((C, NT, o)), s3=S((C, o)), q3=S((C, o)),
         s1=S((C, NT)), q1=S((C, NT)), s2=S((C, 3)), q2=S((C, 3)),
         s4=S((C, o)), q4=S((C, o)), s5=S((C,)), q5=S((C,)), ns=S((4 + o,)), nq=S((4 + o,)),
         sx=S((2, 2, 3)), qx=S((2, 2, 3)), sz=S((2,)), qz=S((2,)),
@@ -1481,23 +1532,45 @@
     )(lens, x, cot, wqkv, wout, wcross, wup, wdown, gain, bias)
 
 
-def finish_kernel(y_in, dx_in, full, ng, y, dx, o_qkv, o_out, o_cross, o_up, o_down, o_gain, o_bias, sems):
-    copies = [pltpu.make_async_copy(y_in, y.at[0], sems.at[0]), pltpu.make_async_copy(dx_in, dx.at[0], sems.at[1])]
-    for c in copies:
+def finish_kernel(y_in, dx_in, full_in, ng, y, dx, o_qkv, o_out, o_cross, o_up, o_down, o_gain, o_bias,
+                  b_y, b_dx, full, b_qkv, b_out, b_cross, b_up, b_down, s_in, s_out):
+    parts = ((G_DOWN, G_UP), (G_UP, G_CROSS), (G_CROSS, G_ROWS))
+    loads = [pltpu.make_async_copy(full_in.at[pl.ds(lo, hi - lo), :], full.at[pl.ds(lo, hi - lo), :], s_in.at[i])
+             for i, (lo, hi) in enumerate(parts)]
+    loads.append(pltpu.make_async_copy(y_in, b_y, s_in.at[3]))
+    loads.append(pltpu.make_async_copy(dx_in, b_dx, s_in.at[4]))
+    for c in loads:
         c.start()
-    for j in range(3):
-        o_qkv[0, j] = full[G_QKV + D * j:G_QKV + D * j + D].astype(F32)
-    for j in range(2):
-        o_cross[0, j] = full[G_CROSS + D * j:G_CROSS + D * j + D].astype(F32)
-    for j in range(4):
-        cols = slice(128 * j, 128 * j + 128)
-        o_out[0, :, cols] = full[G_OUT + 128 * j:G_OUT + 128 * j + 128].astype(F32)
-        o_up[0, :, cols] = full[G_UP + D * j:G_UP + D * j + D].astype(F32)
-        o_down[0, :, cols] = full[G_DOWN + D * j:G_DOWN + D * j + D].astype(F32)
     for i in range(3):
         o_gain[i] = ng[i:i + 1]
         o_bias[i] = ng[i + 3:i + 4]
-    for c in copies:
+    stores = []
+
+    def store(src, dst):
+        c = pltpu.make_async_copy(src, dst.at[0], s_out.at[len(stores)])
+        c.start()
+        stores.append(c)
+
+    for i, (base, buf, out) in enumerate(((G_DOWN, b_down, o_down), (G_UP, b_up, o_up))):
+        loads[i].wait()
+        for j in range(4):
+            buf[:, 128 * j:128 * j + 128] = full[base + D * j:base + D * j + D].astype(F32)
+        store(buf, out)
+    loads[3].wait()
+    store(b_y, y)
+    loads[4].wait()
+    store(b_dx, dx)
+    loads[2].wait()
+    for j in range(3):
+        b_qkv[j] = full[G_QKV + D * j:G_QKV + D * j + D].astype(F32)
+    store(b_qkv, o_qkv)
+    for j in range(2):
+        b_cross[j] = full[G_CROSS + D * j:G_CROSS + D * j + D].astype(F32)
+    store(b_cross, o_cross)
+    for j in range(4):
+        b_out[:, 128 * j:128 * j + 128] = full[G_OUT + 128 * j:G_OUT + 128 * j + 128].astype(F32)
+    store(b_out, o_out)
+    for c in stores:
         c.wait()
 
 
@@ -1509,9 +1582,11 @@
     return pl.pallas_call(
         finish_kernel,
         out_shape=tuple(jax.ShapeDtypeStruct(s, F32) for s in shapes),
-        in_specs=[vmem] * 4,
-        out_specs=(any_, any_) + (vmem,) * 7,
-        scratch_shapes=[pltpu.SemaphoreType.DMA((2,))],
+        in_specs=[any_] * 3 + [vmem],
+        out_specs=(any_,) * 7 + (vmem,) * 2,
+        scratch_shapes=[pltpu.VMEM((R, T, D), F32)] * 2 + [pltpu.VMEM((G_ROWS, 128), BF)]
+        + [pltpu.VMEM(s[1:], F32) for s in shapes[2:7]]
+        + [pltpu.SemaphoreType.DMA((5,)), pltpu.SemaphoreType.DMA((7,))],
         compiler_params=pltpu.CompilerParams(vmem_limit_bytes=VMEM_BYTES),
         name="finish",
     )(y, dx, full, ng)

time: 130 us -> 127 us (0.977)
  Pallas kernels: 129 us -> 126 us
    pallas_call x1, Pallas kernels: 123 us -> 121 us  [layer_call(): pl.pallas_call(kernel, out_shape=(jax.ShapeDtypeStruct((R, T, D), F32), j...]
where the time goes in v5:
time: 127 us; the launch traced here: 126 us
  Pallas kernels  126 us (99%)
    pallas_call x1, Pallas kernels, layer_call(): pl.pallas_call(kernel, out_shape=(jax.ShapeDtypeStruct((R, T, D), F32), j...  121 us
    pallas_call x1, Pallas kernels, finish_call(): pl.pallas_call(finish_kernel, out_shape=tuple((jax.ShapeDtypeStruct(s, F3...  5.07 us

profile of v5, /device:TPU:1, one launch (start us, length us, event | category | flops | bytes accessed | tf_op | source)
XLA Modules:
  0.0 126.4 jit_solution(3909026911273981968)
XLA Ops:
  0.6 120.5 %layers.1 = (f32[2,256,512]{2,1,0:T(8,128)}, f32[2,256,512]{2,1,0:T(8,128)}, bf16[7168,128]{1,0:T(8,128)(2,1)}, f32[8,512]{1,0:T(8,128)}) custom-call(s32[2,16]{1,0:T(2,128)} %refs_0_.1, bf16[2,256,512]{2,1,0:T(8,128)(2,1)} %bitcast.12, f32[2,256,512]{2,1,0:T(8,128)} %bitcast.11, bf16[3,512,128]{2,1,0:T(8,128)(2,1)} %bitcast.15, bf16[128,512]{1,0:T(8,128)(2,1)} %bitcast.17, ...), custom_call_target="tpu_custom_call" | custom-call | tf_op jit(solution)/shard_map/layers/pallas_call | solution.py:1517
  121.2 5.1 %finish.1 = (f32[1,2,256,512]{3,2,1,0:T(8,128)}, f32[1,2,256,512]{3,2,1,0:T(8,128)}, f32[1,3,512,128]{3,2,1,0:T(8,128)}, f32[1,128,512]{2,1,0:T(8,128)}, f32[1,2...) custom-call(f32[2,256,512]{2,1,0:T(8,128)} %get-tuple-element.22.y_i, ...), custom_call_target="tpu_custom_call" | custom-call | tf_op jit(solution)/shard_map/finish/pallas_call | solution.py:1582
